TPU v7x, 32 devices: a whole 2x2x4 slice. The times are simulated.
32 devices in a mesh: row: 32 (over z, y, x, core).
Axes of the slice: x: 2, y: 2, z: 4, core: 2. Of those that a mesh axis runs over, the one named last changes fastest.
Arguments:
- row_ids: int32 [4096, 26, 30], P('row'), may hold values from 0 to 16383, as said below
- hot_counts: int32 [4096, 26], P('row'), may hold values from 1 to 30, as said below
- dense_feats: float32 [4096, 13], P('row'), may hold values from -6 to 6
- click_labels: int32 [4096], P('row'), may hold values 0 or 1
- block_owners: int32 [240], replicated, may hold values from 0 to 383, as said below
- embed_table: float32 [26, 16384, 128], P(None, 'row'), may hold values from -1.5 to 1.5
- table_moment: float32 [26, 16384, 128], P(None, 'row'), may hold values from -2.3834774e-09 to 2.3834774e-09
- table_square: float32 [26, 16384, 128], P(None, 'row'), may hold values from 2.9343825e-20 to 1.173753e-19
- dense_slots: float32 [384, 128, 512], P('row'), may hold values from -0.13258252 to 0.13258252
- dense_moment: float32 [384, 128, 512], P('row'), may hold values from -1.1094483e-07 to 1.1094483e-07
- dense_square: float32 [384, 128, 512], P('row'), may hold values from 6.3578286e-17 to 2.5431315e-16
- dense_proj: float32 [13, 128], replicated, may hold values from -1.75 to 1.75
- proj_moment: float32 [13, 128], replicated, may hold values from -2.2188966e-07 to 2.2188966e-07
- proj_square: float32 [13, 128], replicated, may hold values from 2.5431316e-17 to 1.0172526e-16
- head_weight: float32 [512], replicated, may hold values from -0.25 to 0.25
- head_moment: float32 [512], replicated, may hold values from -3.328345e-06 to 3.328345e-06
- head_square: float32 [512], replicated, may hold values from 5.722046e-14 to 2.2888183e-13
- biases: float32 [13057], replicated, may hold values from -1.8 to 1.8
- bias_moment: float32 [13057], replicated, may hold values from -2.2188966e-07 to 2.2188966e-07
- bias_square: float32 [13057], replicated, may hold values from 2.5431315e-16 to 1.0172526e-15
Outputs:
- loss_total: float32 [], replicated
- grad_norm: float32 [], replicated
- table_out: float32 [26, 16384, 128], P(None, 'row')
- table_moment_out: float32 [26, 16384, 128], P(None, 'row')
- table_square_out: float32 [26, 16384, 128], P(None, 'row')
- dense_out: float32 [384, 128, 512], P('row')
- dense_moment_out: float32 [384, 128, 512], P('row')
- dense_square_out: float32 [384, 128, 512], P('row')
- proj_out: float32 [13, 128], replicated
- proj_moment_out: float32 [13, 128], replicated
- proj_square_out: float32 [13, 128], replicated
- head_out: float32 [512], replicated
- head_moment_out: float32 [512], replicated
- head_square_out: float32 [512], replicated
- bias_out: float32 [13057], replicated
- bias_moment_out: float32 [13057], replicated
- bias_square_out: float32 [13057], replicated
Inputs may be any that keep to these rules, and one draw needn't show every extreme that they name: `hot_counts`: each sample's counts over its 26 features sum to 403. `row_ids`: ids index rows of their feature's table. Of the live slots (j below the count) of the 128 samples of each device, exactly 1612 have ids in the rows [d * 512, (d + 1) * 512) of each device d. `block_owners`: distinct values; value p names slot p % 12 of device p // 12; some device owns 12 blocks.
All inputs are finite; a program needn't handle non-finite values. No bound on the sum of `click_labels` on one device may be relied on, other than what follows from the above.
Results may differ from a plain program's by a relative error of at most 0.013.
Values may be sent and summed in bfloat16 or wider, within the bound.
A program may use at most 384 MiB of HBM per device.

v0:
```python
import jax
import jax.numpy as jnp
from jax import lax
from jax.sharding import PartitionSpec as P

F = 26
HOT = 30
EMB = 128
RANK = 512
LAYERS = 3
H1 = 1024
H2 = 1024
H3 = 512
BR = 128
STEP = 10
WIDTH = 3456
TOTAL = 403
NBIAS = 13057


beta_one = 0.9
beta_two = 0.999
adam_eps = 1e-12
decay_rate = 0.01
clip_norm = 0.001
rate_table = 0.3
rate_dense = 0.03
rate_small = 0.1
highest = lax.Precision.HIGHEST


def split_dense(flat):
    cross_rows = LAYERS * WIDTH
    first = 2 * cross_rows + WIDTH * H1 // RANK
    second = first + H1 * H2 // RANK
    return (
        flat[:cross_rows].reshape(LAYERS, WIDTH, RANK),
        flat[cross_rows : 2 * cross_rows].reshape(LAYERS, WIDTH, RANK),
        flat[2 * cross_rows : first].reshape(WIDTH, H1),
        flat[first:second].reshape(H1, H2),
        flat[second : second + H2 * H3 // RANK],
    )


def split_bias(biases):
    start = EMB + LAYERS * WIDTH
    return (
        biases[:EMB],
        biases[EMB:start].reshape(LAYERS, WIDTH),
        biases[start : start + H1],
        biases[start + H1 : start + H1 + H2],
        biases[start + H1 + H2 : start + H1 + H2 + H3],
        biases[NBIAS - 1],
    )


def cross_forward(anchor, current, weight_down, weight_up, bias_term):
    current_low = current.astype(jnp.bfloat16)
    reduced = jnp.dot(current_low, weight_down, preferred_element_type=jnp.float32).astype(
        jnp.bfloat16
    )
    mixing = (
        jnp.einsum("sr,wr->sw", reduced, weight_up, preferred_element_type=jnp.float32) + bias_term
    )
    return ((current_low, reduced, mixing), anchor * mixing + current)


def cross_backward(anchor, stored, weight_down, weight_up, grad_current):
    current_low, reduced, mixing = stored
    grad_mixing = anchor * grad_current
    grad_mixing_low = grad_mixing.astype(jnp.bfloat16)
    grad_up = jnp.einsum("sw,sr->wr", grad_mixing_low, reduced, preferred_element_type=jnp.float32)
    grad_reduced = jnp.dot(grad_mixing_low, weight_up, preferred_element_type=jnp.float32).astype(
        jnp.bfloat16
    )
    grad_down = jnp.einsum(
        "sw,sr->wr", current_low, grad_reduced, preferred_element_type=jnp.float32
    )
    grad_prev = grad_current + jnp.einsum(
        "sr,wr->sw", grad_reduced, weight_down, preferred_element_type=jnp.float32
    )
    return (grad_prev, grad_current * mixing, grad_down, grad_up, jnp.sum(grad_mixing, axis=0))


def dense_forward(inputs, weight, bias_term):
    inputs_low = inputs.astype(jnp.bfloat16)
    before = jnp.dot(inputs_low, weight, preferred_element_type=jnp.float32) + bias_term
    return ((inputs_low, before), jax.nn.gelu(before))


def dense_backward(stored, weight, grad_out):
    inputs_low, before = stored
    unused, gelu_back = jax.vjp(jax.nn.gelu, before)
    grad_before = gelu_back(grad_out)[0]
    grad_low = grad_before.astype(jnp.bfloat16)
    grad_weight = jnp.einsum("sa,sb->ab", inputs_low, grad_low, preferred_element_type=jnp.float32)
    grad_inputs = jnp.einsum("sb,ab->sa", grad_low, weight, preferred_element_type=jnp.float32)
    return (grad_inputs, grad_weight, jnp.sum(grad_before, axis=0))


def table_gradient(arrived, served, table_rows):
    received = served.shape[0]
    window = min(512, received)
    order_back = jnp.argsort(served, stable=True)
    sorted_ids = jnp.take(served, order_back)
    edges = jnp.arange(F + 1, dtype=jnp.int32) * table_rows
    bounds = jnp.sum((sorted_ids[None, :] < edges[:, None]).astype(jnp.int32), axis=1)
    starts = bounds[:-1]
    finish = bounds[1:]
    windows = (finish - starts + window - 1) // window
    ends_cum = jnp.cumsum(windows)
    begins_cum = ends_cum - windows
    step_count = F + received // window + 1
    turns = jnp.arange(step_count, dtype=jnp.int32)
    feature_of = jnp.sum((ends_cum[None, :] <= turns[:, None]).astype(jnp.int32), axis=1)
    feature_safe = jnp.minimum(feature_of, F - 1)
    first_row = (
        jnp.take(starts, feature_safe) + (turns - jnp.take(begins_cum, feature_safe)) * window
    )
    row_index = first_row[:, None] + jnp.arange(window, dtype=jnp.int32)[None, :]
    row_valid = (feature_of < F)[:, None] & (row_index < jnp.take(finish, feature_safe)[:, None])
    row_safe = jnp.minimum(row_index, received - 1)
    window_grads = jnp.take(arrived, jnp.take(order_back, row_safe), axis=0)
    local_row = jnp.take(sorted_ids, row_safe) - feature_safe[:, None] * table_rows
    local_row = jnp.where(row_valid, local_row, -1)
    selector = (
        local_row[:, :, None] == jnp.arange(table_rows, dtype=jnp.int32)[None, None, :]
    ).astype(jnp.bfloat16)
    partial_sums = jnp.einsum(
        "swr,swe->sre", selector, window_grads, preferred_element_type=jnp.float32
    )
    feature_pick = (feature_of[:, None] == jnp.arange(F, dtype=jnp.int32)[None, :]).astype(
        jnp.float32
    )
    return jnp.einsum(
        "sf,sre->fre",
        feature_pick,
        partial_sums,
        precision=highest,
        preferred_element_type=jnp.float32,
    )


def adamw(weight, moment, square, gradient, step_rate):
    moment = beta_one * moment + (1 - beta_one) * gradient
    square = beta_two * square + (1 - beta_two) * gradient * gradient
    corrected = moment / (1 - beta_one**STEP)
    scaled = square / (1 - beta_two**STEP)
    weight = weight - step_rate * (corrected / (jnp.sqrt(scaled) + adam_eps) + decay_rate * weight)
    return (weight, moment, square)


def body(
    row_ids,
    hot_counts,
    dense_feats,
    click_labels,
    block_owners,
    embed_table,
    table_moment,
    table_square,
    dense_slots,
    dense_moment,
    dense_square,
    dense_proj,
    proj_moment,
    proj_square,
    head_weight,
    head_moment,
    head_square,
    biases,
    bias_moment,
    bias_square,
):
    devices = lax.axis_size("row")
    samples = row_ids.shape[0]
    slot_count = dense_slots.shape[0]
    table_rows = embed_table.shape[1]
    block_count = block_owners.shape[0]
    capacity = samples * TOTAL // devices
    live_total = samples * TOTAL
    everything = lax.all_gather(dense_slots.astype(jnp.bfloat16), "row", axis=0, tiled=True)
    fetched = jnp.take(everything, block_owners, axis=0)
    cross_down, cross_up, first_matrix, middle, third_matrix = split_dense(
        fetched.reshape(block_count * BR, RANK)
    )
    bias_dense, bias_cross, bias_one, bias_two, bias_three, bias_last = split_bias(biases)
    flat_ids = row_ids.reshape(-1)
    live_mask = (
        lax.broadcasted_iota(jnp.int32, row_ids.shape, 2) < hot_counts[:, :, None]
    ).reshape(-1)
    sort_key = jnp.where(live_mask, flat_ids // table_rows, devices)
    full_order = jnp.argsort(sort_key, stable=True)
    slot_place = jnp.argsort(full_order)
    ordering = full_order[:live_total]
    segment = ordering // HOT
    requests = (segment % F * table_rows + jnp.take(flat_ids, ordering) % table_rows).reshape(
        devices, capacity
    )
    flat_table = embed_table.astype(jnp.bfloat16).reshape(F * table_rows, EMB)
    received = lax.all_to_all(requests, "row", split_axis=0, concat_axis=0, tiled=True)
    looked_up = jnp.take(flat_table, received, axis=0)
    returned = lax.all_to_all(looked_up, "row", split_axis=0, concat_axis=0, tiled=True)
    padded_rows = jnp.concatenate(
        [returned.reshape(-1, EMB), jnp.zeros((1, EMB), jnp.bfloat16)], axis=0
    )
    pick = jnp.where(live_mask, slot_place, live_total)
    in_slots = jnp.take(padded_rows, pick, axis=0).reshape(samples, F, HOT, EMB)
    pooled = jnp.sum(in_slots, axis=2, dtype=jnp.float32)
    pooled_low = pooled.astype(jnp.bfloat16).reshape(samples, F * EMB)
    dense_part = (
        jnp.dot(dense_feats, dense_proj, precision=highest, preferred_element_type=jnp.float32)
        + bias_dense
    )
    anchor = jnp.concatenate([dense_part, pooled_low.astype(jnp.float32)], axis=1)
    current = anchor
    stored = []
    for depth in range(LAYERS):
        saved, current = cross_forward(
            anchor, current, cross_down[depth], cross_up[depth], bias_cross[depth]
        )
        stored.append(saved)
    first_saved, hidden = dense_forward(current, first_matrix, bias_one)
    second_saved, hidden = dense_forward(hidden, middle, bias_two)
    third_saved, hidden = dense_forward(hidden, third_matrix, bias_three)
    logits = (
        jnp.dot(hidden, head_weight, precision=highest, preferred_element_type=jnp.float32)
        + bias_last
    )
    labels = click_labels.astype(jnp.float32)
    loss_local = jnp.sum(jax.nn.softplus(logits) - labels * logits)
    grad_logits = (jax.nn.sigmoid(logits) - labels) / (samples * devices)
    grad_head_local = jnp.dot(
        grad_logits, hidden, precision=highest, preferred_element_type=jnp.float32
    )
    grad_hidden = grad_logits[:, None] * head_weight[None, :]
    grad_hidden, grad_third, grad_bias_three = dense_backward(
        third_saved, third_matrix, grad_hidden
    )
    grad_hidden, grad_middle, grad_bias_two = dense_backward(second_saved, middle, grad_hidden)
    grad_current, grad_first, grad_bias_one = dense_backward(first_saved, first_matrix, grad_hidden)
    grad_anchor = jnp.zeros_like(anchor)
    grads_down = [None] * LAYERS
    grads_up = [None] * LAYERS
    grads_cross = [None] * LAYERS
    for depth in reversed(range(LAYERS)):
        grad_current, grad_part, grads_down[depth], grads_up[depth], grads_cross[depth] = (
            cross_backward(anchor, stored[depth], cross_down[depth], cross_up[depth], grad_current)
        )
        grad_anchor = grad_anchor + grad_part
    grad_anchor = grad_anchor + grad_current
    grad_pooled = grad_anchor[:, EMB:].astype(jnp.bfloat16).reshape(samples * F, EMB)
    sent_back = jnp.take(grad_pooled, segment, axis=0).reshape(devices, capacity, EMB)
    arrived = lax.all_to_all(sent_back, "row", split_axis=0, concat_axis=0, tiled=True)
    grad_table = table_gradient(arrived.reshape(-1, EMB), received.reshape(-1), table_rows)
    grad_proj_local = jnp.einsum(
        "sa,sb->ab",
        dense_feats,
        grad_anchor[:, :EMB],
        precision=highest,
        preferred_element_type=jnp.float32,
    )
    stacked = jnp.concatenate(
        [
            jnp.stack(grads_down).reshape(-1, RANK),
            jnp.stack(grads_up).reshape(-1, RANK),
            grad_first.reshape(-1, RANK),
            grad_middle.reshape(-1, RANK),
            grad_third,
            jnp.zeros((BR, RANK), jnp.float32),
        ],
        axis=0,
    ).reshape(block_count + 1, BR, RANK)
    matches = block_owners[None, :] == jnp.arange(devices * slot_count, dtype=jnp.int32)[:, None]
    inverse = jnp.sum(
        jnp.where(matches, jnp.arange(block_count, dtype=jnp.int32)[None, :], 0), axis=1
    )
    inverse = inverse + jnp.where(jnp.any(matches, axis=1), 0, block_count)
    grad_slots = lax.psum_scatter(
        jnp.take(stacked, inverse, axis=0), "row", scatter_dimension=0, tiled=True
    )
    bias_local = jnp.concatenate(
        [
            jnp.sum(grad_anchor[:, :EMB], axis=0),
            jnp.stack(grads_cross).reshape(-1),
            grad_bias_one,
            grad_bias_two,
            grad_bias_three,
            jnp.sum(grad_logits)[None],
        ]
    )
    loss_total, grad_proj, grad_head, grad_bias = lax.psum(
        (loss_local, grad_proj_local, grad_head_local, bias_local), "row"
    )
    local_squares = jnp.sum(grad_table * grad_table) + jnp.sum(grad_slots * grad_slots)
    squares = lax.psum(local_squares, "row")
    squares = (
        squares
        + jnp.sum(grad_proj * grad_proj)
        + jnp.sum(grad_head * grad_head)
        + jnp.sum(grad_bias * grad_bias)
    )
    grad_norm = jnp.sqrt(squares)
    clip_scale = clip_norm / jnp.maximum(grad_norm, clip_norm)
    table_new = adamw(embed_table, table_moment, table_square, clip_scale * grad_table, rate_table)
    dense_new = adamw(dense_slots, dense_moment, dense_square, clip_scale * grad_slots, rate_dense)
    proj_new = adamw(dense_proj, proj_moment, proj_square, clip_scale * grad_proj, rate_small)
    head_new = adamw(head_weight, head_moment, head_square, clip_scale * grad_head, rate_small)
    bias_new = adamw(biases, bias_moment, bias_square, clip_scale * grad_bias, rate_small)
    return (
        loss_total,
        grad_norm,
        table_new[0],
        table_new[1],
        table_new[2],
        dense_new[0],
        dense_new[1],
        dense_new[2],
        proj_new[0],
        proj_new[1],
        proj_new[2],
        head_new[0],
        head_new[1],
        head_new[2],
        bias_new[0],
        bias_new[1],
        bias_new[2],
    )


def solution(mesh):
    in_specs = (
        P("row", None, None),
        P("row", None),
        P("row", None),
        P("row"),
        P(),
        P(None, "row", None),
        P(None, "row", None),
        P(None, "row", None),
        P("row", None, None),
        P("row", None, None),
        P("row", None, None),
        P(),
        P(),
        P(),
        P(),
        P(),
        P(),
        P(),
        P(),
        P(),
    )
    out_specs = (
        P(),
        P(),
        P(None, "row", None),
        P(None, "row", None),
        P(None, "row", None),
        P("row", None, None),
        P("row", None, None),
        P("row", None, None),
        P(),
        P(),
        P(),
        P(),
        P(),
        P(),
        P(),
        P(),
        P(),
    )
    return jax.shard_map(body, mesh=mesh, in_specs=in_specs, out_specs=out_specs, check_vma=False)
```

profile of v0, /device:TPU:0, one launch (start us, length us, event | category | flops | bytes accessed | tf_op | source)
XLA Modules:
  0.0 2757.5 jit_solution(151452029537171882)
XLA Ops:
  7.3 3.3 convert_element_type.84
  16.0 76.0 %sort.51 = (s32[99840]{0:T(1024)}, s32[99840]{0:T(1024)S(1)}) sort(s32[99840]{0:T(1024)S(1)} %fusion.31, s32[99840]{0:T(1024)S(1)} %iota.51), dimensions={0}, to_apply=%region_0.1 | sort | flops 1697280 | bytes 1597440 | tf_op jit(solution)/shard_map/jit(argsort)/sort | solution.py:193
  93.0 264.1 %gather_fusion = s32[51584]{0:T(1024)S(1)} fusion(s32[99840]{0:T(1024)S(1)} %reshape.443, s32[52224]{0:T(1024)S(1)} %pad_clamp_fusion.6), kind=kCustom, calls=%fused_computation.5 | custom fusion | bytes 619008 | tf_op jit(solution)/shard_map/jit(_take)/gather | solution.py:197
  357.8 3.7 fusion.46
  361.5 7.4 all-to-all-start
  368.9 3.5 convert_element_type.80
  372.4 5.9 all-to-all-done
  384.0 113.1 %gather_fusion.1 = bf16[51584,128]{1,0:T(8,128)(2,1)} fusion(bf16[13312,128]{1,0:T(8,128)(2,1)S(1)} %bitcast.100, s32[52224]{0:T(1024)} %pad_clamp_fusion.5), kind=kCustom, calls=%fused_computation.6 | custom fusion | bytes 26617344 | tf_op jit(solution)/shard_map/jit(_take)/gather | solution.py:202
  497.1 16.1 reshape.509
  514.2 11.6 broadcast_select_fusion.3
  525.9 4.0 all-to-all-start.1
  531.0 76.0 %sort.52 = (s32[99840]{0:T(1024)}, s32[99840]{0:T(1024)S(1)}) sort(s32[99840]{0:T(1024)S(1)} %copy-done.40, s32[99840]{0:T(1024)S(1)} %iota.52), dimensions={0}, to_apply=%region_1.2 | sort | flops 1697280 | bytes 1597440 | tf_op jit(solution)/shard_map/jit(argsort)/sort | solution.py:194
  614.8 31.2 %sort.53 = (s32[51584]{0:T(1024)}, s32[51584]{0:T(1024)S(1)}) sort(s32[51584]{0:T(1024)S(1)} %reshape.448, s32[51584]{0:T(1024)S(1)} %iota.53), dimensions={0}, to_apply=%region_5.6 | sort | flops 825344 | bytes 825344 | tf_op jit(solution)/shard_map/jit(argsort)/sort | solution.py:104
  646.1 264.1 %gather_fusion.4 = s32[51584]{0:T(1024)S(1)} fusion(s32[51584]{0:T(1024)S(1)} %reshape.448, s32[52224]{0:T(1024)S(1)} %pad_clamp_fusion.4), kind=kCustom, calls=%fused_computation.9 | custom fusion | bytes 619008 | tf_op jit(solution)/shard_map/jit(_take)/gather | solution.py:105
  914.5 16.1 reshape.445
  930.6 10.2 concatenate.12
  940.8 190.3 %gather_fusion.2 = bf16[99840,128]{1,0:T(8,128)(2,1)} fusion(bf16[51585,128]{1,0:T(8,128)(2,1)} %concatenate.12, s32[100352]{0:T(1024)S(1)} %pad_clamp_fusion), kind=kCustom, calls=%fused_computation.7 | custom fusion | bytes 51517440 | tf_op jit(solution)/shard_map/jit(_take)/gather | solution.py:208
  1131.1 36.8 %gather.48 = bf16[128,26,30,128]{3,2,1,0:T(8,128)(2,1)} reshape(bf16[99840,128]{1,0:T(8,128)(2,1)} %gather_fusion.2) | data formatting | bytes 51118080 | tf_op jit(solution)/shard_map/jit(_take)/gather | solution.py:208
  1167.9 22.3 select_reduce_fusion
  1192.1 22.5 gather_fusion.3
  1214.6 21.4 broadcast_select_fusion.1
  1236.0 13.6 fusion.102
  1249.6 6.7 slice.160
  1256.4 3.1 slice.161
  1261.7 11.2 reshape.446
  1273.0 4.2 reshape.447
  1277.3 2.8 convolution_convert_fusion.5
  1299.0 3.3 multiply_convert_fusion.2
  1306.7 3.3 multiply_reduce_fusion.2
  1310.9 4.0 convolution_bitcast_fusion.2
  1314.9 4.0 convolution_bitcast_fusion.1
  1318.9 3.9 convolution_bitcast_fusion
  1324.0 4.0 convolution_bitcast_fusion.3
  1327.9 7.1 fusion.51
  1335.0 2.8 fusion.55
  1338.9 5.9 pad_maximum_fusion
  1344.8 7.6 constant_dynamic-update-slice_fusion.3
  1352.5 15.8 reshape.455
  1368.3 4.9 reshape.456
  1373.2 8.6 pad_maximum_fusion.1
  1381.8 8.1 constant_dynamic-update-slice_fusion.2
  1389.9 11.7 constant_dynamic-update-slice_fusion.1
  1401.6 4.8 constant_dynamic-update-slice_fusion
  1409.2 64.0 %gather_fusion.7 = f32[384,128,512]{2,1,0:T(8,128)} fusion(f32[241,128,512]{2,1,0:T(8,128)} %bitcast.101, s32[1024]{0:T(1024)S(1)} %copy-done.62), kind=kCustom, calls=%fused_computation.12 | custom fusion | bytes 201328128 | tf_op jit(solution)/shard_map/jit(_take)/gather | solution.py:280
  1473.2 65.5 %broadcast_select_fusion = f32[384,128,512]{2,1,0:T(8,128)} fusion(f32[384,128,512]{2,1,0:T(8,128)} %gather_fusion.7, pred[384]{0:T(512)(128)(4,1)S(1)} %copy-done.85), kind=kLoop, calls=%fused_computation.16 | loop fusion | flops 25165824 | bytes 201326976 | tf_op jit(solution)/shard_map/jit(_take)/select_n | solution.py:280
  1545.7 7.1 fusion.11
  1555.2 103.8 %gather_fusion.5 = bf16[51584,128]{1,0:T(8,128)(2,1)} fusion(bf16[3328,128]{1,0:T(8,128)(2,1)S(1)} %reshape.451, s32[52224]{0:T(1024)S(1)} %copy-done.41), kind=kCustom, calls=%fused_computation.10 | custom fusion | bytes 26617344 | tf_op jit(solution)/shard_map/jit(_take)/gather | solution.py:253
  1659.0 16.8 gather.52
  1675.8 11.7 broadcast_select_fusion.2
  1687.5 6.1 all-to-all-start.2
  1699.2 333.8 %gather_fusion.12 = s32[65024]{0:T(1024)S(1)} fusion(s32[51584]{0:T(1024)S(1)} %copy-done.2, s32[65536]{0:T(1024)S(1)} %pad_clamp_fusion.2), kind=kCustom, calls=%fused_computation.4.clone | custom fusion | bytes 780288 | tf_op jit(solution)/shard_map/jit(_take)/gather | solution.py:123
  2033.1 333.8 %gather_fusion.11 = s32[65024]{0:T(1024)S(1)} fusion(s32[51584]{0:T(1024)S(1)} %copy-done.4, s32[65536]{0:T(1024)S(1)} %pad_clamp_fusion.2), kind=kCustom, calls=%fused_computation.1.clone | custom fusion | bytes 780288 | tf_op jit(solution)/shard_map/jit(_take)/gather | solution.py:124
  2371.1 16.2 reshape.452
  2387.3 126.5 %gather_fusion.6 = bf16[65024,128]{1,0:T(8,128)(2,1)} fusion(bf16[51584,128]{1,0:T(8,128)(2,1)} %reshape.452, s32[65536]{0:T(1024)S(1)} %pad_clamp_fusion.1), kind=kCustom, calls=%fused_computation.11 | custom fusion | bytes 33552384 | tf_op jit(solution)/shard_map/jit(_take)/gather | solution.py:123
  2513.7 32.1 %fusion = f32[127,512,128]{2,1,0:T(8,128)} fusion(s32[127,512]{1,0:T(8,128)S(1)} %fusion.43, bf16[127,512,128]{2,1,0:T(8,128)(2,1)} %bitcast.120, pred[127,512]{1,0:T(8,128)(4,1)S(1)} %get-tuple-element.137), kind=kOutput, calls=%fused_computation.14 | convolution fusion | flops 8564441088 | bytes 50263552 | tf_op jit(solution)/shard_map/swr,swe->sre/dot_general | solution.py:129
  2545.8 27.4 multiply_reduce_fusion
  2573.2 67.9 %reduce-scatter.2.cloned.1.call-done = f32[12,128,512]{2,1,0:T(8,128)} async-done(((f32[384,128,512]{2,1,0:T(8,128)}), f32[12,128,512]{2,1,0:T(8,128)}) %reduce-scatter.2.cloned.1.call-update) | async-done | bytes 3145744 | tf_op jit(solution)/shard_map/reduce_scatter | solution.py:279
  2641.2 3.3 multiply_reduce_fusion.1
  2645.8 40.6 %all-reduce.1 = (f32[]{:T(128)}, f32[]{:T(128)}, f32[13,128]{1,0:T(8,128)S(1)}, f32[512]{0:T(512)S(1)}, f32[13057]{0:T(1024)S(1)}) all-reduce(f32[]{:T(128)} %get-tuple-element.158, f32[]{:T(128)S(6)} %add.491, f32[13,128]{1,0:T(8,128)S(1)} %convolution_bitcast_fusion.6, f32[512]{0:T(512)S(1)} %bitcast.125, ...), channel_id=1, replica_groups=mesh['row'=32] {'row'}, use_global_device_ids=true, to_apply=%region_4.5 | all-reduce | flops 15235 | bytes 121880 | tf_op jit(solution)/shard_map/psum | solution.py:292
  2690.9 27.7 %copy_subtract_fusion = (f32[26,512,128]{2,0,1:T(8,128)}, f32[26,512,128]{2,0,1:T(8,128)}, f32[26,512,128]{2,0,1:T(8,128)}) fusion(f32[26,512,128]{2,1,0:T(8,128)} %param.29, f32[26,512,128]{2,0,1:T(8,128)} %get-tuple-element.177, f32[]{:T(128)S(6)} %div.145, f32[26,512,128]{2,1,0:T(8,128)} %param.30, f32[26,512,128]{2,1,0:T(8,128)} %param.31), kind=kLoop, calls=%fused_computation.29 | loop fusion | flops 27262976 | bytes 47710212 | tf_op jit(solution)/shard_map/sub | solution.py:149
  2718.6 10.4 copy.100
  2729.0 6.8 copy.101
  2735.9 6.8 copy.99
  2744.7 4.6 multiply_subtract_fusion
  (320 shorter events, 82.2 us)
Async XLA Ops:
  7.2 601.7 %copy-start = (f32[128,13]{0,1:T(8,128)S(1)}, f32[128,13]{0,1:T(8,128)}, u32[]{:S(2)}) copy-start(f32[128,13]{0,1:T(8,128)} %param.26) | copy-start | bytes 19972
  7.2 1184.8 %all-gather.2.cloned.1.call-start = ((), (), s32[]{:S(2)}) async-start(), calls=%async_computation.4 | async-start | bytes 51904512 | tf_op jit(solution)/shard_map/all_gather | solution.py:182
  92.1 265.1 %copy-start.39 = (s32[99840]{0:T(1024)}, s32[99840]{0:T(1024)S(1)}, u32[]{:S(2)}) copy-start(s32[99840]{0:T(1024)S(1)} %get-tuple-element.22) | copy-start | bytes 1198084
  361.5 16.8 all-to-all-start
  525.8 4.1 copy-start.48
  525.8 5.2 copy-start.40
  525.8 83.0 %slice-start.4 = ((f32[13057]{0:T(1024)}), f32[128]{0:T(128)S(1)}, s32[]{:S(2)}) async-start(f32[13057]{0:T(1024)} %param.41), calls=%async_computation.10 | async-start | bytes 1024 | tf_op jit(solution)/shard_map/slice | solution.py:48
  525.9 83.0 %copy-start.65 = (f32[13,128]{1,0:T(8,128)S(1)}, f32[13,128]{1,0:T(8,128)}, u32[]{:S(2)}) copy-start(f32[13,128]{1,0:T(8,128)} %param.35) | copy-start | bytes 19972
  525.9 84.0 %copy-start.71 = (s32[240]{0:T(256)S(1)}, s32[240]{0:T(256)}, u32[]{:S(2)}) copy-start(s32[240]{0:T(256)} %param.28) | copy-start | bytes 2884
  525.9 388.6 %all-to-all-start.1 = ((bf16[32,1612,128]{2,1,0:T(8,128)(2,1)}), bf16[32,1612,128]{2,1,0:T(8,128)(2,1)}, u32[]{:S(2)}, u32[]{:S(2)}) async-start(bf16[32,1612,128]{2,1,0:T(8,128)(2,1)} %broadcast_select_fusion.3), calls=%async_computation.1 | async-start | bytes 26476544 | tf_op jit(solution)/shard_map/all_to_all | solution.py:203
  529.8 2111.3 %reduce-scatter.2.cloned.1.call-start = ((), (), s32[]{:S(2)}) async-start(), calls=%async_computation.5 | async-start | bytes 103809024 | tf_op jit(solution)/shard_map/reduce_scatter | solution.py:279
  646.0 264.2 %copy-start.1 = (s32[51584]{0:T(1024)}, s32[51584]{0:T(1024)S(1)}, u32[]{:S(2)}) copy-start(s32[51584]{0:T(1024)S(1)} %get-tuple-element.24) | copy-start | bytes 619012
  913.8 16.9 copy-start.89
  913.8 16.8 copy-start.75
  1131.1 36.8 %copy-start.27 = (pred[128,26,30]{2,1,0:T(8,128)(4,1)S(1)}, pred[128,26,30]{2,1,0:T(8,128)(4,1)}, u32[]{:S(2)}) copy-start(pred[128,26,30]{2,1,0:T(8,128)(4,1)} %broadcast_in_dim.161) | copy-start | bytes 299524
  1192.0 22.6 copy-start.86
  1273.0 4.3 copy-start.23
  1281.6 5.9 copy-start.14
  1286.2 5.5 copy-start.16
  1286.8 4.9 slice-start
  1287.5 4.2 copy-start.34
  1293.0 4.3 copy-start.28
  1295.9 110.5 %copy-start.87 = (f32[128]{0:T(128)}, f32[128]{0:T(128)S(1)}, u32[]{:S(2)}) copy-start(f32[128]{0:T(128)S(1)} %get-tuple-element.134) | copy-start | bytes 1540
  1302.3 4.5 copy-start.15
  1310.9 26.9 copy-start.31
  1310.9 4.0 copy-start.33
  1314.9 4.0 copy-start.35
  1327.9 7.1 copy-start.29
  1327.9 7.1 copy-start.44
  1401.6 4.8 copy-start.46
  1401.6 4.8 copy-start.93
  1409.2 64.0 %copy-start.85 = (pred[384]{0:T(512)(128)(4,1)S(1)}, pred[384]{0:T(512)(128)(4,1)}, u32[]{:S(2)}) copy-start(pred[384]{0:T(512)(128)(4,1)} %get-tuple-element.135) | copy-start | bytes 1156
  1538.7 7.0 copy-start.13
  1659.0 16.8 copy-start.50
  1687.5 6.2 copy-start.79
  1687.5 6.2 copy-start.90
  1687.5 7.7 copy-start.6
  1687.5 9.1 copy-start.5
  1687.5 10.4 copy-start.76
  1687.5 683.5 %all-to-all-start.2 = ((bf16[32,1612,128]{2,1,0:T(8,128)(2,1)}), bf16[32,1612,128]{2,1,0:T(8,128)(2,1)}, u32[]{:S(2)}, u32[]{:S(2)}) async-start(bf16[32,1612,128]{2,1,0:T(8,128)(2,1)} %broadcast_select_fusion.2), calls=%async_computation.2 | async-start | bytes 26476544 | tf_op jit(solution)/shard_map/all_to_all | solution.py:254
  1693.7 5.5 copy-start.2
  1699.2 333.8 %copy-start.4 = (s32[51584]{0:T(1024)S(1)}, s32[51584]{0:T(1024)}, u32[]{:S(2)}) copy-start(s32[51584]{0:T(1024)} %copy-done.3) | copy-start | bytes 619012
  2033.0 334.0 %copy-start.70 = (s32[127]{0:T(128)S(1)}, s32[127]{0:T(128)}, u32[]{:S(2)}) copy-start(s32[127]{0:T(128)} %copy-done.69) | copy-start | bytes 1528
  2033.0 334.3 %copy-start.77 = (s32[127]{0:T(128)S(1)}, s32[127]{0:T(128)}, u32[]{:S(2)}) copy-start(s32[127]{0:T(128)} %copy-done.75) | copy-start | bytes 1528
  2033.0 334.3 %copy-start.83 = (s32[127]{0:T(128)S(1)}, s32[127]{0:T(128)}, u32[]{:S(2)}) copy-start(s32[127]{0:T(128)} %get-tuple-element.159) | copy-start | bytes 1528
  2033.1 334.3 %copy-start.84 = (s32[127]{0:T(128)S(1)}, s32[127]{0:T(128)}, u32[]{:S(2)}) copy-start(s32[127]{0:T(128)} %get-tuple-element.161) | copy-start | bytes 1528
  2033.1 334.6 %copy-start.53 = (f32[3456]{0:T(1024)S(1)}, f32[3456]{0:T(1024)}, u32[]{:S(2)}) copy-start(f32[3456]{0:T(1024)} %get-tuple-element.110) | copy-start | bytes 41476
  2033.1 334.6 %copy-start.52 = (f32[3456]{0:T(1024)S(1)}, f32[3456]{0:T(1024)}, u32[]{:S(2)}) copy-start(f32[3456]{0:T(1024)} %get-tuple-element.111) | copy-start | bytes 41476
  2033.1 334.6 %copy-start.51 = (f32[3456]{0:T(1024)S(1)}, f32[3456]{0:T(1024)}, u32[]{:S(2)}) copy-start(f32[3456]{0:T(1024)} %get-tuple-element.112) | copy-start | bytes 41476
  2718.6 10.4 copy-start.7
  2718.6 17.2 slice-start.2
  2729.0 6.8 slice-start.3
  2735.8 7.0 copy-start.49
  2735.8 7.0 copy-start.57
  2735.8 6.9 copy-start.58
  2735.8 7.6 copy-start.81
  2735.8 7.6 copy-start.82
  2735.8 8.2 copy-start.66
  2735.9 8.2 copy-start.67
  2735.9 8.2 copy-start.68
  2735.9 8.8 copy-start.18
  2735.9 8.8 copy-start.19
  2735.9 8.8 copy-start.25
  2735.9 8.8 copy-start.26
  (40 other events, 93.4 us)
Sparse Core Ops, SparseCore 0:
  11.5 278.2 all-gather.1
  1538.9 1102.2 reduce-scatter.1
where the time goes:
time: 2770 us; the launch traced here: 2760 us
  local copies, waits for them, and re-layouts  2080 us (75%)
  other arithmetic  400 us (14%)
  matrix products  126 us (5%)
  waiting for transfers between devices  73.9 us (3%)
  blocking collectives  40.6 us (1%)
    gather x3, local copies, waits for them, and re-layouts, table_gradient(): window_grads = jnp.take(arrived, jnp.take(order_back, row_safe), axis=0)  460 us
    gather x2, local copies, waits for them, and re-layouts, table_gradient(): jnp.take(sorted_ids, row_safe) - feature_safe[:, None] * table_rows  334 us
    gather x2, local copies, waits for them, and re-layouts, body(): jnp.take(flat_ids, ordering) % table_rows  264 us
    gather x1, local copies, waits for them, and re-layouts, table_gradient(): sorted_ids = jnp.take(served, order_back)  264 us
    gather x2, local copies, waits for them, and re-layouts, body(): in_slots = jnp.take(padded_rows, pick, axis=0).reshape(samples, F, HOT, EMB)  227 us
    gather x2, local copies, waits for them, and re-layouts, body(): looked_up = jnp.take(flat_table, received, axis=0)  129 us
    gather x2, local copies, waits for them, and re-layouts, body(): jnp.take(grad_pooled, segment, axis=0).reshape(devices, capacity, EMB)  121 us
    sort x1, other arithmetic, body(): full_order = jnp.argsort(sort_key, stable=True)  76 us
  transfers between devices with their start and end apart: 5, of which 2 were waited for; matrix products, arithmetic and copies ran while one was open for 79% of the time, Pallas kernels for 0%

commit v1 on v0

--- a/solution.py
+++ b/solution.py
@@ -1,6 +1,10 @@
+import functools
+
 import jax
 import jax.numpy as jnp
 from jax import lax
+from jax.experimental import pallas as pl
+from jax.experimental.pallas import tpu as pltpu
 from jax.sharding import PartitionSpec as P
 
 F = 26
@@ -148,6 +152,478 @@
     scaled = square / (1 - beta_two**STEP)
     weight = weight - step_rate * (corrected / (jnp.sqrt(scaled) + adam_eps) + decay_rate * weight)
     return (weight, moment, square)
+
+
+def count_kernel(devices, samples, table_rows, off_ref, keys_ref, table_ref, counts_ref, partial_ref):
+    feature = pl.program_id(0)
+    low_table = table_ref[0].T.astype(jnp.bfloat16)
+    lane = lax.broadcasted_iota(jnp.int32, (1, samples), 1)
+    row_iota = lax.broadcasted_iota(jnp.int32, (table_rows, 2 * samples), 0)
+    sample_iota = lax.broadcasted_iota(jnp.int32, (2 * samples, 2 * samples), 0)
+
+    def window(source, turn):
+        start = off_ref[source * (F + 1) + feature] + turn * samples
+        stop = off_ref[source * (F + 1) + feature + 1]
+        tile = start // samples
+        base = pl.multiple_of(tile * samples, samples)
+        piece = keys_ref[pl.ds(source, 1), pl.ds(base, 2 * samples)]
+        turned = pltpu.roll(piece, 2 * samples - (start - base), 1)[:, :samples]
+        valid = lane < stop - start
+        row = jnp.where(valid, (turned >> 7) & (table_rows - 1), -1)
+        return row, turned & (samples - 1)
+
+    def counted(first, turn):
+        row_a, sample_a = window(first, turn)
+        row_b, sample_b = window(first + 1, turn)
+        row = jnp.concatenate([row_a, row_b], axis=1)
+        sample = jnp.concatenate([sample_a, sample_b + samples], axis=1)
+        row_hot = (row_iota == row).astype(jnp.float32).astype(jnp.bfloat16)
+        sample_hot = (sample_iota == sample).astype(jnp.float32).astype(jnp.bfloat16)
+        return lax.dot_general(
+            row_hot, sample_hot, (((1,), (1,)), ((), ())), preferred_element_type=jnp.float32
+        )
+
+    def pair(step, carry):
+        first = step * 2
+        total = counted(first, 0)
+        spans = [
+            off_ref[(first + i) * (F + 1) + feature + 1] - off_ref[(first + i) * (F + 1) + feature]
+            for i in (0, 1)
+        ]
+        turns = (jnp.maximum(spans[0], spans[1]) + samples - 1) // samples
+        total = lax.fori_loop(1, turns, lambda turn, acc: acc + counted(first, turn), total)
+        low = total.astype(jnp.bfloat16)
+        counts_ref[0, :, pl.ds(pl.multiple_of(first * samples, 2 * samples), 2 * samples)] = low
+        part = jnp.dot(low_table, low, preferred_element_type=jnp.float32).astype(jnp.bfloat16)
+        partial_ref[first, 0] = part[:, :samples]
+        partial_ref[first + 1, 0] = part[:, samples:]
+        return carry
+
+    lax.fori_loop(0, devices // 2, pair, 0, unroll=2)
+
+
+def count_tables(offsets, keys, embed_table, devices, samples):
+    table_rows = embed_table.shape[1]
+    return pl.pallas_call(
+        functools.partial(count_kernel, devices, samples, table_rows),
+        grid_spec=pltpu.PrefetchScalarGridSpec(
+            num_scalar_prefetch=1,
+            grid=(F,),
+            in_specs=[
+                pl.BlockSpec(keys.shape, lambda f, off: (0, 0)),
+                pl.BlockSpec((1, table_rows, EMB), lambda f, off: (f, 0, 0)),
+            ],
+            out_specs=[
+                pl.BlockSpec((1, table_rows, devices * samples), lambda f, off: (f, 0, 0)),
+                pl.BlockSpec((devices, 1, EMB, samples), lambda f, off: (0, f, 0, 0)),
+            ],
+        ),
+        out_shape=[
+            jax.ShapeDtypeStruct((F, table_rows, devices * samples), jnp.bfloat16),
+            jax.ShapeDtypeStruct((devices, F, EMB, samples), jnp.bfloat16),
+        ],
+        compiler_params=pltpu.CompilerParams(vmem_limit_bytes=48 << 20),
+        name="count_tables",
+    )(offsets, keys, embed_table)
+
+
+def row_grad_kernel(counts_ref, grads_ref, out_ref, square_ref):
+    @pl.when(pl.program_id(0) == 0)
+    def start():
+        square_ref[...] = jnp.zeros_like(square_ref)
+
+    total = jnp.dot(counts_ref[0], grads_ref[...], preferred_element_type=jnp.float32)
+    out_ref[0] = total
+    square_ref[...] += jnp.sum((total * total).reshape(-1, 8, EMB), axis=0)
+
+
+def row_grads(counts, grads):
+    table_rows, batch = counts.shape[1:]
+    return pl.pallas_call(
+        row_grad_kernel,
+        grid=(F,),
+        in_specs=[
+            pl.BlockSpec((1, table_rows, batch), lambda f: (f, 0, 0)),
+            pl.BlockSpec((batch, EMB), lambda f: (0, f)),
+        ],
+        out_specs=[
+            pl.BlockSpec((1, table_rows, EMB), lambda f: (f, 0, 0)),
+            pl.BlockSpec((8, EMB), lambda f: (0, 0)),
+        ],
+        out_shape=[
+            jax.ShapeDtypeStruct((F, table_rows, EMB), jnp.float32),
+            jax.ShapeDtypeStruct((8, EMB), jnp.float32),
+        ],
+        compiler_params=pltpu.CompilerParams(vmem_limit_bytes=48 << 20),
+        name="row_grads",
+    )(counts, grads)
+
+
+MESH = pl.DeviceIdType.MESH
+
+
+def place():
+    me = lax.axis_index("row")
+    return me // 8, (me // 4) % 2, (me // 2) % 2, me % 2
+
+
+def device_at(z, y, x, core):
+    return (((z * 2 + y) * 2 + x) * 2 + core,)
+
+
+def greet(z, y, x, core):
+    barrier = pltpu.get_barrier_semaphore()
+
+    def hail(*where):
+        pl.semaphore_signal(barrier, inc=1, device_id=device_at(*where), device_id_type=MESH)
+
+    hail(z, y, x, 1 - core)
+    hail(z, y, 1 - x, core)
+    hail(z, 1 - y, x, core)
+
+    @pl.when(z > 0)
+    def below():
+        hail(z - 1, y, x, core)
+
+    @pl.when(z < 3)
+    def above():
+        hail(z + 1, y, x, core)
+
+    @pl.when(jnp.logical_and(z > 0, z < 3))
+    def inside():
+        pl.semaphore_wait(barrier, 5)
+
+    @pl.when(jnp.logical_or(z == 0, z == 3))
+    def edge():
+        pl.semaphore_wait(barrier, 4)
+
+
+def remote(source, target, send_sem, recv_sem, where):
+    return pltpu.make_async_remote_copy(
+        src_ref=source,
+        dst_ref=target,
+        send_sem=send_sem,
+        recv_sem=recv_sem,
+        device_id=device_at(*where),
+        device_id_type=MESH,
+    )
+
+
+def add_into(target, source, count):
+    @pl.loop(0, count)
+    def step(i):
+        target[i] = target[i] + source[i]
+
+
+def scatter_kernel(
+    base, slices, lags, x_ref, out_ref, own, got_core, got_one, got_two, got_up, got_down,
+    local_sem, send_core, recv_core, send_one, recv_one, send_two, recv_two,
+    send_up, recv_up, send_down, recv_down,
+):
+    z, y, x, core = place()
+    rows = own.shape[4]
+
+    def span(q):
+        return pl.ds(base + q * rows, rows)
+
+    def kept(q):
+        return pl.ds(q * rows, rows)
+
+    def to_core(q):
+        return remote(x_ref.at[:, :, :, 1 - core, span(q)], got_core.at[q], send_core.at[q], recv_core.at[q], (z, y, x, 1 - core))
+
+    def to_one(q):
+        if q % 2 == 0:
+            source, where = own.at[q, :, :, 1 - x], (z, y, 1 - x, core)
+        else:
+            source, where = own.at[q, :, 1 - y], (z, 1 - y, x, core)
+        return remote(source, got_one.at[q], send_one.at[q], recv_one.at[q], where)
+
+    def to_two(q):
+        if q % 2 == 0:
+            source, where = own.at[q, :, 1 - y, x], (z, 1 - y, x, core)
+        else:
+            source, where = own.at[q, :, y, 1 - x], (z, y, 1 - x, core)
+        return remote(source, got_two.at[q], send_two.at[q], recv_two.at[q], where)
+
+    def to_up(q, level):
+        count = 3 - level
+        source = own.at[q, 1:4, y, x] if level == 0 else got_up.at[q, 1 : count + 1]
+        return remote(source, got_up.at[q, 0:count], send_up.at[q], recv_up.at[q], (z + 1, y, x, core))
+
+    def to_down(q, level):
+        count = level
+        source = own.at[q, 0:3, y, x] if level == 3 else got_down.at[q, 0:count]
+        return remote(source, got_down.at[q, 0:count], send_down.at[q], recv_down.at[q], (z - 1, y, x, core))
+
+    def local(q):
+        return pltpu.make_async_copy(x_ref.at[:, :, :, core, span(q)], own.at[q], local_sem.at[q])
+
+    def stage_zero(q):
+        local(q).wait()
+        to_core(q).wait_recv()
+
+        @pl.loop(0, 16)
+        def step(i):
+            a, b, c = i // 4, (i // 2) % 2, i % 2
+            own[q, a, b, c] = own[q, a, b, c] + got_core[q, a, b, c]
+
+        to_one(q).start()
+
+    def stage_one(q):
+        to_one(q).wait_recv()
+
+        @pl.loop(0, 8)
+        def step(i):
+            a, b = i // 2, i % 2
+            if q % 2 == 0:
+                own[q, a, b, x] = own[q, a, b, x] + got_one[q, a, b]
+            else:
+                own[q, a, y, b] = own[q, a, y, b] + got_one[q, a, b]
+
+        to_two(q).start()
+
+    def stage_two(q):
+        to_two(q).wait_recv()
+
+        @pl.loop(0, 4)
+        def step(a):
+            own[q, a, y, x] = own[q, a, y, x] + got_two[q, a]
+
+        @pl.when(z == 0)
+        def rise():
+            to_up(q, 0).start()
+
+        @pl.when(z == 3)
+        def fall():
+            to_down(q, 3).start()
+
+    def stage_chain(q, hop):
+        @pl.when(z == hop)
+        def rise():
+            to_up(q, hop - 1).wait_recv()
+            for t in range(hop + 1, 4):
+                got_up[q, t - hop] = got_up[q, t - hop] + own[q, t, y, x]
+            if hop < 3:
+                to_up(q, hop).start()
+
+        @pl.when(z == 3 - hop)
+        def fall():
+            to_down(q, 4 - hop).wait_recv()
+            for t in range(0, 3 - hop):
+                got_down[q, t] = got_down[q, t] + own[q, t, y, x]
+            if hop < 3:
+                to_down(q, 3 - hop).start()
+
+    def stage_end(q):
+        @pl.when(z == 0)
+        def bottom():
+            total = own[q, 0, y, x].astype(jnp.float32) + got_down[q, 0].astype(jnp.float32)
+            out_ref[kept(q)] = total.astype(out_ref.dtype)
+
+        @pl.when(z == 3)
+        def top():
+            total = own[q, 3, y, x].astype(jnp.float32) + got_up[q, 0].astype(jnp.float32)
+            out_ref[kept(q)] = total.astype(out_ref.dtype)
+
+        for level in (1, 2):
+
+            @pl.when(z == level)
+            def middle():
+                total = own[q, level, y, x].astype(jnp.float32) + got_up[q, 0].astype(jnp.float32)
+                total = total + got_down[q, level].astype(jnp.float32)
+                out_ref[kept(q)] = total.astype(out_ref.dtype)
+
+    for q in range(slices):
+        local(q).start()
+    greet(z, y, x, core)
+    for q in range(slices):
+        to_core(q).start()
+    stages = (
+        stage_zero,
+        stage_one,
+        stage_two,
+        lambda q: stage_chain(q, 1),
+        lambda q: stage_chain(q, 2),
+        lambda q: (stage_chain(q, 3), stage_end(q)),
+    )
+    for tick in range(slices + lags[-1]):
+        for lag, stage in zip((0,) + lags, stages):
+            if 0 <= tick - lag < slices:
+                stage(tick - lag)
+    for q in range(slices):
+        to_core(q).wait_send()
+        to_one(q).wait_send()
+        to_two(q).wait_send()
+        for level in range(4):
+
+            @pl.when(z == level)
+            def sent():
+                if level < 3:
+                    to_up(q, level).wait_send()
+                if level > 0:
+                    to_down(q, level).wait_send()
+
+
+def scatter_sum(array, base, chunk, out_dtype, slices, lags, collective_id, name):
+    lanes = array.shape[-1]
+    rows = chunk // slices
+    low = array.dtype
+    dma = pltpu.SemaphoreType.DMA
+    return pl.pallas_call(
+        functools.partial(scatter_kernel, base, slices, lags),
+        out_shape=jax.ShapeDtypeStruct((chunk, lanes), out_dtype),
+        in_specs=[pl.BlockSpec(memory_space=pl.ANY)],
+        out_specs=pl.BlockSpec(memory_space=pltpu.VMEM),
+        scratch_shapes=[
+            pltpu.VMEM((slices, 4, 2, 2, rows, lanes), low),
+            pltpu.VMEM((slices, 4, 2, 2, rows, lanes), low),
+            pltpu.VMEM((slices, 4, 2, rows, lanes), low),
+            pltpu.VMEM((slices, 4, rows, lanes), low),
+            pltpu.VMEM((slices, 3, rows, lanes), low),
+            pltpu.VMEM((slices, 3, rows, lanes), low),
+            dma((slices,)),
+            dma((slices,)), dma((slices,)),
+            dma((slices,)), dma((slices,)),
+            dma((slices,)), dma((slices,)),
+            dma((slices,)), dma((slices,)),
+            dma((slices,)), dma((slices,)),
+        ],
+        compiler_params=pltpu.CompilerParams(
+            collective_id=collective_id, has_side_effects=True, vmem_limit_bytes=60 << 20
+        ),
+        name=name,
+    )(array.reshape(4, 2, 2, 2, -1, lanes))
+
+
+def spread_kernel(slices, lags, x_ref, out_ref, local_sem, send_up, recv_up, send_down, recv_down,
+    send_one, recv_one, send_two, recv_two, send_core, recv_core):
+    z, y, x, core = place()
+    rows = x_ref.shape[0] // slices
+
+    def span(q):
+        return pl.ds(q * rows, rows)
+
+    def local(q):
+        return pltpu.make_async_copy(x_ref.at[span(q)], out_ref.at[z, y, x, core, span(q)], local_sem.at[q])
+
+    def to_up(q, k):
+        block = z - k
+        target = out_ref.at[block, y, x, core, span(q)]
+        source = x_ref.at[span(q)] if k == 0 else target
+        return remote(source, target, send_up.at[q, k], recv_up.at[q, k], (z + 1, y, x, core))
+
+    def to_down(q, k):
+        block = z + k
+        target = out_ref.at[block, y, x, core, span(q)]
+        source = x_ref.at[span(q)] if k == 0 else target
+        return remote(source, target, send_down.at[q, k], recv_down.at[q, k], (z - 1, y, x, core))
+
+    def to_one(q):
+        block = out_ref.at[:, y, x, core, span(q)]
+        where = (z, y, 1 - x, core) if q % 2 == 0 else (z, 1 - y, x, core)
+        return remote(block, block, send_one.at[q], recv_one.at[q], where)
+
+    def to_two(q):
+        if q % 2 == 0:
+            block, where = out_ref.at[:, y, :, core, span(q)], (z, 1 - y, x, core)
+        else:
+            block, where = out_ref.at[:, :, x, core, span(q)], (z, y, 1 - x, core)
+        return remote(block, block, send_two.at[q], recv_two.at[q], where)
+
+    def to_core(q):
+        block = out_ref.at[:, :, :, core, span(q)]
+        return remote(block, block, send_core.at[q], recv_core.at[q], (z, y, x, 1 - core))
+
+    def stage_start(q):
+        @pl.when(z < 3)
+        def rise():
+            to_up(q, 0).start()
+
+        @pl.when(z > 0)
+        def fall():
+            to_down(q, 0).start()
+
+    def stage_chain(q):
+        for k in range(3):
+
+            @pl.when(z - 1 - k >= 0)
+            def rise():
+                to_up(q, k).wait_recv()
+                if k < 2:
+
+                    @pl.when(z < 3)
+                    def go_on():
+                        to_up(q, k + 1).start()
+
+            @pl.when(z + 1 + k <= 3)
+            def fall():
+                to_down(q, k).wait_recv()
+                if k < 2:
+
+                    @pl.when(z > 0)
+                    def go_on():
+                        to_down(q, k + 1).start()
+
+        local(q).wait()
+        to_one(q).start()
+
+    def stage_one(q):
+        to_one(q).wait_recv()
+        to_two(q).start()
+
+    def stage_two(q):
+        to_two(q).wait_recv()
+        to_core(q).start()
+
+    def stage_core(q):
+        to_core(q).wait_recv()
+
+    for q in range(slices):
+        local(q).start()
+    greet(z, y, x, core)
+    for q in range(slices):
+        stage_start(q)
+    for tick in range(slices + lags[2]):
+        for lag, stage in zip((0,) + lags, (stage_chain, stage_one, stage_two, stage_core)):
+            if 0 <= tick - lag < slices:
+                stage(tick - lag)
+    for q in range(slices):
+        for k in range(3):
+
+            @pl.when(jnp.logical_and(z < 3, z - k >= 0))
+            def rise():
+                to_up(q, k).wait_send()
+
+            @pl.when(jnp.logical_and(z > 0, z + k <= 3))
+            def fall():
+                to_down(q, k).wait_send()
+
+        to_one(q).wait_send()
+        to_two(q).wait_send()
+        to_core(q).wait_send()
+
+
+def spread(array, slices, lags, collective_id, name):
+    chunk, lanes = array.shape
+    dma = pltpu.SemaphoreType.DMA
+    gathered = pl.pallas_call(
+        functools.partial(spread_kernel, slices, lags),
+        out_shape=jax.ShapeDtypeStruct((4, 2, 2, 2, chunk, lanes), array.dtype),
+        in_specs=[pl.BlockSpec(memory_space=pl.ANY)],
+        out_specs=pl.BlockSpec(memory_space=pl.ANY),
+        scratch_shapes=[
+            dma((slices,)),
+            dma((slices, 3)), dma((slices, 3)),
+            dma((slices, 3)), dma((slices, 3)),
+            dma((slices,)), dma((slices,)),
+            dma((slices,)), dma((slices,)),
+            dma((slices,)), dma((slices,)),
+        ],
+        compiler_params=pltpu.CompilerParams(collective_id=collective_id, has_side_effects=True),
+        name=name,
+    )(array)
+    return gathered.reshape(32 * chunk, lanes)
 
 
 def body(
@@ -328,6 +804,188 @@
     )
 
 
+def body_counted(
+    row_ids,
+    hot_counts,
+    dense_feats,
+    click_labels,
+    block_owners,
+    embed_table,
+    table_moment,
+    table_square,
+    dense_slots,
+    dense_moment,
+    dense_square,
+    dense_proj,
+    proj_moment,
+    proj_square,
+    head_weight,
+    head_moment,
+    head_square,
+    biases,
+    bias_moment,
+    bias_square,
+):
+    devices = lax.axis_size("row")
+    samples = row_ids.shape[0]
+    slot_count = dense_slots.shape[0]
+    table_rows = embed_table.shape[1]
+    block_count = block_owners.shape[0]
+    capacity = samples * TOTAL // devices
+    live_total = samples * TOTAL
+    everything = lax.all_gather(dense_slots.astype(jnp.bfloat16), "row", axis=0, tiled=True)
+    fetched = jnp.take(everything, block_owners, axis=0, mode="clip")
+    cross_down, cross_up, first_matrix, middle, third_matrix = split_dense(
+        fetched.reshape(block_count * BR, RANK)
+    )
+    bias_dense, bias_cross, bias_one, bias_two, bias_three, bias_last = split_bias(biases)
+    lanes = lax.broadcasted_iota(jnp.int32, row_ids.shape, 2)
+    features = lax.broadcasted_iota(jnp.int32, row_ids.shape, 1)
+    sample_of = lax.broadcasted_iota(jnp.int32, row_ids.shape, 0)
+    key = (
+        ((row_ids // table_rows) << 21)
+        | (features << 16)
+        | ((row_ids % table_rows) << 7)
+        | sample_of
+    )
+    key = jnp.where(lanes < hot_counts[:, :, None], key, devices << 21)
+    ordered = lax.sort(key.reshape(-1), is_stable=False)[:live_total]
+    requests = (ordered & ((1 << 21) - 1)).reshape(devices, capacity)
+    received = lax.all_to_all(requests, "row", split_axis=0, concat_axis=0, tiled=True)
+    edges = jnp.arange(F + 1, dtype=jnp.int32) << 16
+    offsets = jnp.sum((received[:, None, :] < edges[None, :, None]).astype(jnp.int32), axis=2)
+    room = (capacity + samples - 1) // samples * samples + samples
+    keys = jnp.pad(received, ((0, 0), (0, room - capacity)), constant_values=-1)
+    counts, partial = count_tables(offsets.reshape(-1), keys, embed_table, devices, samples)
+    summed = scatter_sum(
+        partial, 0, F * EMB, jnp.bfloat16, 16, (2, 4, 6, 7, 8), 0, "scatter_pooled"
+    )
+    pooled_low = summed.T
+    dense_part = (
+        jnp.dot(dense_feats, dense_proj, precision=highest, preferred_element_type=jnp.float32)
+        + bias_dense
+    )
+    anchor = jnp.concatenate([dense_part, pooled_low.astype(jnp.float32)], axis=1)
+    current = anchor
+    stored = []
+    for depth in range(LAYERS):
+        saved, current = cross_forward(
+            anchor, current, cross_down[depth], cross_up[depth], bias_cross[depth]
+        )
+        stored.append(saved)
+    first_saved, hidden = dense_forward(current, first_matrix, bias_one)
+    second_saved, hidden = dense_forward(hidden, middle, bias_two)
+    third_saved, hidden = dense_forward(hidden, third_matrix, bias_three)
+    logits = (
+        jnp.dot(hidden, head_weight, precision=highest, preferred_element_type=jnp.float32)
+        + bias_last
+    )
+    labels = click_labels.astype(jnp.float32)
+    loss_local = jnp.sum(jax.nn.softplus(logits) - labels * logits)
+    grad_logits = (jax.nn.sigmoid(logits) - labels) / (samples * devices)
+    grad_head_local = jnp.dot(
+        grad_logits, hidden, precision=highest, preferred_element_type=jnp.float32
+    )
+    grad_hidden = grad_logits[:, None] * head_weight[None, :]
+    grad_hidden, grad_third, grad_bias_three = dense_backward(
+        third_saved, third_matrix, grad_hidden
+    )
+    grad_hidden, grad_middle, grad_bias_two = dense_backward(second_saved, middle, grad_hidden)
+    grad_current, grad_first, grad_bias_one = dense_backward(first_saved, first_matrix, grad_hidden)
+    grad_anchor = jnp.zeros_like(anchor)
+    grads_down = [None] * LAYERS
+    grads_up = [None] * LAYERS
+    grads_cross = [None] * LAYERS
+    for depth in reversed(range(LAYERS)):
+        grad_current, grad_part, grads_down[depth], grads_up[depth], grads_cross[depth] = (
+            cross_backward(anchor, stored[depth], cross_down[depth], cross_up[depth], grad_current)
+        )
+        grad_anchor = grad_anchor + grad_part
+    grad_anchor = grad_anchor + grad_current
+    grad_pooled = grad_anchor[:, EMB:].astype(jnp.bfloat16)
+    gathered_grads = lax.all_gather(grad_pooled, "row", axis=0, tiled=True)
+    grad_table, table_squares = row_grads(counts, gathered_grads)
+    grad_proj_local = jnp.einsum(
+        "sa,sb->ab",
+        dense_feats,
+        grad_anchor[:, :EMB],
+        precision=highest,
+        preferred_element_type=jnp.float32,
+    )
+    stacked = jnp.concatenate(
+        [
+            jnp.stack(grads_down).reshape(-1, RANK),
+            jnp.stack(grads_up).reshape(-1, RANK),
+            grad_first.reshape(-1, RANK),
+            grad_middle.reshape(-1, RANK),
+            grad_third,
+            jnp.zeros((BR, RANK), jnp.float32),
+        ],
+        axis=0,
+    ).astype(jnp.bfloat16).reshape(block_count + 1, BR, RANK)
+    matches = block_owners[None, :] == jnp.arange(devices * slot_count, dtype=jnp.int32)[:, None]
+    inverse = jnp.sum(
+        jnp.where(matches, jnp.arange(block_count, dtype=jnp.int32)[None, :], 0), axis=1
+    )
+    inverse = inverse + jnp.where(jnp.any(matches, axis=1), 0, block_count)
+    placed = jnp.take(stacked, inverse, axis=0, mode="clip")
+    half = slot_count * BR // 2
+    grad_slots = jnp.concatenate(
+        [
+            scatter_sum(placed, part * half, half, jnp.float32, 16, (2, 4, 6, 7, 8), part + 1, "scatter_dense")
+            for part in (0, 1)
+        ],
+        axis=0,
+    ).reshape(slot_count, BR, RANK)
+    bias_local = jnp.concatenate(
+        [
+            jnp.sum(grad_anchor[:, :EMB], axis=0),
+            jnp.stack(grads_cross).reshape(-1),
+            grad_bias_one,
+            grad_bias_two,
+            grad_bias_three,
+            jnp.sum(grad_logits)[None],
+        ]
+    )
+    loss_total, grad_proj, grad_head, grad_bias = lax.psum(
+        (loss_local, grad_proj_local, grad_head_local, bias_local), "row"
+    )
+    local_squares = jnp.sum(table_squares) + jnp.sum(grad_slots * grad_slots)
+    squares = lax.psum(local_squares, "row")
+    squares = (
+        squares
+        + jnp.sum(grad_proj * grad_proj)
+        + jnp.sum(grad_head * grad_head)
+        + jnp.sum(grad_bias * grad_bias)
+    )
+    grad_norm = jnp.sqrt(squares)
+    clip_scale = clip_norm / jnp.maximum(grad_norm, clip_norm)
+    table_new = adamw(embed_table, table_moment, table_square, clip_scale * grad_table, rate_table)
+    dense_new = adamw(dense_slots, dense_moment, dense_square, clip_scale * grad_slots, rate_dense)
+    proj_new = adamw(dense_proj, proj_moment, proj_square, clip_scale * grad_proj, rate_small)
+    head_new = adamw(head_weight, head_moment, head_square, clip_scale * grad_head, rate_small)
+    bias_new = adamw(biases, bias_moment, bias_square, clip_scale * grad_bias, rate_small)
+    return (
+        loss_total,
+        grad_norm,
+        table_new[0],
+        table_new[1],
+        table_new[2],
+        dense_new[0],
+        dense_new[1],
+        dense_new[2],
+        proj_new[0],
+        proj_new[1],
+        proj_new[2],
+        head_new[0],
+        head_new[1],
+        head_new[2],
+        bias_new[0],
+        bias_new[1],
+        bias_new[2],
+    )
+
+
 def solution(mesh):
     in_specs = (
         P("row", None, None),
@@ -370,4 +1028,6 @@
         P(),
         P(),
     )
-    return jax.shard_map(body, mesh=mesh, in_specs=in_specs, out_specs=out_specs, check_vma=False)
+    fits = mesh.shape["row"] <= 32
+    chosen = body_counted if fits else body
+    return jax.shard_map(chosen, mesh=mesh, in_specs=in_specs, out_specs=out_specs, check_vma=False)

time: 2770 us -> 1070 us (0.39)
  local copies, waits for them, and re-layouts: 2080 us -> 140 us
  Pallas kernels: 0 us -> 719 us
  other arithmetic: 400 us -> 75.3 us
  matrix products: 126 us -> 45.9 us
  waiting for transfers between devices: 73.9 us -> 8.48 us
    gather x19 -> x2, local copies, waits for them, and re-layouts: 1890 us -> 51.8 us  [the longest x1 29.5 us: body_counted(): placed = jnp.take(stacked, inverse, axis=0, mode='clip')]
    pallas_call x0 -> x5, Pallas kernels: none -> 719 us  [the longest x3 433 us: scatter_sum(): pl.pallas_call(functools.partial(scatter_kernel, base, slices, lags), out...]
    sort x3 -> x1, other arithmetic: 183 us -> 37.7 us  [body_counted(): ordered = lax.sort(key.reshape(-1), is_stable=False)[:live_total]]
    select_n x15 -> x1, other arithmetic: 115 us -> 0.46 us  [body_counted(): key = jnp.where(lanes < hot_counts[:, :, None], key, devices << 21)]
    reduce_scatter x1 -> x0, waiting for transfers between devices: 67.9 us -> none  [body(): lax.psum_scatter(jnp.take(stacked, inverse, axis=0), 'row', scatter_dimen...]
    dot_general x6 -> x4, matrix products: 62.8 us -> 3.3 us  [the longest x1 1.69 us: body_counted(): jnp.dot(hidden, head_weight, precision=highest, preferred_element_type=jn...]
    unnamed x210 -> x158, local copies, waits for them, and re-layouts: 66.7 us -> 23.7 us
    reshape x8 -> x5, local copies, waits for them, and re-layouts: 55.4 us -> 16.5 us  [the longest x1 11.3 us: body_counted(): grad_first.reshape(-1, RANK)]
  transfers between devices with their start and end apart: 5 -> 3, of which waited for: 2 -> 1; matrix products, arithmetic and copies ran while one was open for 79% -> 12% of each run, Pallas kernels for 0% -> 63%
where the time goes in v1:
time: 1070 us; the launch traced here: 1060 us
  Pallas kernels  719 us (67%)
  local copies, waits for them, and re-layouts  140 us (13%)
  other arithmetic  75.3 us (7%)
  matrix products  45.9 us (4%)
  blocking collectives  38.9 us (4%)
  between operations  20.5 us (2%)
    pallas_call x3, Pallas kernels, scatter_sum(): pl.pallas_call(functools.partial(scatter_kernel, base, slices, lags), out...  433 us
    pallas_call x1, Pallas kernels, count_tables(): pl.pallas_call(functools.partial(count_kernel, devices, samples, table_ro...  232 us
    pallas_call x1, Pallas kernels, row_grads(): pl.pallas_call(row_grad_kernel, grid=(F,), in_specs=[pl.BlockSpec((1, tab...  54 us
    psum x1, blocking collectives, body_counted(): lax.psum((loss_local, grad_proj_local, grad_head_local, bias_local), 'row')  38.9 us
    sort x1, other arithmetic, body_counted(): ordered = lax.sort(key.reshape(-1), is_stable=False)[:live_total]  37.7 us
    gather x1, local copies, waits for them, and re-layouts, body_counted(): placed = jnp.take(stacked, inverse, axis=0, mode='clip')  29.5 us
    unnamed x158, local copies, waits for them, and re-layouts  23.7 us
    sub x5, other arithmetic, adamw(): weight - step_rate * (corrected / (jnp.sqrt(scaled) + adam_eps) + decay_r...  23.3 us
  transfers between devices with their start and end apart: 3, of which 1 were waited for; matrix products, arithmetic and copies ran while one was open for 12% of the time, Pallas kernels for 63%

profile of v1, /device:TPU:0, one launch (start us, length us, event | category | flops | bytes accessed | tf_op | source)
XLA Modules:
  0.0 1055.2 jit_solution(1529789441786420885)
XLA Ops:
  7.3 3.3 convert_element_type.79
  11.1 1.9 copy.49
  13.1 1.0 reshape.157
  14.1 37.7 %sort.7 = s32[99840]{0:T(1024)S(1)} sort(s32[99840]{0:T(1024)S(1)} %reshape.157), dimensions={0}, to_apply=%region_0.1 | sort | flops 1697280 | bytes 798720 | tf_op jit(solution)/shard_map/sort | solution.py:852
  51.8 1.0 and.31
  52.8 7.3 all-to-all-start
  61.1 8.4 all-to-all-done
  69.5 0.8 convert_reduce_fusion
  70.6 231.9 %count_tables.1 = (bf16[26,512,4096]{2,1,0:T(8,128)(2,1)}, bf16[32,26,128,128]{3,2,1,0:T(8,128)(2,1)}) custom-call(s32[864]{0:T(1024)S(1)} %reshape.158.off_ref, s32[32,1792]{1,0:T(8,128)S(1)} %pad.4.keys_ref, f32[26,512,128]{2,1,0:T(8,128)} %table_ref.1), custom_call_target="tpu_custom_call" | custom-call | tf_op jit(solution)/shard_map/count_tables/pallas_call | solution.py:207
  302.5 135.2 %scatter_pooled.1 = bf16[3328,128]{1,0:T(8,128)(2,1)} custom-call(bf16[4,2,2,2,3328,128]{5,4,3,2,1,0:T(8,128)(2,1)} %bitcast.115), custom_call_target="tpu_custom_call" | custom-call | tf_op jit(solution)/shard_map/scatter_pooled/pallas_call | solution.py:473
  437.8 1.5 copy.51
  439.4 22.3 %gather_fusion = bf16[240,128,512]{2,1,0:T(8,128)(2,1)} fusion(bf16[384,128,512]{2,1,0:T(8,128)(2,1)} %all-gather.3.cloned.1.call-done, s32[1024]{0:T(1024)S(1)} %pad_clamp_fusion.1), kind=kCustom, calls=%fused_computation | custom fusion | bytes 62915520 | tf_op jit(solution)/shard_map/jit(_take)/gather | solution.py:837
  461.7 1.3 slice.130
  463.0 3.1 slice.129
  466.1 6.6 slice.128
  472.8 13.6 %fusion.88 = (bf16[27,128,512]{2,1,0:T(8,128)(2,1)}, bf16[27,128,512]{2,1,0:T(8,128)(2,1)}, bf16[27,128,512]{2,1,0:T(8,128)(2,1)}, bf16[27,128,512]{2,1,0:T(8,12...) fusion(bf16[240,128,512]{2,1,0:T(8,128)(2,1)} %gather_fusion), kind=kLoop, calls=%fused_computation.182 | loop fusion | bytes 42467328 | tf_op jit(solution)/shard_map/slice | solution.py:873
  486.4 4.1 reshape.161
  490.5 11.4 %reshape.160 = bf16[3456,1024]{1,0:T(8,128)(2,1)} reshape(bf16[54,128,512]{2,1,0:T(8,128)(2,1)} %slice.128) | data formatting | bytes 14155776 | tf_op jit(solution)/shard_map/reshape | solution.py:43
  501.9 2.8 convolution_convert_fusion.14
  505.0 1.3 fusion.13
  507.6 1.1 copy-done.2
  508.8 1.4 fusion.12
  511.5 1.9 copy-done.4
  513.3 2.6 add_convert_fusion
  516.0 1.2 convolution_add_fusion.7
  518.8 1.7 fusion.86
  520.5 1.3 fusion.92
  521.9 1.6 fusion.91
  523.5 3.3 multiply_convert_fusion.2
  526.9 1.8 convolution_convert_fusion.11
  528.7 1.3 multiply_convert_fusion.1
  530.7 2.1 multiply_reduce_fusion.1
  533.6 1.7 copy-done.6
  535.2 1.8 fusion.7
  537.1 1.2 copy-done.24
  538.3 1.0 slice.138
  539.6 3.3 convolution_convert_fusion.7
  542.9 4.1 reshape.165
  547.0 4.9 convolution_convert_fusion
  551.8 11.3 %reshape.164 = bf16[6912,512]{1,0:T(8,128)(2,1)} reshape(bf16[3456,1024]{1,0:T(8,128)(2,1)} %convolution_convert_fusion) | data formatting | bytes 14155776 | tf_op jit(solution)/shard_map/reshape | solution.py:919
  563.2 1.1 fusion.1
  564.4 1.1 fusion.2
  565.5 1.1 fusion.5
  566.7 1.1 fusion.3
  567.9 1.1 fusion.6
  569.0 1.1 fusion.4
  570.1 1.3 pad_maximum_fusion
  571.4 1.3 pad_maximum_fusion.1
  572.8 5.1 constant_dynamic-update-slice_fusion.3
  577.9 5.1 constant_dynamic-update-slice_fusion.2
  583.0 3.3 constant_dynamic-update-slice_fusion.1
  586.4 1.4 constant_dynamic-update-slice_fusion
  587.8 1.7 fusion.10
  590.1 29.5 %gather_fusion.1 = bf16[384,128,512]{2,1,0:T(8,128)(2,1)} fusion(bf16[241,128,512]{2,1,0:T(8,128)(2,1)} %bitcast.20, s32[1024]{0:T(1024)S(1)} %pad_clamp_fusion), kind=kCustom, calls=%fused_computation.1 | custom fusion | bytes 100664832 | tf_op jit(solution)/shard_map/jit(_take)/gather | solution.py:931
  619.7 172.7 %scatter_dense.3 = f32[768,512]{1,0:T(8,128)} custom-call(bf16[4,2,2,2,1536,512]{5,4,3,2,1,0:T(8,128)(2,1)} %bitcast.93), custom_call_target="tpu_custom_call" | custom-call | tf_op jit(solution)/shard_map/scatter_dense/pallas_call | solution.py:473
  792.4 125.5 %scatter_dense.2 = f32[768,512]{1,0:T(8,128)} custom-call(bf16[4,2,2,2,1536,512]{5,4,3,2,1,0:T(8,128)(2,1)} %bitcast.94), custom_call_target="tpu_custom_call" | custom-call | tf_op jit(solution)/shard_map/scatter_dense/pallas_call | solution.py:473
  918.1 0.9 slice_reduce_fusion
  919.9 2.8 multiply_reduce_fusion
  922.7 1.0 convolution_bitcast_fusion
  924.0 54.0 %row_grads.1 = (f32[26,512,128]{2,1,0:T(8,128)}, f32[8,128]{1,0:T(8,128)S(1)}) custom-call(bf16[26,512,4096]{2,1,0:T(8,128)(2,1)} %get-tuple-element.22.counts_ref, bf16[4096,3328]{1,0:T(8,128)(2,1)} %all-gather.5.cloned.1.call-done.grads_ref), custom_call_target="tpu_custom_call" | custom-call | tf_op jit(solution)/shard_map/row_grads/pallas_call | solution.py:242
  980.0 38.9 %all-reduce.1 = (f32[]{:T(128)}, f32[]{:T(128)}, f32[13,128]{1,0:T(8,128)S(1)}, f32[512]{0:T(512)S(1)}, f32[13057]{0:T(1024)S(1)}) all-reduce(f32[]{:T(128)} %get-tuple-element.62, f32[]{:T(128)S(6)} %add.278, f32[13,128]{1,0:T(8,128)S(1)} %convolution_bitcast_fusion, f32[512]{0:T(512)S(1)} %bitcast.122, ...), channel_id=1, replica_groups=mesh['row'=32] {'row'}, use_global_device_ids=true, to_apply=%region_3.4 | all-reduce | flops 15235 | bytes 121880 | tf_op jit(solution)/shard_map/psum | solution.py:950
  1025.0 0.7 multiply_subtract_fusion.2
  1025.7 7.0 multiply_subtract_fusion.1
  1032.7 14.3 %multiply_subtract_fusion = (f32[26,512,128]{2,1,0:T(8,128)}, f32[26,512,128]{2,1,0:T(8,128)}, f32[26,512,128]{2,1,0:T(8,128)}) fusion(f32[26,512,128]{2,1,0:T(8,128)S(1)} %bitcast.114, f32[26,512,128]{2,1,0:T(8,128)} %get-tuple-element.24, f32[]{:T(128)S(6)} %div.106, f32[26,512,128]{2,1,0:T(8,128)} %param.26, f32[26,512,128]{2,1,0:T(8,128)} %param.27), kind=kLoop, calls=%fused_computation.7 | loop fusion | flops 27262976 | bytes 47710212 | tf_op jit(solution)/shard_map/sub | solution.py:153
  (202 shorter events, 14.2 us)
Async XLA Ops:
  7.2 53.6 %copy-start = (f32[128,13]{0,1:T(8,128)S(1)}, f32[128,13]{0,1:T(8,128)}, u32[]{:S(2)}) copy-start(f32[128,13]{0,1:T(8,128)} %param.22) | copy-start | bytes 19972
  7.2 3.4 copy-start.54
  7.2 3.4 copy-start.41
  7.2 432.2 %all-gather.3.cloned.1.call-start = ((), (), s32[]{:S(2)}) async-start(), calls=%async_computation.1 | async-start | bytes 51904512 | tf_op jit(solution)/shard_map/all_gather | solution.py:836
  11.1 49.1 %copy-start.45 = (f32[13057]{0:T(1024)S(1)}, f32[13057]{0:T(1024)}, u32[]{:S(2)}) copy-start(f32[13057]{0:T(1024)} %param.37) | copy-start | bytes 156688
  11.1 49.6 %copy-start.58 = (s32[240]{0:T(256)S(1)}, s32[240]{0:T(256)}, u32[]{:S(2)}) copy-start(s32[240]{0:T(256)} %param.24) | copy-start | bytes 2884
  11.1 49.7 %slice-start.6 = ((f32[13057]{0:T(1024)}), f32[128]{0:T(128)S(1)}, s32[]{:S(2)}) async-start(f32[13057]{0:T(1024)} %param.37), calls=%async_computation.9 | async-start | bytes 1024 | tf_op jit(solution)/shard_map/slice | solution.py:52
  11.1 49.7 %copy-start.52 = (f32[13,128]{1,0:T(8,128)S(1)}, f32[13,128]{1,0:T(8,128)}, u32[]{:S(2)}) copy-start(f32[13,128]{1,0:T(8,128)} %param.31) | copy-start | bytes 19972
  52.8 16.7 %all-to-all-start = ((s32[32,1,1612]{2,1,0:T(1,128)}), s32[32,1,1612]{2,1,0:T(1,128)S(1)}, u32[]{:S(2)}, u32[]{:S(2)}) async-start(s32[32,1,1612]{2,1,0:T(1,128)} %and.31), calls=%async_computation | async-start | bytes 425984 | tf_op jit(solution)/shard_map/all_to_all | solution.py:854
  60.2 863.9 %all-gather.5.cloned.1.call-start = ((), (), s32[]{:S(2)}) async-start(), calls=%async_computation.2 | async-start | bytes 28114944 | tf_op jit(solution)/shard_map/all_gather | solution.py:906
  501.9 3.1 copy-start.5
  504.7 1.6 copy-start.29
  505.0 2.0 copy-start.1
  506.3 1.3 copy-start.20
  506.3 2.5 copy-start.2
  507.6 2.6 copy-start.31
  508.8 2.0 copy-start.3
  510.2 5.8 copy-start.9
  510.2 3.2 copy-start.4
  510.8 5.2 slice-start
  511.4 4.6 copy-start.33
  513.3 2.7 slice-start.1
  516.0 1.9 copy-start.25
  517.3 4.6 copy-start.26
  517.3 1.5 copy-start.55
  517.3 1.5 copy-start.65
  518.5 3.4 copy-start.66
  518.8 3.1 copy-start.42
  520.5 3.0 copy-start.63
  521.9 1.7 copy-start.44
  523.5 3.3 copy-start.39
  530.0 2.8 copy-start.18
  530.7 2.2 copy-start.37
  530.7 2.8 copy-start.10
  530.7 2.8 copy-start.23
  532.9 4.2 copy-start.16
  532.9 2.4 copy-start.6
  533.5 3.5 copy-start.27
  539.6 7.3 copy-start.8
  539.6 7.3 copy-start.40
  551.8 11.3 %copy-start.28 = (bf16[128,512]{1,0:T(8,128)(2,1)S(1)}, bf16[128,512]{1,0:T(8,128)(2,1)}, u32[]{:S(2)}) copy-start(bf16[128,512]{1,0:T(8,128)(2,1)} %copy-done.27) | copy-start | bytes 393220
  572.8 10.2 slice-start.2
  577.9 5.1 slice-start.3
  583.0 3.3 copy-start.22
  586.4 1.4 copy-start.43
  586.4 1.4 copy-start.64
  586.4 1.4 copy-start.67
  792.4 125.5 %copy-start.49 = (f32[3456]{0:T(1024)S(1)}, f32[3456]{0:T(1024)}, u32[]{:S(2)}) copy-start(f32[3456]{0:T(1024)} %get-tuple-element.25) | copy-start | bytes 41476
  792.4 125.6 %copy-start.48 = (f32[3456]{0:T(1024)S(1)}, f32[3456]{0:T(1024)}, u32[]{:S(2)}) copy-start(f32[3456]{0:T(1024)} %get-tuple-element.26) | copy-start | bytes 41476
  792.4 125.6 %copy-start.47 = (f32[3456]{0:T(1024)S(1)}, f32[3456]{0:T(1024)}, u32[]{:S(2)}) copy-start(f32[3456]{0:T(1024)} %get-tuple-element.27) | copy-start | bytes 41476
  792.4 126.6 %copy-start.60 = (f32[1024]{0:T(1024)S(1)}, f32[1024]{0:T(1024)}, u32[]{:S(2)}) copy-start(f32[1024]{0:T(1024)} %get-tuple-element.74) | copy-start | bytes 12292
  792.4 126.6 %copy-start.59 = (f32[1024]{0:T(1024)S(1)}, f32[1024]{0:T(1024)}, u32[]{:S(2)}) copy-start(f32[1024]{0:T(1024)} %get-tuple-element.76) | copy-start | bytes 12292
  792.4 127.5 %copy-start.11 = (f32[768,512]{1,0:T(8,128)S(1)}, f32[768,512]{1,0:T(8,128)}, u32[]{:S(2)}) copy-start(f32[768,512]{1,0:T(8,128)} %scatter_dense.3) | copy-start | bytes 4718596
  924.0 99.3 %copy-start.12 = (f32[768,512]{1,0:T(8,128)S(1)}, f32[768,512]{1,0:T(8,128)}, u32[]{:S(2)}) copy-start(f32[768,512]{1,0:T(8,128)} %scatter_dense.2) | copy-start | bytes 4718596
  978.0 45.7 %copy-start.61 = (f32[512]{0:T(512)S(1)}, f32[512]{0:T(512)}, u32[]{:S(2)}) copy-start(f32[512]{0:T(512)} %param.35) | copy-start | bytes 6148
  978.0 45.7 %copy-start.62 = (f32[512]{0:T(512)S(1)}, f32[512]{0:T(512)}, u32[]{:S(2)}) copy-start(f32[512]{0:T(512)} %param.36) | copy-start | bytes 6148
  978.0 46.4 %copy-start.53 = (f32[13,128]{1,0:T(8,128)S(1)}, f32[13,128]{1,0:T(8,128)}, u32[]{:S(2)}) copy-start(f32[13,128]{1,0:T(8,128)} %param.31) | copy-start | bytes 19972
  978.0 46.4 %copy-start.56 = (f32[13,128]{1,0:T(8,128)S(1)}, f32[13,128]{1,0:T(8,128)}, u32[]{:S(2)}) copy-start(f32[13,128]{1,0:T(8,128)} %param.32) | copy-start | bytes 19972
  978.1 46.3 %copy-start.57 = (f32[13,128]{1,0:T(8,128)S(1)}, f32[13,128]{1,0:T(8,128)}, u32[]{:S(2)}) copy-start(f32[13,128]{1,0:T(8,128)} %param.33) | copy-start | bytes 19972
  978.1 47.0 %copy-start.46 = (f32[13057]{0:T(1024)S(1)}, f32[13057]{0:T(1024)}, u32[]{:S(2)}) copy-start(f32[13057]{0:T(1024)} %param.37) | copy-start | bytes 156688
  978.1 47.0 %copy-start.50 = (f32[13057]{0:T(1024)S(1)}, f32[13057]{0:T(1024)}, u32[]{:S(2)}) copy-start(f32[13057]{0:T(1024)} %param.38) | copy-start | bytes 156688
  978.1 47.0 %copy-start.51 = (f32[13057]{0:T(1024)S(1)}, f32[13057]{0:T(1024)}, u32[]{:S(2)}) copy-start(f32[13057]{0:T(1024)} %param.39) | copy-start | bytes 156688
  1023.4 9.3 slice-start.4
  1025.7 7.0 slice-start.5
  (14 other events, 16.8 us)
Sparse Core Ops, SparseCore 0:
  11.5 278.7 all-gather.2
  539.5 226.3 all-gather.4

commit v2 on v1

--- a/solution.py
+++ b/solution.py
@@ -154,9 +154,9 @@
     return (weight, moment, square)
 
 
-def count_kernel(devices, samples, table_rows, off_ref, keys_ref, table_ref, counts_ref, partial_ref):
+def count_kernel(devices, samples, table_rows, off_ref, most_ref, keys_ref, table_ref, counts_ref, partial_ref, low_ref, rows_ref, samples_ref):
     feature = pl.program_id(0)
-    low_table = table_ref[0].T.astype(jnp.bfloat16)
+    low_ref[...] = table_ref[0].T.astype(jnp.bfloat16)
     lane = lax.broadcasted_iota(jnp.int32, (1, samples), 1)
     row_iota = lax.broadcasted_iota(jnp.int32, (table_rows, 2 * samples), 0)
     sample_iota = lax.broadcasted_iota(jnp.int32, (2 * samples, 2 * samples), 0)
@@ -172,34 +172,69 @@
         row = jnp.where(valid, (turned >> 7) & (table_rows - 1), -1)
         return row, turned & (samples - 1)
 
+    def product(row, sample):
+        row_hot = jnp.where(row_iota == row, 1.0, 0.0).astype(jnp.bfloat16)
+        sample_hot = jnp.where(sample_iota == sample, 1.0, 0.0).astype(jnp.bfloat16)
+        return lax.dot_general(
+            row_hot, sample_hot, (((1,), (1,)), ((), ())), preferred_element_type=jnp.float32
+        )
+
     def counted(first, turn):
         row_a, sample_a = window(first, turn)
         row_b, sample_b = window(first + 1, turn)
-        row = jnp.concatenate([row_a, row_b], axis=1)
-        sample = jnp.concatenate([sample_a, sample_b + samples], axis=1)
-        row_hot = (row_iota == row).astype(jnp.float32).astype(jnp.bfloat16)
-        sample_hot = (sample_iota == sample).astype(jnp.float32).astype(jnp.bfloat16)
-        return lax.dot_general(
-            row_hot, sample_hot, (((1,), (1,)), ((), ())), preferred_element_type=jnp.float32
+        return product(
+            jnp.concatenate([row_a, row_b], axis=1),
+            jnp.concatenate([sample_a, sample_b + samples], axis=1),
         )
 
+    def span(first):
+        return pl.ds(pl.multiple_of(first * samples, 2 * samples), 2 * samples)
+
+    for source in range(devices):
+        row, sample = window(source, 0)
+        half = pl.ds((source % 2) * samples, samples)
+        rows_ref[pl.ds(source // 2, 1), half] = row
+        samples_ref[pl.ds(source // 2, 1), half] = sample + (source % 2) * samples
+
     def pair(step, carry):
+        total = product(rows_ref[pl.ds(step, 1), :], samples_ref[pl.ds(step, 1), :])
+        counts_ref[0, :, span(step * 2)] = total.astype(jnp.bfloat16)
+        return carry
+
+    lax.fori_loop(0, devices // 2, pair, 0, unroll=devices // 2)
+
+    def late(step, carry):
         first = step * 2
-        total = counted(first, 0)
         spans = [
             off_ref[(first + i) * (F + 1) + feature + 1] - off_ref[(first + i) * (F + 1) + feature]
             for i in (0, 1)
         ]
         turns = (jnp.maximum(spans[0], spans[1]) + samples - 1) // samples
-        total = lax.fori_loop(1, turns, lambda turn, acc: acc + counted(first, turn), total)
-        low = total.astype(jnp.bfloat16)
-        counts_ref[0, :, pl.ds(pl.multiple_of(first * samples, 2 * samples), 2 * samples)] = low
-        part = jnp.dot(low_table, low, preferred_element_type=jnp.float32).astype(jnp.bfloat16)
-        partial_ref[first, 0] = part[:, :samples]
-        partial_ref[first + 1, 0] = part[:, samples:]
+
+        @pl.when(turns > 1)
+        def again():
+            total = lax.fori_loop(1, turns, lambda turn, acc: acc + counted(first, turn), counted(first, 0))
+            counts_ref[0, :, span(first)] = total.astype(jnp.bfloat16)
+
         return carry
 
-    lax.fori_loop(0, devices // 2, pair, 0, unroll=2)
+    @pl.when(most_ref[feature] > samples)
+    def crowded():
+        lax.fori_loop(0, devices // 2, late, 0)
+
+    group = devices
+
+    def pool(step, carry):
+        part = jnp.dot(
+            low_ref[...],
+            counts_ref[0, :, pl.ds(pl.multiple_of(step * group * samples, group * samples), group * samples)],
+            preferred_element_type=jnp.float32,
+        ).astype(jnp.bfloat16)
+        for i in range(group):
+            partial_ref[step * group + i, 0] = part[:, i * samples : (i + 1) * samples]
+        return carry
+
+    lax.fori_loop(0, devices // group, pool, 0)
 
 
 def count_tables(offsets, keys, embed_table, devices, samples):
@@ -207,15 +242,20 @@
     return pl.pallas_call(
         functools.partial(count_kernel, devices, samples, table_rows),
         grid_spec=pltpu.PrefetchScalarGridSpec(
-            num_scalar_prefetch=1,
+            num_scalar_prefetch=2,
             grid=(F,),
             in_specs=[
-                pl.BlockSpec(keys.shape, lambda f, off: (0, 0)),
-                pl.BlockSpec((1, table_rows, EMB), lambda f, off: (f, 0, 0)),
+                pl.BlockSpec(keys.shape, lambda f, off, most: (0, 0)),
+                pl.BlockSpec((1, table_rows, EMB), lambda f, off, most: (f, 0, 0)),
             ],
             out_specs=[
-                pl.BlockSpec((1, table_rows, devices * samples), lambda f, off: (f, 0, 0)),
-                pl.BlockSpec((devices, 1, EMB, samples), lambda f, off: (0, f, 0, 0)),
+                pl.BlockSpec((1, table_rows, devices * samples), lambda f, off, most: (f, 0, 0)),
+                pl.BlockSpec((devices, 1, EMB, samples), lambda f, off, most: (0, f, 0, 0)),
+            ],
+            scratch_shapes=[
+                pltpu.VMEM((EMB, table_rows), jnp.bfloat16),
+                pltpu.VMEM((devices // 2, 2 * samples), jnp.int32),
+                pltpu.VMEM((devices // 2, 2 * samples), jnp.int32),
             ],
         ),
         out_shape=[
@@ -224,7 +264,7 @@
         ],
         compiler_params=pltpu.CompilerParams(vmem_limit_bytes=48 << 20),
         name="count_tables",
-    )(offsets, keys, embed_table)
+    )(offsets.reshape(-1), jnp.max(offsets[:, 1:] - offsets[:, :-1], axis=0), keys, embed_table)
 
 
 def row_grad_kernel(counts_ref, grads_ref, out_ref, square_ref):
@@ -496,134 +536,352 @@
     )(array.reshape(4, 2, 2, 2, -1, lanes))
 
 
-def spread_kernel(slices, lags, x_ref, out_ref, local_sem, send_up, recv_up, send_down, recv_down,
-    send_one, recv_one, send_two, recv_two, send_core, recv_core):
+def total_kernel(x_ref, out_ref, held, got, send_sem, recv_sem):
     z, y, x, core = place()
-    rows = x_ref.shape[0] // slices
-
-    def span(q):
-        return pl.ds(q * rows, rows)
-
-    def local(q):
-        return pltpu.make_async_copy(x_ref.at[span(q)], out_ref.at[z, y, x, core, span(q)], local_sem.at[q])
-
-    def to_up(q, k):
-        block = z - k
-        target = out_ref.at[block, y, x, core, span(q)]
-        source = x_ref.at[span(q)] if k == 0 else target
-        return remote(source, target, send_up.at[q, k], recv_up.at[q, k], (z + 1, y, x, core))
-
-    def to_down(q, k):
-        block = z + k
-        target = out_ref.at[block, y, x, core, span(q)]
-        source = x_ref.at[span(q)] if k == 0 else target
-        return remote(source, target, send_down.at[q, k], recv_down.at[q, k], (z - 1, y, x, core))
-
-    def to_one(q):
-        block = out_ref.at[:, y, x, core, span(q)]
-        where = (z, y, 1 - x, core) if q % 2 == 0 else (z, 1 - y, x, core)
-        return remote(block, block, send_one.at[q], recv_one.at[q], where)
-
-    def to_two(q):
-        if q % 2 == 0:
-            block, where = out_ref.at[:, y, :, core, span(q)], (z, 1 - y, x, core)
+    partners = (
+        (z, y, x, 1 - core),
+        (z, y, 1 - x, core),
+        (z, 1 - y, x, core),
+        (z + 1 - 2 * (z % 2), y, x, core),
+        ((z + 2) % 4, y, x, core),
+    )
+    barrier = pltpu.get_barrier_semaphore()
+    for where in partners:
+        pl.semaphore_signal(barrier, inc=1, device_id=device_at(*where), device_id_type=MESH)
+    pl.semaphore_wait(barrier, len(partners))
+    sends = []
+    for step, where in enumerate(partners):
+        source = x_ref if step == 0 else held.at[step]
+        copy = remote(source, got.at[step], send_sem.at[step], recv_sem.at[step], where)
+        copy.start()
+        copy.wait_recv()
+        sends.append(copy)
+        if step < len(partners) - 1:
+            held[step + 1] = source[...] + got[step]
         else:
-            block, where = out_ref.at[:, :, x, core, span(q)], (z, y, 1 - x, core)
-        return remote(block, block, send_two.at[q], recv_two.at[q], where)
-
-    def to_core(q):
-        block = out_ref.at[:, :, :, core, span(q)]
-        return remote(block, block, send_core.at[q], recv_core.at[q], (z, y, x, 1 - core))
-
-    def stage_start(q):
-        @pl.when(z < 3)
-        def rise():
-            to_up(q, 0).start()
-
-        @pl.when(z > 0)
-        def fall():
-            to_down(q, 0).start()
-
-    def stage_chain(q):
-        for k in range(3):
-
-            @pl.when(z - 1 - k >= 0)
-            def rise():
-                to_up(q, k).wait_recv()
-                if k < 2:
-
-                    @pl.when(z < 3)
-                    def go_on():
-                        to_up(q, k + 1).start()
-
-            @pl.when(z + 1 + k <= 3)
-            def fall():
-                to_down(q, k).wait_recv()
-                if k < 2:
-
-                    @pl.when(z > 0)
-                    def go_on():
-                        to_down(q, k + 1).start()
-
-        local(q).wait()
-        to_one(q).start()
-
-    def stage_one(q):
-        to_one(q).wait_recv()
-        to_two(q).start()
-
-    def stage_two(q):
-        to_two(q).wait_recv()
-        to_core(q).start()
-
-    def stage_core(q):
-        to_core(q).wait_recv()
-
-    for q in range(slices):
-        local(q).start()
-    greet(z, y, x, core)
-    for q in range(slices):
-        stage_start(q)
-    for tick in range(slices + lags[2]):
-        for lag, stage in zip((0,) + lags, (stage_chain, stage_one, stage_two, stage_core)):
-            if 0 <= tick - lag < slices:
-                stage(tick - lag)
-    for q in range(slices):
-        for k in range(3):
-
-            @pl.when(jnp.logical_and(z < 3, z - k >= 0))
-            def rise():
-                to_up(q, k).wait_send()
-
-            @pl.when(jnp.logical_and(z > 0, z + k <= 3))
-            def fall():
-                to_down(q, k).wait_send()
-
-        to_one(q).wait_send()
-        to_two(q).wait_send()
-        to_core(q).wait_send()
-
-
-def spread(array, slices, lags, collective_id, name):
-    chunk, lanes = array.shape
-    dma = pltpu.SemaphoreType.DMA
-    gathered = pl.pallas_call(
-        functools.partial(spread_kernel, slices, lags),
-        out_shape=jax.ShapeDtypeStruct((4, 2, 2, 2, chunk, lanes), array.dtype),
-        in_specs=[pl.BlockSpec(memory_space=pl.ANY)],
-        out_specs=pl.BlockSpec(memory_space=pl.ANY),
+            out_ref[...] = source[...] + got[step]
+    for copy in sends:
+        copy.wait_send()
+
+
+def total_of(array, collective_id):
+    steps = 5
+    return pl.pallas_call(
+        total_kernel,
+        out_shape=jax.ShapeDtypeStruct(array.shape, array.dtype),
+        in_specs=[pl.BlockSpec(memory_space=pltpu.VMEM)],
+        out_specs=pl.BlockSpec(memory_space=pltpu.VMEM),
         scratch_shapes=[
-            dma((slices,)),
-            dma((slices, 3)), dma((slices, 3)),
-            dma((slices, 3)), dma((slices, 3)),
-            dma((slices,)), dma((slices,)),
-            dma((slices,)), dma((slices,)),
-            dma((slices,)), dma((slices,)),
+            pltpu.VMEM((steps,) + array.shape, array.dtype),
+            pltpu.VMEM((steps,) + array.shape, array.dtype),
+            pltpu.SemaphoreType.DMA((steps,)),
+            pltpu.SemaphoreType.DMA((steps,)),
         ],
         compiler_params=pltpu.CompilerParams(collective_id=collective_id, has_side_effects=True),
-        name=name,
+        name="total_small",
     )(array)
-    return gathered.reshape(32 * chunk, lanes)
+
+
+def slot_kernel(scale_ref, tiles_ref, weight_ref, moment_ref, square_ref, weight_out, moment_out, square_out):
+    columns = []
+    for h in range(4):
+        pieces = [tiles_ref[4 * j + h, 0] for j in range(8)]
+        columns.append(jnp.concatenate(pieces, axis=0))
+    gradient = scale_ref[0] * jnp.concatenate(columns, axis=1).astype(jnp.float32)
+    weight, moment, square = adamw(weight_ref[0], moment_ref[0], square_ref[0], gradient, rate_dense)
+    weight_out[0] = weight
+    moment_out[0] = moment
+    square_out[0] = square
+
+
+def slot_update(scale, tiles, weight, moment, square):
+    slots = weight.shape[0]
+    block = pl.BlockSpec((1, BR, RANK), lambda s: (s, 0, 0))
+    return tuple(
+        pl.pallas_call(
+            slot_kernel,
+            grid=(slots,),
+            in_specs=[
+                pl.BlockSpec(memory_space=pltpu.SMEM),
+                pl.BlockSpec((32, 1, 16, 128), lambda s: (0, s, 0, 0)),
+                block,
+                block,
+                block,
+            ],
+            out_specs=[block] * 3,
+            out_shape=[jax.ShapeDtypeStruct(weight.shape, jnp.float32)] * 3,
+            name="slot_update",
+        )(scale[None], tiles, weight, moment, square)
+    )
+
+
+NN = (((1,), (0,)), ((), ()))
+NT = (((1,), (1,)), ((), ()))
+TN = (((0,), (0,)), ((), ()))
+CHUNKS = 3
+CBLK = 9
+CW = CBLK * BR
+FCH = 9
+FBLK = 6
+ONE_AT = 6 * CHUNKS * CBLK
+TWO_AT = ONE_AT + FCH * FBLK
+THREE_AT = TWO_AT + 16
+GROUPS = tuple((k * 27, 27) for k in (0, 3, 1, 4, 2, 5)) + ((ONE_AT, 54), (TWO_AT, 16), (THREE_AT, 8))
+GELU_A = 0.7978845608028654
+GELU_B = 0.044715
+
+
+def mul(left, right, dims):
+    return lax.dot_general(left, right, dims, preferred_element_type=jnp.float32)
+
+
+def gelu_of(value):
+    return 0.5 * value * (1.0 + jnp.tanh(GELU_A * (value + GELU_B * (value * value * value))))
+
+
+def gelu_slope(value):
+    bend = jnp.tanh(GELU_A * (value + GELU_B * (value * value * value)))
+    inner = GELU_A * (1.0 + 3.0 * GELU_B * (value * value))
+    return 0.5 * (1.0 + bend) + 0.5 * value * (1.0 - bend * bend) * inner
+
+
+def dense_kernel(
+    batch, tiles_hbm, pooled_ref, dense_ref, label_ref, head_ref, last_ref, cross_bias_ref, one_bias_ref,
+    two_bias_ref, three_bias_ref, grads_hbm, grad_pooled_ref, grad_dense_ref, cross_grad_ref, small_ref,
+    tiles, anchor, current, mixing, low, grad_anchor, wide_one, wide_two, stage, load_sem, store_sem,
+):
+    samples = dense_ref.shape[0]
+    bf16, f32 = jnp.bfloat16, jnp.float32
+
+    def load(group):
+        first, count = GROUPS[group]
+        return pltpu.make_async_copy(
+            tiles_hbm.at[:, pl.ds(first, count)], tiles.at[:, pl.ds(first, count)], load_sem.at[group]
+        )
+
+    for group in range(len(GROUPS)):
+        load(group).start()
+
+    def matrix(first, count):
+        columns = []
+        for h in range(4):
+            pieces = [tiles[4 * j + h, pl.ds(first, count)] for j in range(8)]
+            columns.append(jnp.stack(pieces, axis=1).reshape(count * BR, 128))
+        return jnp.concatenate(columns, axis=1)
+
+    def store(slot, first, count):
+        return pltpu.make_async_copy(
+            stage.at[slot, :, pl.ds(0, count)], grads_hbm.at[:, pl.ds(first, count)], store_sem.at[slot]
+        )
+
+    def emit(slot, first, count, value):
+        value = value.astype(bf16).reshape(count, BR, RANK)
+        for j in range(8):
+            for h in range(4):
+                stage[slot, 4 * j + h, pl.ds(0, count)] = value[:, 16 * j : 16 * j + 16, 128 * h : 128 * h + 128]
+        store(slot, first, count).start()
+
+    for i in range(F + 1):
+        block = dense_ref[...] if i == 0 else pooled_ref[(i - 1) * EMB : i * EMB, :].astype(f32).T
+        c, at = i // CBLK, (i % CBLK) * BR
+        anchor[c, :, at : at + BR] = block
+        current[c, :, at : at + BR] = block
+        low[c, :, at : at + BR] = block.astype(bf16)
+
+    reduced = []
+    for depth in range(LAYERS):
+        load(2 * depth).wait()
+        down, up = depth * 27, (LAYERS + depth) * 27
+        total = lax.fori_loop(
+            0,
+            CHUNKS,
+            lambda c, acc: acc + mul(low[depth * CHUNKS + c], matrix(down + c * CBLK, CBLK), NN),
+            jnp.zeros((samples, RANK), f32),
+        )
+        small = total.astype(bf16)
+        reduced.append(small)
+        load(2 * depth + 1).wait()
+
+        @pl.loop(0, CHUNKS)
+        def mix(c):
+            value = mul(small, matrix(up + c * CBLK, CBLK), NT) + cross_bias_ref[pl.ds(depth * CHUNKS + c, 1), :]
+            mixing[depth * CHUNKS + c] = value
+            after = anchor[c] * value + current[c]
+            current[c] = after
+            if depth + 1 < LAYERS:
+                low[(depth + 1) * CHUNKS + c] = after.astype(bf16)
+
+    at_row = lax.broadcasted_iota(jnp.int32, (BR, 4 * BR), 0)
+    at_col = lax.broadcasted_iota(jnp.int32, (BR, 4 * BR), 1)
+    widen = jnp.where(at_col % (2 * BR) == 2 * at_row + at_col // (2 * BR), 1.0, 0.0).astype(bf16)
+    pick_row = lax.broadcasted_iota(jnp.int32, (8 * BR, BR), 0)
+    pick_col = lax.broadcasted_iota(jnp.int32, (8 * BR, BR), 1)
+    pick = jnp.where(pick_row % (2 * BR) == 2 * pick_col + pick_row // (4 * BR), 1.0, 0.0).astype(bf16)
+
+    def widened(block):
+        spreaded = mul(block, widen, NN).astype(bf16)
+        return jnp.concatenate([spreaded[:, : 2 * BR], spreaded[:, 2 * BR :]], axis=0)
+
+    def narrowed(wide):
+        parts = []
+        for p in range(2):
+            value = wide[p * samples : (p + 1) * samples]
+            high = value.astype(bf16)
+            parts += [high, (value - high.astype(f32)).astype(bf16)]
+        return mul(jnp.concatenate(parts, axis=1), pick, NN)
+
+    load(6).wait()
+
+    def first_step(c, acc):
+        for m in range(3):
+            at = pl.multiple_of((c % 3) * 3 * BR + m * BR, BR)
+            wide_one[c, :, m * 2 * BR : (m + 1) * 2 * BR] = widened(current[c // 3, :, pl.ds(at, BR)].astype(bf16))
+        return acc + mul(wide_one[c], matrix(ONE_AT + c * FBLK, FBLK), NN)
+
+    total = lax.fori_loop(0, FCH, first_step, jnp.zeros((2 * samples, RANK), f32))
+    pre_one = [total[p * samples : (p + 1) * samples] + one_bias_ref[pl.ds(p, 1), :] for p in range(2)]
+    load(7).wait()
+    total = jnp.zeros((2 * samples, RANK), f32)
+    for c in range(2):
+        hidden = gelu_of(pre_one[c]).astype(bf16)
+        for m in range(4):
+            wide_two[c, :, m * 2 * BR : (m + 1) * 2 * BR] = widened(hidden[:, m * BR : (m + 1) * BR])
+        total = total + mul(wide_two[c], matrix(TWO_AT + c * 8, 8), NN)
+    pre_two = [total[p * samples : (p + 1) * samples] + two_bias_ref[pl.ds(p, 1), :] for p in range(2)]
+    load(8).wait()
+    hidden_two = jnp.concatenate([gelu_of(value).astype(bf16) for value in pre_two], axis=1)
+    pre_three = mul(hidden_two, matrix(THREE_AT, 8), NN) + three_bias_ref[...]
+    hidden_three = gelu_of(pre_three)
+    head = head_ref[...]
+    logits = jnp.sum(hidden_three * head, axis=1, keepdims=True) + last_ref[...]
+    labels = label_ref[...]
+    losses = jnp.maximum(logits, 0.0) + jnp.log1p(jnp.exp(-jnp.abs(logits))) - labels * logits
+    grad_logits = (1.0 / (1.0 + jnp.exp(-logits)) - labels) / batch
+    small_ref[6:7, :] = jnp.broadcast_to(jnp.sum(losses, axis=0, keepdims=True), (1, RANK))
+    small_ref[7:8, :] = jnp.broadcast_to(jnp.sum(grad_logits, axis=0, keepdims=True), (1, RANK))
+    small_ref[5:6, :] = jnp.sum(hidden_three * grad_logits, axis=0, keepdims=True)
+
+    grad_before = grad_logits * head * gelu_slope(pre_three)
+    small_ref[4:5, :] = jnp.sum(grad_before, axis=0, keepdims=True)
+    grad_low = grad_before.astype(bf16)
+    emit(0, THREE_AT, 8, mul(hidden_two, grad_low, TN))
+    grad_hidden = mul(grad_low, matrix(THREE_AT, 8), NT)
+    parts = []
+    for p in range(2):
+        grad_before = grad_hidden[:, p * RANK : (p + 1) * RANK] * gelu_slope(pre_two[p])
+        small_ref[2 + p : 3 + p, :] = jnp.sum(grad_before, axis=0, keepdims=True)
+        parts.append(grad_before.astype(bf16))
+    grad_low = jnp.concatenate(parts, axis=0)
+    parts = []
+    for c in range(2):
+        if c == 1:
+            store(0, THREE_AT, 8).wait()
+        emit(1 - c, TWO_AT + c * 8, 8, mul(wide_two[c], grad_low, TN))
+        wide = mul(grad_low, matrix(TWO_AT + c * 8, 8), NT)
+        grad_hidden = jnp.concatenate(
+            [narrowed(wide[:, m * 2 * BR : (m + 1) * 2 * BR]) for m in range(4)], axis=1
+        )
+        grad_before = grad_hidden * gelu_slope(pre_one[c])
+        small_ref[c : c + 1, :] = jnp.sum(grad_before, axis=0, keepdims=True)
+        parts.append(grad_before.astype(bf16))
+    grad_one = jnp.concatenate(parts, axis=0)
+    store(1, TWO_AT, 8).wait()
+    store(0, TWO_AT + 8, 8).wait()
+
+    @pl.loop(0, FCH)
+    def first_back(c):
+        slot = c % 2
+        at = ONE_AT + c * FBLK
+
+        @pl.when(c >= 2)
+        def ready():
+            store(slot, at, FBLK).wait()
+
+        emit(slot, at, FBLK, mul(wide_one[c], grad_one, TN))
+        wide = mul(grad_one, matrix(at, FBLK), NT)
+        for m in range(3):
+            spot = pl.multiple_of((c % 3) * 3 * BR + m * BR, BR)
+            current[c // 3, :, pl.ds(spot, BR)] = narrowed(wide[:, m * 2 * BR : (m + 1) * 2 * BR])
+
+    for slot in range(2):
+        store(slot, ONE_AT, FBLK).wait()
+
+    sent = 0
+    for depth in reversed(range(LAYERS)):
+        down, up = depth * 27, (LAYERS + depth) * 27
+        base = sent
+
+        def up_back(c, acc):
+            slot = (base + c) % 2
+            before = current[c]
+            grad_mixing = anchor[c] * before
+            cross_grad_ref[pl.ds(depth * CHUNKS + c, 1), :] = jnp.sum(grad_mixing, axis=0, keepdims=True)
+            grad_low = grad_mixing.astype(bf16)
+
+            @pl.when(base + c >= 2)
+            def ready():
+                store(slot, up, CBLK).wait()
+
+            emit(slot, up + c * CBLK, CBLK, mul(grad_low, reduced[depth], TN))
+            part = before * mixing[depth * CHUNKS + c]
+            grad_anchor[c] = part if depth == LAYERS - 1 else grad_anchor[c] + part
+            return acc + mul(grad_low, matrix(up + c * CBLK, CBLK), NN)
+
+        total = lax.fori_loop(0, CHUNKS, up_back, jnp.zeros((samples, RANK), f32))
+        grad_reduced = total.astype(bf16)
+
+        @pl.loop(0, CHUNKS)
+        def down_back(c):
+            slot = (base + CHUNKS + c) % 2
+            store(slot, down, CBLK).wait()
+            emit(slot, down + c * CBLK, CBLK, mul(low[depth * CHUNKS + c], grad_reduced, TN))
+            after = current[c] + mul(grad_reduced, matrix(down + c * CBLK, CBLK), NT)
+            current[c] = after
+            if depth == 0:
+                grad_anchor[c] = grad_anchor[c] + after
+
+        sent += 2 * CHUNKS
+    grad_dense_ref[...] = grad_anchor[0, :, :EMB]
+    for i in range(1, F + 1):
+        c, at = i // CBLK, (i % CBLK) * BR
+        grad_pooled_ref[:, (i - 1) * EMB : i * EMB] = grad_anchor[c, :, at : at + BR].astype(bf16)
+    for slot in range(2):
+        store(slot, 0, CBLK).wait()
+
+
+def dense_step(tiles, pooled, dense_part, labels, head, bias_last, bias_cross, bias_one, bias_two, bias_three, batch):
+    samples = dense_part.shape[0]
+    f32, bf16 = jnp.float32, jnp.bfloat16
+    whole = pl.BlockSpec(memory_space=pltpu.VMEM)
+    away = pl.BlockSpec(memory_space=pl.ANY)
+    shape = jax.ShapeDtypeStruct
+    return pl.pallas_call(
+        functools.partial(dense_kernel, batch),
+        out_shape=[
+            shape(tiles.shape, bf16),
+            shape((samples, F * EMB), bf16),
+            shape((samples, EMB), f32),
+            shape((LAYERS * CHUNKS, CW), f32),
+            shape((8, RANK), f32),
+        ],
+        in_specs=[away] + [whole] * 9,
+        out_specs=[away] + [whole] * 4,
+        scratch_shapes=[
+            pltpu.VMEM(tiles.shape, bf16),
+            pltpu.VMEM((CHUNKS, samples, CW), f32),
+            pltpu.VMEM((CHUNKS, samples, CW), f32),
+            pltpu.VMEM((LAYERS * CHUNKS, samples, CW), f32),
+            pltpu.VMEM((LAYERS * CHUNKS, samples, CW), bf16),
+            pltpu.VMEM((CHUNKS, samples, CW), f32),
+            pltpu.VMEM((FCH, 2 * samples, FBLK * BR), bf16),
+            pltpu.VMEM((2, 2 * samples, 8 * BR), bf16),
+            pltpu.VMEM((2, 32, CBLK, 16, 128), bf16),
+            pltpu.SemaphoreType.DMA((len(GROUPS),)),
+            pltpu.SemaphoreType.DMA((2,)),
+        ],
+        compiler_params=pltpu.CompilerParams(vmem_limit_bytes=61 << 20),
+        name="dense_step",
+    )(tiles, pooled, dense_part, labels, head, bias_last, bias_cross, bias_one, bias_two, bias_three)
 
 
 def body(
@@ -833,12 +1091,14 @@
     block_count = block_owners.shape[0]
     capacity = samples * TOTAL // devices
     live_total = samples * TOTAL
-    everything = lax.all_gather(dense_slots.astype(jnp.bfloat16), "row", axis=0, tiled=True)
-    fetched = jnp.take(everything, block_owners, axis=0, mode="clip")
-    cross_down, cross_up, first_matrix, middle, third_matrix = split_dense(
-        fetched.reshape(block_count * BR, RANK)
-    )
-    bias_dense, bias_cross, bias_one, bias_two, bias_three, bias_last = split_bias(biases)
+    bf16 = jnp.bfloat16
+    slot_tiles = (
+        dense_slots.astype(bf16)
+        .reshape(slot_count, 8, 16, 4, 128)
+        .transpose(1, 3, 0, 2, 4)
+        .reshape(devices, slot_count * 16, 128)
+    )
+    slot_tiles = lax.all_to_all(slot_tiles, "row", split_axis=0, concat_axis=0, tiled=True)
     lanes = lax.broadcasted_iota(jnp.int32, row_ids.shape, 2)
     features = lax.broadcasted_iota(jnp.int32, row_ids.shape, 1)
     sample_of = lax.broadcasted_iota(jnp.int32, row_ids.shape, 0)
@@ -850,108 +1110,99 @@
     )
     key = jnp.where(lanes < hot_counts[:, :, None], key, devices << 21)
     ordered = lax.sort(key.reshape(-1), is_stable=False)[:live_total]
+    block_tiles = jnp.take(
+        slot_tiles.reshape(devices * slot_count, 16, 128),
+        block_owners + jnp.minimum(ordered[0], 0),
+        axis=0,
+        mode="clip",
+    )
+    tiles = lax.all_gather(block_tiles.reshape(block_count * 16, 128), "row", axis=0, tiled=True)
+    tiles = tiles.reshape(devices, block_count, 16, 128)
+    bias_dense, bias_cross, bias_one, bias_two, bias_three, bias_last = split_bias(biases)
     requests = (ordered & ((1 << 21) - 1)).reshape(devices, capacity)
     received = lax.all_to_all(requests, "row", split_axis=0, concat_axis=0, tiled=True)
     edges = jnp.arange(F + 1, dtype=jnp.int32) << 16
     offsets = jnp.sum((received[:, None, :] < edges[None, :, None]).astype(jnp.int32), axis=2)
     room = (capacity + samples - 1) // samples * samples + samples
     keys = jnp.pad(received, ((0, 0), (0, room - capacity)), constant_values=-1)
-    counts, partial = count_tables(offsets.reshape(-1), keys, embed_table, devices, samples)
-    summed = scatter_sum(
-        partial, 0, F * EMB, jnp.bfloat16, 16, (2, 4, 6, 7, 8), 0, "scatter_pooled"
-    )
-    pooled_low = summed.T
+    counts, partial = count_tables(offsets, keys, embed_table, devices, samples)
+    pooled = scatter_sum(partial, 0, F * EMB, bf16, 16, (2, 4, 6, 7, 8), 0, "scatter_pooled")
     dense_part = (
         jnp.dot(dense_feats, dense_proj, precision=highest, preferred_element_type=jnp.float32)
         + bias_dense
     )
-    anchor = jnp.concatenate([dense_part, pooled_low.astype(jnp.float32)], axis=1)
-    current = anchor
-    stored = []
-    for depth in range(LAYERS):
-        saved, current = cross_forward(
-            anchor, current, cross_down[depth], cross_up[depth], bias_cross[depth]
-        )
-        stored.append(saved)
-    first_saved, hidden = dense_forward(current, first_matrix, bias_one)
-    second_saved, hidden = dense_forward(hidden, middle, bias_two)
-    third_saved, hidden = dense_forward(hidden, third_matrix, bias_three)
-    logits = (
-        jnp.dot(hidden, head_weight, precision=highest, preferred_element_type=jnp.float32)
-        + bias_last
-    )
-    labels = click_labels.astype(jnp.float32)
-    loss_local = jnp.sum(jax.nn.softplus(logits) - labels * logits)
-    grad_logits = (jax.nn.sigmoid(logits) - labels) / (samples * devices)
-    grad_head_local = jnp.dot(
-        grad_logits, hidden, precision=highest, preferred_element_type=jnp.float32
-    )
-    grad_hidden = grad_logits[:, None] * head_weight[None, :]
-    grad_hidden, grad_third, grad_bias_three = dense_backward(
-        third_saved, third_matrix, grad_hidden
-    )
-    grad_hidden, grad_middle, grad_bias_two = dense_backward(second_saved, middle, grad_hidden)
-    grad_current, grad_first, grad_bias_one = dense_backward(first_saved, first_matrix, grad_hidden)
-    grad_anchor = jnp.zeros_like(anchor)
-    grads_down = [None] * LAYERS
-    grads_up = [None] * LAYERS
-    grads_cross = [None] * LAYERS
-    for depth in reversed(range(LAYERS)):
-        grad_current, grad_part, grads_down[depth], grads_up[depth], grads_cross[depth] = (
-            cross_backward(anchor, stored[depth], cross_down[depth], cross_up[depth], grad_current)
-        )
-        grad_anchor = grad_anchor + grad_part
-    grad_anchor = grad_anchor + grad_current
-    grad_pooled = grad_anchor[:, EMB:].astype(jnp.bfloat16)
+    grad_tiles, grad_pooled, grad_dense, grad_cross, grad_small = dense_step(
+        tiles,
+        pooled,
+        dense_part,
+        click_labels.astype(jnp.float32)[:, None],
+        head_weight[None, :],
+        jnp.broadcast_to(bias_last, (samples, 1)),
+        bias_cross.reshape(LAYERS * CHUNKS, CW),
+        bias_one.reshape(2, RANK),
+        bias_two.reshape(2, RANK),
+        bias_three[None, :],
+        samples * devices,
+    )
     gathered_grads = lax.all_gather(grad_pooled, "row", axis=0, tiled=True)
+    grad_mine = scatter_sum(
+        grad_tiles.reshape(devices, block_count * 16, 128),
+        0,
+        block_count * 16,
+        jnp.float32,
+        16,
+        (2, 4, 6, 7, 8),
+        1,
+        "scatter_dense",
+    )
     grad_table, table_squares = row_grads(counts, gathered_grads)
+    matches = block_owners[None, :] == jnp.arange(devices * slot_count, dtype=jnp.int32)[:, None]
+    inverse = jnp.sum(
+        jnp.where(matches, jnp.arange(block_count, dtype=jnp.int32)[None, :], 0), axis=1
+    )
+    named = jnp.any(matches, axis=1)
+    returned = jnp.take(
+        grad_mine.astype(bf16).reshape(block_count, 16, 128), inverse, axis=0, mode="clip"
+    )
+    returned = jnp.where(named[:, None, None], returned, 0)
+    returned = lax.all_to_all(
+        returned.reshape(devices, slot_count * 16, 128), "row", split_axis=0, concat_axis=0, tiled=True
+    )
     grad_proj_local = jnp.einsum(
         "sa,sb->ab",
         dense_feats,
-        grad_anchor[:, :EMB],
+        grad_dense,
         precision=highest,
         preferred_element_type=jnp.float32,
     )
-    stacked = jnp.concatenate(
-        [
-            jnp.stack(grads_down).reshape(-1, RANK),
-            jnp.stack(grads_up).reshape(-1, RANK),
-            grad_first.reshape(-1, RANK),
-            grad_middle.reshape(-1, RANK),
-            grad_third,
-            jnp.zeros((BR, RANK), jnp.float32),
-        ],
-        axis=0,
-    ).astype(jnp.bfloat16).reshape(block_count + 1, BR, RANK)
-    matches = block_owners[None, :] == jnp.arange(devices * slot_count, dtype=jnp.int32)[:, None]
-    inverse = jnp.sum(
-        jnp.where(matches, jnp.arange(block_count, dtype=jnp.int32)[None, :], 0), axis=1
-    )
-    inverse = inverse + jnp.where(jnp.any(matches, axis=1), 0, block_count)
-    placed = jnp.take(stacked, inverse, axis=0, mode="clip")
-    half = slot_count * BR // 2
-    grad_slots = jnp.concatenate(
-        [
-            scatter_sum(placed, part * half, half, jnp.float32, 16, (2, 4, 6, 7, 8), part + 1, "scatter_dense")
-            for part in (0, 1)
-        ],
-        axis=0,
-    ).reshape(slot_count, BR, RANK)
     bias_local = jnp.concatenate(
         [
-            jnp.sum(grad_anchor[:, :EMB], axis=0),
-            jnp.stack(grads_cross).reshape(-1),
-            grad_bias_one,
-            grad_bias_two,
-            grad_bias_three,
-            jnp.sum(grad_logits)[None],
+            jnp.sum(grad_dense, axis=0),
+            grad_cross.reshape(-1),
+            grad_small[0:5].reshape(-1),
+            grad_small[7, :1],
         ]
     )
-    loss_total, grad_proj, grad_head, grad_bias = lax.psum(
-        (loss_local, grad_proj_local, grad_head_local, bias_local), "row"
-    )
-    local_squares = jnp.sum(table_squares) + jnp.sum(grad_slots * grad_slots)
-    squares = lax.psum(local_squares, "row")
+    squares_local = jnp.sum(table_squares) + jnp.sum(grad_mine * grad_mine)
+    packed = jnp.concatenate(
+        [
+            grad_small[6, :1],
+            squares_local[None],
+            grad_proj_local.reshape(-1),
+            grad_small[5],
+            bias_local,
+        ]
+    )
+    room = -packed.shape[0] % 1024
+    packed = total_of(jnp.pad(packed, (0, room)).reshape(-1, 128), 2).reshape(-1)
+    cuts = [0, 1, 2]
+    for size in (dense_proj.size, head_weight.size, biases.size):
+        cuts.append(cuts[-1] + size)
+    loss_total, squares, grad_proj, grad_head, grad_bias = [
+        packed[first:last] for first, last in zip(cuts[:-1], cuts[1:])
+    ]
+    loss_total, squares = loss_total[0], squares[0]
+    grad_proj = grad_proj.reshape(dense_proj.shape)
     squares = (
         squares
         + jnp.sum(grad_proj * grad_proj)
@@ -961,28 +1212,18 @@
     grad_norm = jnp.sqrt(squares)
     clip_scale = clip_norm / jnp.maximum(grad_norm, clip_norm)
     table_new = adamw(embed_table, table_moment, table_square, clip_scale * grad_table, rate_table)
-    dense_new = adamw(dense_slots, dense_moment, dense_square, clip_scale * grad_slots, rate_dense)
+    dense_new = slot_update(
+        clip_scale,
+        returned.reshape(devices, slot_count, 16, 128),
+        dense_slots,
+        dense_moment,
+        dense_square,
+    )
     proj_new = adamw(dense_proj, proj_moment, proj_square, clip_scale * grad_proj, rate_small)
     head_new = adamw(head_weight, head_moment, head_square, clip_scale * grad_head, rate_small)
     bias_new = adamw(biases, bias_moment, bias_square, clip_scale * grad_bias, rate_small)
     return (
-        loss_total,
-        grad_norm,
-        table_new[0],
-        table_new[1],
-        table_new[2],
-        dense_new[0],
-        dense_new[1],
-        dense_new[2],
-        proj_new[0],
-        proj_new[1],
-        proj_new[2],
-        head_new[0],
-        head_new[1],
-        head_new[2],
-        bias_new[0],
-        bias_new[1],
-        bias_new[2],
+        (loss_total, grad_norm) + table_new + dense_new + proj_new + head_new + bias_new
     )
 
 
@@ -1028,6 +1269,6 @@
         P(),
         P(),
     )
-    fits = mesh.shape["row"] <= 32
+    fits = mesh.shape["row"] == 32
     chosen = body_counted if fits else body
     return jax.shard_map(chosen, mesh=mesh, in_specs=in_specs, out_specs=out_specs, check_vma=False)

time: 1070 us -> 776 us (0.73)
  local copies, waits for them, and re-layouts: 140 us -> 22.1 us
  Pallas kernels: 719 us -> 629 us
  matrix products: 45.9 us -> 1.08 us
  blocking collectives: 38.9 us -> 0 us
  starting transfers between devices: 7.38 us -> 18.1 us
    pallas_call x1, Pallas kernels: 232 us -> 60.7 us  [count_tables(): pl.pallas_call(functools.partial(count_kernel, devices, samples, table_ro...]
    pallas_call x0 -> x3, Pallas kernels: none -> 78.8 us  [the longest x1 47 us: dense_step(): pl.pallas_call(functools.partial(dense_kernel, batch), out_shape=[shape(t...]
    gather x2, local copies, waits for them, and re-layouts: 51.8 us -> 5.05 us  [the longest x1 3.13 us: body_counted(): jnp.take(slot_tiles.reshape(devices * slot_count, 16, 128), block_owners...]
    dot_general x30 -> x1, matrix products: 45.6 us -> 0.16 us  [body_counted(): jnp.einsum('sa,sb->ab', dense_feats, grad_dense, precision=highest, prefe...]
    psum x1 -> x0, blocking collectives: 38.9 us -> none  [body_counted(): lax.psum((loss_local, grad_proj_local, grad_head_local, bias_local), 'row')]
    reshape x6 -> x7, local copies, waits for them, and re-layouts: 31 us -> 2.36 us  [the longest x1 0.63 us: body_counted(): jnp.pad(packed, (0, room)).reshape(-1, 128)]
    slice x7 -> x6, local copies, waits for them, and re-layouts: 25.7 us -> 2.38 us  [the longest x1 1.33 us: body_counted(): packed[first:last]]
    unnamed x158 -> x37, local copies, waits for them, and re-layouts: 23.7 us -> 1.27 us
  transfers between devices with their start and end apart: 3 -> 5, of which waited for: 1 -> 1; matrix products, arithmetic and copies ran while one was open for 12% -> 12% of each run, Pallas kernels for 63% -> 74%
where the time goes in v2:
time: 776 us; the launch traced here: 771 us
  Pallas kernels  629 us (81%)
  other arithmetic  75.7 us (10%)
  local copies, waits for them, and re-layouts  22.1 us (3%)
  between operations  20.5 us (3%)
  starting transfers between devices  18.1 us (2%)
    pallas_call x2, Pallas kernels, scatter_sum(): pl.pallas_call(functools.partial(scatter_kernel, base, slices, lags), out...  436 us
    pallas_call x1, Pallas kernels, count_tables(): pl.pallas_call(functools.partial(count_kernel, devices, samples, table_ro...  60.7 us
    pallas_call x1, Pallas kernels, row_grads(): pl.pallas_call(row_grad_kernel, grid=(F,), in_specs=[pl.BlockSpec((1, tab...  53.9 us
    pallas_call x1, Pallas kernels, dense_step(): pl.pallas_call(functools.partial(dense_kernel, batch), out_shape=[shape(t...  47 us
    sort x1, other arithmetic, body_counted(): ordered = lax.sort(key.reshape(-1), is_stable=False)[:live_total]  37.7 us
    sub x4, other arithmetic, adamw(): weight - step_rate * (corrected / (jnp.sqrt(scaled) + adam_eps) + decay_r...  22.7 us
    pallas_call x1, Pallas kernels, total_of(): pl.pallas_call(total_kernel, out_shape=jax.ShapeDtypeStruct(array.shape,...  19.3 us
  transfers between devices with their start and end apart: 5, of which 1 were waited for; matrix products, arithmetic and copies ran while one was open for 12% of the time, Pallas kernels for 74%

profile of v2, /device:TPU:0, one launch (start us, length us, event | category | flops | bytes accessed | tf_op | source)
XLA Modules:
  0.0 771.5 jit_solution(415687041237389792)
XLA Ops:
  7.2 0.0 copy-start
  7.2 2.1 convert_element_type.16
  9.3 0.4 reshape.122
  9.8 0.0 copy-start.14
  9.8 1.5 copy.58
  11.3 7.4 all-to-all-start
  18.7 0.0 all-gather.3.cloned.1.call-start
  18.8 1.5 fusion.5
  20.3 1.9 copy.59
  22.2 1.0 reshape.125
  23.2 37.7 %sort.7 = s32[99840]{0:T(1024)S(1)} sort(s32[99840]{0:T(1024)S(1)} %reshape.125), dimensions={0}, to_apply=%region_0.1 | sort | flops 1697280 | bytes 798720 | tf_op jit(solution)/shard_map/sort | solution.py:1112
  61.0 0.5 slice.81
  62.2 3.1 gather_fusion
  65.3 0.0 all-gather.3.cloned.1.call-update
  65.4 1.0 and.31
  66.4 5.8 all-to-all-start.1
  72.1 0.0 all-gather.5.cloned.1.call-start
  72.2 0.5 slice.63
  72.8 0.6 slice.67
  73.3 0.6 reshape.131.two_bias_ref
  73.9 0.6 reshape.130.one_bias_ref
  74.5 0.6 reshape_reshape.6.cross_bias_ref
  75.2 0.7 copy.62.label_ref
  75.9 0.9 convolution_add_fusion.dense_ref
  76.9 5.0 all-to-all-done.1
  81.9 0.8 convert_reduce_fusion
  82.7 0.1 copy.60
  82.8 0.1 reshape.128.off_ref
  82.9 0.1 fusion.13.most_ref
  83.0 60.7 %count_tables.1 = (bf16[26,512,4096]{2,1,0:T(8,128)(2,1)}, bf16[32,26,128,128]{3,2,1,0:T(8,128)(2,1)}) custom-call(s32[864]{0:T(1024)S(1)} %reshape.128.off_ref, s32[26]{0:T(128)S(1)} %fusion.13.most_ref, s32[32,1792]{1,0:T(8,128)S(1)} %pad.8.keys_ref, f32[26,512,128]{2,1,0:T(8,128)} %table_ref.1), custom_call_target="tpu_custom_call" | custom-call | tf_op jit(solution)/shard_map/count_tables/pallas_call | solution.py:242
  143.8 199.3 %scatter_pooled.1.pooled_ref = bf16[3328,128]{1,0:T(8,128)(2,1)} custom-call(bf16[4,2,2,2,3328,128]{5,4,3,2,1,0:T(8,128)(2,1)} %bitcast.50), custom_call_target="tpu_custom_call" | custom-call | tf_op jit(solution)/shard_map/scatter_pooled/pallas_call | solution.py:513
  343.0 0.0 all-gather.3.cloned.1.call-done
  343.1 1.3 broadcast_in_dim.72.last_ref
  344.4 47.0 %dense_step.1 = (bf16[32,240,16,128]{3,2,1,0:T(8,128)(2,1)}, bf16[128,3328]{1,0:T(8,128)(2,1)}, f32[128,128]{1,0:T(8,128)}, f32[9,1152]{1,0:T(8,128)}, f32[8,512]{1,0:T(8,128)}) custom-call(bf16[32,240,16,128]{3,2,1,0:T(8,128)(2,1)} %bitcast.48, bf16[3328,128]{1,0:T(8,128)(2,1)} %scatter_pooled.1.pooled_ref, f32[128,128]{1,0:T(8,128)} %convolution_add_fusion.dense_ref, ...), custom_call_target="tpu_custom_call" | custom-call | tf_op jit(solution)/shard_map/dense_step/pallas_call | solution.py:858
  391.4 0.0 all-gather.5.cloned.1.call-update
  391.4 0.1 fusion.11
  391.5 0.1 broadcast_in_dim.76
  391.7 0.1 copy.63
  391.8 0.1 copy.64
  391.9 0.1 select_reduce_fusion
  392.0 0.0 copy-start.5
  392.0 236.3 %scatter_dense.1 = f32[3840,128]{1,0:T(8,128)} custom-call(bf16[4,2,2,2,3840,128]{5,4,3,2,1,0:T(8,128)(2,1)} %bitcast.49), custom_call_target="tpu_custom_call" | custom-call | tf_op jit(solution)/shard_map/scatter_dense/pallas_call | solution.py:513
  628.4 3.2 fusion.22
  631.6 1.9 gather_fusion.1
  633.5 2.3 bitcast_select_fusion
  635.9 4.8 all-to-all-start.2
  640.7 0.5 fusion.25
  641.2 0.2 convolution_bitcast_fusion
  641.4 0.0 copy-start.11
  641.5 53.9 %row_grads.1 = (f32[26,512,128]{2,1,0:T(8,128)}, f32[8,128]{1,0:T(8,128)S(1)}) custom-call(bf16[26,512,4096]{2,1,0:T(8,128)(2,1)} %get-tuple-element.31.counts_ref, bf16[4096,3328]{1,0:T(8,128)(2,1)} %all-gather.5.cloned.1.call-done.grads_ref), custom_call_target="tpu_custom_call" | custom-call | tf_op jit(solution)/shard_map/row_grads/pallas_call | solution.py:282
  695.4 0.6 reduce_sum.73
  697.3 1.4 concatenate.3
  698.7 0.6 pad_bitcast_fusion.x_ref
  699.3 19.3 %total_small.1 = f32[120,128]{1,0:T(8,128)} custom-call(f32[120,128]{1,0:T(8,128)} %pad_bitcast_fusion.x_ref), custom_call_target="tpu_custom_call" | custom-call | tf_op jit(solution)/shard_map/total_small/pallas_call | solution.py:569
  718.6 1.4 multiply_reduce_fusion.3
  720.0 1.4 multiply_reduce_fusion.2
  721.4 1.3 fusion.23
  724.6 1.5 multiply_reduce_fusion.1
  726.9 1.4 multiply_subtract_fusion.3
  728.3 1.4 multiply_subtract_fusion.2
  729.7 1.6 multiply_subtract_fusion.1
  731.3 18.4 %multiply_subtract_fusion = (f32[26,512,128]{2,1,0:T(8,128)}, f32[26,512,128]{2,1,0:T(8,128)}, f32[26,512,128]{2,1,0:T(8,128)}) fusion(f32[26,512,128]{2,1,0:T(8,128)} %table_ref.1, f32[26,512,128]{2,1,0:T(8,128)} %get-tuple-element.37, f32[]{:T(128)} %div.79, f32[26,512,128]{2,1,0:T(8,128)} %param.26, f32[26,512,128]{2,1,0:T(8,128)} %param.27), kind=kLoop, calls=%fused_computation.4 | loop fusion | flops 27262976 | bytes 47710212 | tf_op jit(solution)/shard_map/sub | solution.py:153
  749.6 1.1 copy-done.2
  750.8 12.5 %slot_update.1 = (f32[12,128,512]{2,1,0:T(8,128)}, f32[12,128,512]{2,1,0:T(8,128)}, f32[12,128,512]{2,1,0:T(8,128)}) custom-call(f32[1]{0:T(128)} %bitcast.22.scale_ref, bf16[32,12,16,128]{3,2,1,0:T(8,128)(2,1)} %bitcast.54, f32[12,128,512]{2,1,0:T(8,128)} %weight_ref.1, f32[12,128,512]{2,1,0:T(8,128)} %moment_ref.1, f32[12,128,512]{2,1,0:T(8,128)} %square_ref.1), custom_call_target="tpu_custom_call" | custom-call | tf_op jit(solution)/shard_map/slot_update/pallas_call | solution.py:601
  (52 shorter events, 0.2 us)
Async XLA Ops:
  7.2 68.7 %copy-start = (f32[128,13]{0,1:T(8,128)S(1)}, f32[128,13]{0,1:T(8,128)}, u32[]{:S(2)}) copy-start(f32[128,13]{0,1:T(8,128)} %param.22) | copy-start | bytes 19972
  7.2 11.6 %copy-start.10 = (s32[128,26]{0,1:T(8,128)S(1)}, s32[128,26]{0,1:T(8,128)}, u32[]{:S(2)}) copy-start(s32[128,26]{0,1:T(8,128)} %param.21) | copy-start | bytes 39940
  9.8 52.4 %copy-start.14 = (s32[240]{0:T(256)S(1)}, s32[240]{0:T(256)}, u32[]{:S(2)}) copy-start(s32[240]{0:T(256)} %param.24) | copy-start | bytes 2884
  11.3 60.9 %copy-start.4 = (f32[13057]{0:T(1024)S(1)}, f32[13057]{0:T(1024)}, u32[]{:S(2)}) copy-start(f32[13057]{0:T(1024)} %param.37) | copy-start | bytes 156688
  11.3 60.9 %copy-start.17 = (s32[128]{0:T(128)S(1)}, s32[128]{0:T(128)}, u32[]{:S(2)}) copy-start(s32[128]{0:T(128)} %param.23) | copy-start | bytes 1540
  11.3 64.6 %slice-start = ((f32[13057]{0:T(1024)}), f32[128]{0:T(128)S(1)}, s32[]{:S(2)}) async-start(f32[13057]{0:T(1024)} %param.37), calls=%async_computation.5 | async-start | bytes 1024 | tf_op jit(solution)/shard_map/slice | solution.py:52
  11.3 64.6 %copy-start.8 = (f32[13,128]{1,0:T(8,128)S(1)}, f32[13,128]{1,0:T(8,128)}, u32[]{:S(2)}) copy-start(f32[13,128]{1,0:T(8,128)} %param.31) | copy-start | bytes 19972
  11.3 50.8 %all-to-all-start = ((bf16[32,192,128]{2,1,0:T(8,128)(2,1)}), bf16[32,192,128]{2,1,0:T(8,128)(2,1)}, u32[]{:S(2)}, u32[]{:S(2)}) async-start(bf16[32,192,128]{2,1,0:T(8,128)(2,1)} %bitcast.1), calls=%async_computation | async-start | bytes 3145728 | tf_op jit(solution)/shard_map/all_to_all | solution.py:1101
  18.7 324.3 %all-gather.3.cloned.1.call-start = ((), (), s32[]{:S(2)}) async-start(), calls=%async_computation.3 | async-start | bytes 32440320 | tf_op jit(solution)/shard_map/all_gather | solution.py:1119
  66.4 15.5 %all-to-all-start.1 = ((s32[32,1,1612]{2,1,0:T(1,128)}), s32[32,1,1612]{2,1,0:T(1,128)S(1)}, u32[]{:S(2)}, u32[]{:S(2)}) async-start(s32[32,1,1612]{2,1,0:T(1,128)} %and.31), calls=%async_computation.1 | async-start | bytes 425984 | tf_op jit(solution)/shard_map/all_to_all | solution.py:1123
  72.1 569.3 %all-gather.5.cloned.1.call-start = ((), (), s32[]{:S(2)}) async-start(), calls=%async_computation.4 | async-start | bytes 28114944 | tf_op jit(solution)/shard_map/all_gather | solution.py:1147
  392.0 236.3 %copy-start.9 = (f32[8,512]{1,0:T(8,128)S(1)}, f32[8,512]{1,0:T(8,128)}, u32[]{:S(2)}) copy-start(f32[8,512]{1,0:T(8,128)} %get-tuple-element.30) | copy-start | bytes 49156
  392.0 236.3 %copy-start.5 = (f32[9,1152]{1,0:T(8,128)S(1)}, f32[9,1152]{1,0:T(8,128)}, u32[]{:S(2)}) copy-start(f32[9,1152]{1,0:T(8,128)} %get-tuple-element.36) | copy-start | bytes 124420
  628.3 12.4 %copy-start.3 = (f32[128,128]{1,0:T(8,128)S(1)}, f32[128,128]{1,0:T(8,128)}, u32[]{:S(2)}) copy-start(f32[128,128]{1,0:T(8,128)} %get-tuple-element.35) | copy-start | bytes 196612
  635.9 113.8 %all-to-all-start.2 = ((bf16[32,192,128]{2,1,0:T(8,128)(2,1)}), bf16[32,192,128]{2,1,0:T(8,128)(2,1)S(1)}, u32[]{:S(2)}, u32[]{:S(2)}) async-start(bf16[32,192,128]{2,1,0:T(8,128)(2,1)} %bitcast_select_fusion), calls=%async_computation.2 | async-start | bytes 3145728 | tf_op jit(solution)/shard_map/all_to_all | solution.py:1168
  641.4 85.5 %copy-start.11 = (f32[512]{0:T(512)S(1)}, f32[512]{0:T(512)}, u32[]{:S(2)}) copy-start(f32[512]{0:T(512)} %param.34) | copy-start | bytes 6148
  641.4 85.5 %copy-start.15 = (f32[512]{0:T(512)S(1)}, f32[512]{0:T(512)}, u32[]{:S(2)}) copy-start(f32[512]{0:T(512)} %param.35) | copy-start | bytes 6148
  641.4 85.5 %copy-start.16 = (f32[512]{0:T(512)S(1)}, f32[512]{0:T(512)}, u32[]{:S(2)}) copy-start(f32[512]{0:T(512)} %param.36) | copy-start | bytes 6148
  641.4 86.8 %copy-start.12 = (f32[13,128]{1,0:T(8,128)S(1)}, f32[13,128]{1,0:T(8,128)}, u32[]{:S(2)}) copy-start(f32[13,128]{1,0:T(8,128)} %param.32) | copy-start | bytes 19972
  641.5 86.8 %copy-start.13 = (f32[13,128]{1,0:T(8,128)S(1)}, f32[13,128]{1,0:T(8,128)}, u32[]{:S(2)}) copy-start(f32[13,128]{1,0:T(8,128)} %param.33) | copy-start | bytes 19972
  641.5 88.2 %copy-start.6 = (f32[13057]{0:T(1024)S(1)}, f32[13057]{0:T(1024)}, u32[]{:S(2)}) copy-start(f32[13057]{0:T(1024)} %param.38) | copy-start | bytes 156688
  641.5 88.2 %copy-start.7 = (f32[13057]{0:T(1024)S(1)}, f32[13057]{0:T(1024)}, u32[]{:S(2)}) copy-start(f32[13057]{0:T(1024)} %param.39) | copy-start | bytes 156688
  731.3 32.0 %copy-start.1 = (f32[128,13]{0,1:T(8,128)S(1)}, f32[128,13]{0,1:T(8,128)}, u32[]{:S(2)}) copy-start(f32[128,13]{0,1:T(8,128)} %param.22) | copy-start | bytes 19972
  749.6 1.2 copy-start.2
Sparse Core Ops, SparseCore 0:
  65.4 259.8 all-gather.2
  391.5 244.1 all-gather.4

commit v3 on v2

--- a/solution.py
+++ b/solution.py
@@ -267,38 +267,6 @@
     )(offsets.reshape(-1), jnp.max(offsets[:, 1:] - offsets[:, :-1], axis=0), keys, embed_table)
 
 
-def row_grad_kernel(counts_ref, grads_ref, out_ref, square_ref):
-    @pl.when(pl.program_id(0) == 0)
-    def start():
-        square_ref[...] = jnp.zeros_like(square_ref)
-
-    total = jnp.dot(counts_ref[0], grads_ref[...], preferred_element_type=jnp.float32)
-    out_ref[0] = total
-    square_ref[...] += jnp.sum((total * total).reshape(-1, 8, EMB), axis=0)
-
-
-def row_grads(counts, grads):
-    table_rows, batch = counts.shape[1:]
-    return pl.pallas_call(
-        row_grad_kernel,
-        grid=(F,),
-        in_specs=[
-            pl.BlockSpec((1, table_rows, batch), lambda f: (f, 0, 0)),
-            pl.BlockSpec((batch, EMB), lambda f: (0, f)),
-        ],
-        out_specs=[
-            pl.BlockSpec((1, table_rows, EMB), lambda f: (f, 0, 0)),
-            pl.BlockSpec((8, EMB), lambda f: (0, 0)),
-        ],
-        out_shape=[
-            jax.ShapeDtypeStruct((F, table_rows, EMB), jnp.float32),
-            jax.ShapeDtypeStruct((8, EMB), jnp.float32),
-        ],
-        compiler_params=pltpu.CompilerParams(vmem_limit_bytes=48 << 20),
-        name="row_grads",
-    )(counts, grads)
-
-
 MESH = pl.DeviceIdType.MESH
 
 
@@ -311,7 +279,7 @@
     return (((z * 2 + y) * 2 + x) * 2 + core,)
 
 
-def greet(z, y, x, core):
+def greet(z, y, x, core, far=0):
     barrier = pltpu.get_barrier_semaphore()
 
     def hail(*where):
@@ -320,6 +288,8 @@
     hail(z, y, x, 1 - core)
     hail(z, y, 1 - x, core)
     hail(z, 1 - y, x, core)
+    if far:
+        hail((z + 2) % 4, y, x, core)
 
     @pl.when(z > 0)
     def below():
@@ -331,11 +301,11 @@
 
     @pl.when(jnp.logical_and(z > 0, z < 3))
     def inside():
-        pl.semaphore_wait(barrier, 5)
+        pl.semaphore_wait(barrier, 5 + far)
 
     @pl.when(jnp.logical_or(z == 0, z == 3))
     def edge():
-        pl.semaphore_wait(barrier, 4)
+        pl.semaphore_wait(barrier, 4 + far)
 
 
 def remote(source, target, send_sem, recv_sem, where):
@@ -349,18 +319,12 @@
     )
 
 
-def add_into(target, source, count):
-    @pl.loop(0, count)
-    def step(i):
-        target[i] = target[i] + source[i]
-
-
-def scatter_kernel(
-    base, slices, lags, x_ref, out_ref, own, got_core, got_one, got_two, got_up, got_down,
-    local_sem, send_core, recv_core, send_one, recv_one, send_two, recv_two,
-    send_up, recv_up, send_down, recv_down,
+def scatter_parts(
+    base, kinds, x_ref, out_ref, own, got_core, got_one, tail, local_sem, send_core, recv_core,
+    send_one, recv_one, send_two, recv_two, send_up, recv_up, send_down, recv_down, squares=None,
 ):
     z, y, x, core = place()
+    slices = len(kinds)
     rows = own.shape[4]
 
     def span(q):
@@ -369,35 +333,99 @@
     def kept(q):
         return pl.ds(q * rows, rows)
 
+    def along_x(q):
+        return kinds[q] % 2 == 0
+
+    def chain_last(q):
+        return kinds[q] < 2
+
+    def got_two(q):
+        return tail.at[q, 0:4] if chain_last(q) else tail.at[q, 12]
+
+    def rising(q, first, count):
+        if chain_last(q):
+            return tail.at[q, 4 + first : 4 + first + count]
+        return tail.at[q, 2 * first : 2 * first + 2 * count]
+
+    def falling(q, count):
+        if chain_last(q):
+            return tail.at[q, 7 : 7 + count]
+        return tail.at[q, 6 : 6 + 2 * count]
+
+    def close(q, total):
+        out_ref[kept(q)] = total.astype(out_ref.dtype)
+        if squares is not None:
+            squares[...] += jnp.sum((total * total).reshape(-1, 8, total.shape[1]), axis=0)
+
     def to_core(q):
         return remote(x_ref.at[:, :, :, 1 - core, span(q)], got_core.at[q], send_core.at[q], recv_core.at[q], (z, y, x, 1 - core))
 
     def to_one(q):
-        if q % 2 == 0:
+        if along_x(q):
             source, where = own.at[q, :, :, 1 - x], (z, y, 1 - x, core)
         else:
             source, where = own.at[q, :, 1 - y], (z, 1 - y, x, core)
         return remote(source, got_one.at[q], send_one.at[q], recv_one.at[q], where)
 
     def to_two(q):
-        if q % 2 == 0:
-            source, where = own.at[q, :, 1 - y, x], (z, 1 - y, x, core)
+        there = (z, 1 - y, x, core) if along_x(q) else (z, y, 1 - x, core)
+        if chain_last(q):
+            source = own.at[q, :, 1 - y, x] if along_x(q) else own.at[q, :, y, 1 - x]
         else:
-            source, where = own.at[q, :, y, 1 - x], (z, y, 1 - x, core)
-        return remote(source, got_two.at[q], send_two.at[q], recv_two.at[q], where)
+            source = own.at[q, z, 1 - y, x] if along_x(q) else own.at[q, z, y, 1 - x]
+        return remote(source, got_two(q), send_two.at[q], recv_two.at[q], there)
+
+    def chained(q, first, count):
+        part = pl.ds(first, count)
+        if chain_last(q):
+            return own.at[q, part, y, x]
+        return own.at[q, part, :, x] if along_x(q) else own.at[q, part, y]
 
     def to_up(q, level):
         count = 3 - level
-        source = own.at[q, 1:4, y, x] if level == 0 else got_up.at[q, 1 : count + 1]
-        return remote(source, got_up.at[q, 0:count], send_up.at[q], recv_up.at[q], (z + 1, y, x, core))
+        target = rising(q, 0, count)
+        if level == 0:
+            source = chained(q, 1, 3)
+            target = target if chain_last(q) else tail.at[q, 0:6].reshape(3, 2, rows, own.shape[5])
+        else:
+            source = rising(q, 1, count)
+        return remote(source, target, send_up.at[q], recv_up.at[q], (z + 1, y, x, core))
 
     def to_down(q, level):
         count = level
-        source = own.at[q, 0:3, y, x] if level == 3 else got_down.at[q, 0:count]
-        return remote(source, got_down.at[q, 0:count], send_down.at[q], recv_down.at[q], (z - 1, y, x, core))
+        target = falling(q, count)
+        if level == 3:
+            source = chained(q, 0, 3)
+            target = target if chain_last(q) else tail.at[q, 6:12].reshape(3, 2, rows, own.shape[5])
+        else:
+            source = target
+        return remote(source, target, send_down.at[q], recv_down.at[q], (z - 1, y, x, core))
 
     def local(q):
         return pltpu.make_async_copy(x_ref.at[:, :, :, core, span(q)], own.at[q], local_sem.at[q])
+
+    def width(q):
+        return 1 if chain_last(q) else 2
+
+    def own_at(q, t, b):
+        if chain_last(q):
+            return (q, t, y, x)
+        return (q, t, b, x) if along_x(q) else (q, t, y, b)
+
+    def rise_at(q, place_of, b):
+        return (q, 4 + place_of) if chain_last(q) else (q, 2 * place_of + b)
+
+    def fall_at(q, place_of, b):
+        return (q, 7 + place_of) if chain_last(q) else (q, 6 + 2 * place_of + b)
+
+    def start_chain(q):
+        @pl.when(z == 0)
+        def rise():
+            to_up(q, 0).start()
+
+        @pl.when(z == 3)
+        def fall():
+            to_down(q, 3).start()
 
     def stage_zero(q):
         local(q).wait()
@@ -416,34 +444,33 @@
         @pl.loop(0, 8)
         def step(i):
             a, b = i // 2, i % 2
-            if q % 2 == 0:
+            if along_x(q):
                 own[q, a, b, x] = own[q, a, b, x] + got_one[q, a, b]
             else:
                 own[q, a, y, b] = own[q, a, y, b] + got_one[q, a, b]
 
-        to_two(q).start()
+        if chain_last(q):
+            to_two(q).start()
+        else:
+            start_chain(q)
 
     def stage_two(q):
         to_two(q).wait_recv()
 
         @pl.loop(0, 4)
         def step(a):
-            own[q, a, y, x] = own[q, a, y, x] + got_two[q, a]
-
-        @pl.when(z == 0)
-        def rise():
-            to_up(q, 0).start()
-
-        @pl.when(z == 3)
-        def fall():
-            to_down(q, 3).start()
+            own[q, a, y, x] = own[q, a, y, x] + tail[q, a]
+
+        start_chain(q)
 
     def stage_chain(q, hop):
         @pl.when(z == hop)
         def rise():
             to_up(q, hop - 1).wait_recv()
             for t in range(hop + 1, 4):
-                got_up[q, t - hop] = got_up[q, t - hop] + own[q, t, y, x]
+                for b in range(width(q)):
+                    at = rise_at(q, t - hop, b)
+                    tail[at] = tail[at] + own[own_at(q, t, b)]
             if hop < 3:
                 to_up(q, hop).start()
 
@@ -451,84 +478,110 @@
         def fall():
             to_down(q, 4 - hop).wait_recv()
             for t in range(0, 3 - hop):
-                got_down[q, t] = got_down[q, t] + own[q, t, y, x]
+                for b in range(width(q)):
+                    at = fall_at(q, t, b)
+                    tail[at] = tail[at] + own[own_at(q, t, b)]
             if hop < 3:
                 to_down(q, 3 - hop).start()
 
+        if hop == 3:
+            for level in range(4):
+
+                @pl.when(z == level)
+                def finish_chain():
+                    for b in range(width(q)):
+                        total = own[own_at(q, level, b)].astype(jnp.float32)
+                        if level > 0:
+                            total = total + tail[rise_at(q, 0, b)].astype(jnp.float32)
+                        if level < 3:
+                            total = total + tail[fall_at(q, level, b)].astype(jnp.float32)
+                        if chain_last(q):
+                            close(q, total)
+                        else:
+                            own[own_at(q, level, b)] = total.astype(own.dtype)
+
+            if not chain_last(q):
+                to_two(q).start()
+
     def stage_end(q):
-        @pl.when(z == 0)
-        def bottom():
-            total = own[q, 0, y, x].astype(jnp.float32) + got_down[q, 0].astype(jnp.float32)
-            out_ref[kept(q)] = total.astype(out_ref.dtype)
-
-        @pl.when(z == 3)
-        def top():
-            total = own[q, 3, y, x].astype(jnp.float32) + got_up[q, 0].astype(jnp.float32)
-            out_ref[kept(q)] = total.astype(out_ref.dtype)
-
-        for level in (1, 2):
-
-            @pl.when(z == level)
-            def middle():
-                total = own[q, level, y, x].astype(jnp.float32) + got_up[q, 0].astype(jnp.float32)
-                total = total + got_down[q, level].astype(jnp.float32)
-                out_ref[kept(q)] = total.astype(out_ref.dtype)
-
-    for q in range(slices):
-        local(q).start()
-    greet(z, y, x, core)
-    for q in range(slices):
-        to_core(q).start()
-    stages = (
-        stage_zero,
-        stage_one,
-        stage_two,
-        lambda q: stage_chain(q, 1),
-        lambda q: stage_chain(q, 2),
-        lambda q: (stage_chain(q, 3), stage_end(q)),
-    )
-    for tick in range(slices + lags[-1]):
-        for lag, stage in zip((0,) + lags, stages):
-            if 0 <= tick - lag < slices:
-                stage(tick - lag)
-    for q in range(slices):
-        to_core(q).wait_send()
-        to_one(q).wait_send()
-        to_two(q).wait_send()
-        for level in range(4):
-
-            @pl.when(z == level)
-            def sent():
-                if level < 3:
-                    to_up(q, level).wait_send()
-                if level > 0:
-                    to_down(q, level).wait_send()
-
-
-def scatter_sum(array, base, chunk, out_dtype, slices, lags, collective_id, name):
+        to_two(q).wait_recv()
+        total = own[q, z, y, x].astype(jnp.float32) + tail[q, 12].astype(jnp.float32)
+        close(q, total)
+
+    def prepare():
+        for q in range(slices):
+            local(q).start()
+
+    def begin():
+        for q in range(slices):
+            to_core(q).start()
+
+    def step_of(number):
+        def run(q):
+            if number == 0:
+                stage_zero(q)
+            elif number == 1:
+                stage_one(q)
+            elif chain_last(q):
+                stage_two(q) if number == 2 else stage_chain(q, number - 2)
+            else:
+                stage_end(q) if number == 5 else stage_chain(q, number - 1)
+
+        return run
+
+    stages = tuple(step_of(number) for number in range(6))
+
+    def finish():
+        for q in range(slices):
+            to_core(q).wait_send()
+            to_one(q).wait_send()
+            to_two(q).wait_send()
+            for level in range(4):
+
+                @pl.when(z == level)
+                def sent():
+                    if level < 3:
+                        to_up(q, level).wait_send()
+                    if level > 0:
+                        to_down(q, level).wait_send()
+
+    return prepare, begin, stages, finish
+
+
+def run_tick(tick, slices, lags, stages):
+    for lag, stage in zip((0,) + lags, stages):
+        if 0 <= tick - lag < slices:
+            stage(tick - lag)
+
+
+def scatter_kernel(base, kinds, lags, *refs):
+    prepare, begin, stages, finish = scatter_parts(base, kinds, *refs)
+    prepare()
+    greet(*place())
+    begin()
+    for tick in range(len(kinds) + lags[-1]):
+        run_tick(tick, len(kinds), lags, stages)
+    finish()
+
+
+def scatter_room(slices, rows, lanes, low):
+    return [
+        pltpu.VMEM((slices, 4, 2, 2, rows, lanes), low),
+        pltpu.VMEM((slices, 4, 2, 2, rows, lanes), low),
+        pltpu.VMEM((slices, 4, 2, rows, lanes), low),
+        pltpu.VMEM((slices, 13, rows, lanes), low),
+    ] + [pltpu.SemaphoreType.DMA((slices,))] * 11
+
+
+def scatter_sum(array, base, chunk, out_dtype, kinds, lags, collective_id, name):
     lanes = array.shape[-1]
-    rows = chunk // slices
-    low = array.dtype
-    dma = pltpu.SemaphoreType.DMA
+    slices = len(kinds)
     return pl.pallas_call(
-        functools.partial(scatter_kernel, base, slices, lags),
+        functools.partial(scatter_kernel, base, kinds, lags),
         out_shape=jax.ShapeDtypeStruct((chunk, lanes), out_dtype),
         in_specs=[pl.BlockSpec(memory_space=pl.ANY)],
         out_specs=pl.BlockSpec(memory_space=pltpu.VMEM),
-        scratch_shapes=[
-            pltpu.VMEM((slices, 4, 2, 2, rows, lanes), low),
-            pltpu.VMEM((slices, 4, 2, 2, rows, lanes), low),
-            pltpu.VMEM((slices, 4, 2, rows, lanes), low),
-            pltpu.VMEM((slices, 4, rows, lanes), low),
-            pltpu.VMEM((slices, 3, rows, lanes), low),
-            pltpu.VMEM((slices, 3, rows, lanes), low),
-            dma((slices,)),
-            dma((slices,)), dma((slices,)),
-            dma((slices,)), dma((slices,)),
-            dma((slices,)), dma((slices,)),
-            dma((slices,)), dma((slices,)),
-            dma((slices,)), dma((slices,)),
-        ],
+        scratch_shapes=scatter_room(slices, chunk // slices, lanes, array.dtype),
         compiler_params=pltpu.CompilerParams(
             collective_id=collective_id, has_side_effects=True, vmem_limit_bytes=60 << 20
         ),
@@ -536,8 +589,210 @@
     )(array.reshape(4, 2, 2, 2, -1, lanes))
 
 
-def total_kernel(x_ref, out_ref, held, got, send_sem, recv_sem):
+def spread_parts(
+    slices, width, x_ref, out_ref, local_sem, send_one, recv_one, send_up, recv_up, send_down, recv_down,
+    send_two, recv_two, send_core, recv_core,
+):
     z, y, x, core = place()
+
+    def span(q):
+        return pl.ds(q * width, width)
+
+    def local(q):
+        return pltpu.make_async_copy(x_ref.at[span(q)], out_ref.at[z, y, x, core, span(q)], local_sem.at[q])
+
+    def to_one(q):
+        where = (z, y, 1 - x, core) if q % 2 == 0 else (z, 1 - y, x, core)
+        target = out_ref.at[z, y, x, core, span(q)]
+        return remote(x_ref.at[span(q)], target, send_one.at[q], recv_one.at[q], where)
+
+    def level(block, q):
+        if q % 2 == 0:
+            return out_ref.at[block, y, :, core, span(q)]
+        return out_ref.at[block, :, x, core, span(q)]
+
+    def to_up(q, k):
+        block = level(z - k, q)
+        return remote(block, block, send_up.at[q, k], recv_up.at[q, k], (z + 1, y, x, core))
+
+    def to_down(q, k):
+        block = level(z + k, q)
+        return remote(block, block, send_down.at[q, k], recv_down.at[q, k], (z - 1, y, x, core))
+
+    def to_two(q):
+        if q % 2 == 0:
+            block, where = out_ref.at[:, y, :, core, span(q)], (z, 1 - y, x, core)
+        else:
+            block, where = out_ref.at[:, :, x, core, span(q)], (z, y, 1 - x, core)
+        return remote(block, block, send_two.at[q], recv_two.at[q], where)
+
+    def to_core(q):
+        block = out_ref.at[:, :, :, core, span(q)]
+        return remote(block, block, send_core.at[q], recv_core.at[q], (z, y, x, 1 - core))
+
+    def send_on(q, k):
+        @pl.when(jnp.logical_and(z < 3, z >= k))
+        def rise():
+            to_up(q, k).start()
+
+        @pl.when(jnp.logical_and(z > 0, z + k <= 3))
+        def fall():
+            to_down(q, k).start()
+
+    def stage_one(q):
+        local(q).wait()
+        to_one(q).wait_recv()
+        send_on(q, 0)
+
+    def stage_chain(q, hop):
+        @pl.when(z >= hop)
+        def rise():
+            to_up(q, hop - 1).wait_recv()
+
+        @pl.when(z + hop <= 3)
+        def fall():
+            to_down(q, hop - 1).wait_recv()
+
+        if hop < 3:
+            send_on(q, hop)
+        else:
+            to_two(q).start()
+
+    def stage_two(q):
+        to_two(q).wait_recv()
+        to_core(q).start()
+
+    def stage_core(q):
+        to_core(q).wait_recv()
+
+    def prepare():
+        for q in range(slices):
+            local(q).start()
+
+    def begin():
+        for q in range(slices):
+            to_one(q).start()
+
+    stages = (
+        stage_one,
+        lambda q: stage_chain(q, 1),
+        lambda q: stage_chain(q, 2),
+        lambda q: stage_chain(q, 3),
+        stage_two,
+        stage_core,
+    )
+
+    def finish():
+        for q in range(slices):
+            to_one(q).wait_send()
+            for k in range(3):
+
+                @pl.when(jnp.logical_and(z < 3, z >= k))
+                def rise():
+                    to_up(q, k).wait_send()
+
+                @pl.when(jnp.logical_and(z > 0, z + k <= 3))
+                def fall():
+                    to_down(q, k).wait_send()
+
+            to_two(q).wait_send()
+            to_core(q).wait_send()
+
+    return prepare, begin, stages, finish
+
+
+def spread_room(slices):
+    dma = pltpu.SemaphoreType.DMA
+    return [dma((slices,))] * 3 + [dma((slices, 3))] * 4 + [dma((slices,))] * 4
+
+
+def back_kernel(
+    kinds, lags, spread_slices, spread_lags, compute_lag, order,
+    x_ref, grads_ref, counts_ref, small_ref, out_ref, gathered_ref, table_ref, small_out, norm_ref, scale_ref,
+    square_ref, held, got_small, send_small, recv_small, counts_buf, grads_buf, partial, ready, counts_sem, grads_sem, table_sem, *rest,
+):
+    slices = len(kinds)
+    per_slice = F // spread_slices
+    steps = 2 * per_slice
+    last = 2 * F
+    half = counts_buf.shape[2]
+    prepare, begin, stages, finish = scatter_parts(0, kinds, x_ref, out_ref, *rest[:15], squares=square_ref)
+    also_prepare, also_begin, also_stages, also_finish = spread_parts(
+        spread_slices, per_slice, grads_ref, gathered_ref, *rest[15:]
+    )
+
+    def counts_load(n):
+        at = pl.ds(pl.multiple_of((n % 2) * half, half), half)
+        return pltpu.make_async_copy(counts_ref.at[n // 2, :, at], counts_buf.at[n % 2], counts_sem.at[n % 2])
+
+    def grads_load(n):
+        source = gathered_ref.at[pl.ds((n % 2) * 2, 2), :, :, :, n // 2]
+        return pltpu.make_async_copy(source, grads_buf.at[n % 2], grads_sem.at[n % 2])
+
+    def table_store(f):
+        return pltpu.make_async_copy(ready.at[f % 2], table_ref.at[f], table_sem.at[f % 2])
+
+    def compute(q):
+        first = q * steps
+        grads_load(first).start()
+        grads_load(first + 1).start()
+
+        @pl.loop(0, steps)
+        def step(i):
+            n = first + i
+            f = n // 2
+            slot = n % 2
+            counts_load(n).wait()
+            grads_load(n).wait()
+            part = jnp.dot(
+                counts_buf[slot], grads_buf[slot].reshape(half, EMB), preferred_element_type=jnp.float32
+            )
+
+            @pl.when(n + 2 < last)
+            def more():
+                counts_load(n + 2).start()
+
+            @pl.when(i + 2 < steps)
+            def also():
+                grads_load(n + 2).start()
+
+            @pl.when(slot == 0)
+            def keep():
+                partial[...] = part
+
+            @pl.when(slot == 1)
+            def close():
+                @pl.when(f >= 2)
+                def free():
+                    table_store(f).wait()
+
+                total = partial[...] + part
+                ready[f % 2] = total
+                table_store(f).start()
+                square_ref[...] += jnp.sum((total * total).reshape(-1, 8, EMB), axis=0)
+
+    also_prepare()
+    prepare()
+    counts_load(0).start()
+    counts_load(1).start()
+    square_ref[...] = jnp.zeros_like(square_ref)
+    greet(*place(), far=1)
+    also_begin()
+    begin()
+    for tick in range(max(slices + lags[-1], spread_slices + compute_lag)):
+        for which in order:
+            if which == 0:
+                run_tick(tick, spread_slices, spread_lags, also_stages)
+            elif which == 1:
+                run_tick(tick, slices, lags, stages)
+            elif which == 2:
+                if 0 <= tick - compute_lag < spread_slices:
+                    compute(tick - compute_lag)
+    z, y, x, core = place()
+    row = lax.broadcasted_iota(jnp.int32, small_ref.shape, 0)
+    lane = lax.broadcasted_iota(jnp.int32, small_ref.shape, 1)
+    own_square = jnp.sum(jnp.sum(square_ref[...], axis=1, keepdims=True), axis=0, keepdims=True)
+    held[0] = small_ref[...] + jnp.where(jnp.logical_and(row == 0, lane == 1), own_square, 0.0)
     partners = (
         (z, y, x, 1 - core),
         (z, y, 1 - x, core),
@@ -545,73 +800,106 @@
         (z + 1 - 2 * (z % 2), y, x, core),
         ((z + 2) % 4, y, x, core),
     )
-    barrier = pltpu.get_barrier_semaphore()
-    for where in partners:
-        pl.semaphore_signal(barrier, inc=1, device_id=device_at(*where), device_id_type=MESH)
-    pl.semaphore_wait(barrier, len(partners))
     sends = []
     for step, where in enumerate(partners):
-        source = x_ref if step == 0 else held.at[step]
-        copy = remote(source, got.at[step], send_sem.at[step], recv_sem.at[step], where)
+        copy = remote(held.at[step], got_small.at[step], send_small.at[step], recv_small.at[step], where)
         copy.start()
         copy.wait_recv()
         sends.append(copy)
+        total = held[step] + got_small[step]
         if step < len(partners) - 1:
-            held[step + 1] = source[...] + got[step]
-        else:
-            out_ref[...] = source[...] + got[step]
+            held[step + 1] = total
+    small_out[...] = total
+    squares = jnp.where(row > 0, total * total, jnp.where(lane == 1, total, 0.0))
+    norm = jnp.sqrt(jnp.sum(jnp.sum(squares, axis=1, keepdims=True), axis=0, keepdims=True))
+    norm_ref[...] = norm
+    scale_ref[...] = clip_norm / jnp.maximum(norm, clip_norm)
     for copy in sends:
         copy.wait_send()
-
-
-def total_of(array, collective_id):
-    steps = 5
-    return pl.pallas_call(
-        total_kernel,
-        out_shape=jax.ShapeDtypeStruct(array.shape, array.dtype),
-        in_specs=[pl.BlockSpec(memory_space=pltpu.VMEM)],
-        out_specs=pl.BlockSpec(memory_space=pltpu.VMEM),
+    for f in (F - 2, F - 1):
+        table_store(f).wait()
+    also_finish()
+    finish()
+
+
+def back_exchange(tiles, grads, counts, small, kinds, lags, spread_slices, spread_lags, compute_lag, order, collective_id):
+    chunk, lanes = tiles.shape[-2:]
+    slices = len(kinds)
+    table_rows, batch = counts.shape[1:]
+    samples = grads.shape[1]
+    f32, bf16 = jnp.float32, jnp.bfloat16
+    away = pl.BlockSpec(memory_space=pl.ANY)
+    near = pl.BlockSpec(memory_space=pltpu.VMEM)
+    dma = pltpu.SemaphoreType.DMA
+    mine, _, table, total, norm, scale = pl.pallas_call(
+        functools.partial(back_kernel, kinds, lags, spread_slices, spread_lags, compute_lag, order),
+        out_shape=[
+            jax.ShapeDtypeStruct((chunk, lanes), bf16),
+            jax.ShapeDtypeStruct((4, 2, 2, 2) + grads.shape, bf16),
+            jax.ShapeDtypeStruct((F, table_rows, EMB), f32),
+            jax.ShapeDtypeStruct(small.shape, f32),
+            jax.ShapeDtypeStruct((1, 1), f32),
+            jax.ShapeDtypeStruct((1, 1), f32),
+        ],
+        in_specs=[away] * 3 + [near],
+        out_specs=[near, away, away] + [near] * 3,
         scratch_shapes=[
-            pltpu.VMEM((steps,) + array.shape, array.dtype),
-            pltpu.VMEM((steps,) + array.shape, array.dtype),
-            pltpu.SemaphoreType.DMA((steps,)),
-            pltpu.SemaphoreType.DMA((steps,)),
-        ],
-        compiler_params=pltpu.CompilerParams(collective_id=collective_id, has_side_effects=True),
-        name="total_small",
-    )(array)
+            pltpu.VMEM((8, EMB), f32),
+            pltpu.VMEM((5,) + small.shape, f32),
+            pltpu.VMEM((5,) + small.shape, f32),
+            dma((5,)),
+            dma((5,)),
+            pltpu.VMEM((2, table_rows, batch // 2), bf16),
+            pltpu.VMEM((2, 2, 2, 2, 2, samples, EMB), bf16),
+            pltpu.VMEM((table_rows, EMB), f32),
+            pltpu.VMEM((2, table_rows, EMB), f32),
+            dma((2,)),
+            dma((2,)),
+            dma((2,)),
+        ]
+        + scatter_room(slices, chunk // slices, lanes, bf16)
+        + spread_room(spread_slices),
+        compiler_params=pltpu.CompilerParams(
+            collective_id=collective_id, has_side_effects=True, vmem_limit_bytes=61 << 20
+        ),
+        name="back_exchange",
+    )(tiles.reshape(4, 2, 2, 2, chunk, lanes), grads, counts, small)
+    return mine, table, total, norm[0, 0], scale[0, 0]
 
 
 def slot_kernel(scale_ref, tiles_ref, weight_ref, moment_ref, square_ref, weight_out, moment_out, square_out):
     columns = []
+    count = tiles_ref.shape[1]
     for h in range(4):
-        pieces = [tiles_ref[4 * j + h, 0] for j in range(8)]
-        columns.append(jnp.concatenate(pieces, axis=0))
-    gradient = scale_ref[0] * jnp.concatenate(columns, axis=1).astype(jnp.float32)
-    weight, moment, square = adamw(weight_ref[0], moment_ref[0], square_ref[0], gradient, rate_dense)
-    weight_out[0] = weight
-    moment_out[0] = moment
-    square_out[0] = square
+        pieces = [tiles_ref[4 * j + h] for j in range(8)]
+        columns.append(jnp.stack(pieces, axis=1).reshape(count, BR, 128))
+    gradient = scale_ref[0] * jnp.concatenate(columns, axis=2).astype(jnp.float32)
+    weight, moment, square = adamw(weight_ref[...], moment_ref[...], square_ref[...], gradient, rate_dense)
+    weight_out[...] = weight
+    moment_out[...] = moment
+    square_out[...] = square
 
 
 def slot_update(scale, tiles, weight, moment, square):
     slots = weight.shape[0]
-    block = pl.BlockSpec((1, BR, RANK), lambda s: (s, 0, 0))
+    group = 3
+    block = pl.BlockSpec((group, BR, RANK), lambda s: (s, 0, 0))
     return tuple(
         pl.pallas_call(
             slot_kernel,
-            grid=(slots,),
+            grid=(slots // group,),
             in_specs=[
                 pl.BlockSpec(memory_space=pltpu.SMEM),
-                pl.BlockSpec((32, 1, 16, 128), lambda s: (0, s, 0, 0)),
+                pl.BlockSpec((32, group, 16, 128), lambda s: (0, s, 0, 0)),
                 block,
                 block,
                 block,
             ],
             out_specs=[block] * 3,
             out_shape=[jax.ShapeDtypeStruct(weight.shape, jnp.float32)] * 3,
+            compiler_params=pltpu.CompilerParams(vmem_limit_bytes=48 << 20),
             name="slot_update",
-        )(scale[None], tiles, weight, moment, square)
+        )(scale.reshape(1), tiles, weight, moment, square)
     )
 
 
@@ -627,6 +915,16 @@
 TWO_AT = ONE_AT + FCH * FBLK
 THREE_AT = TWO_AT + 16
 GROUPS = tuple((k * 27, 27) for k in (0, 3, 1, 4, 2, 5)) + ((ONE_AT, 54), (TWO_AT, 16), (THREE_AT, 8))
+NDENSE = 13
+PROJ_ROW = 1
+HEAD_ROW = PROJ_ROW + NDENSE
+DENSE_ROW = HEAD_ROW + 4
+CROSS_ROW = DENSE_ROW + 1
+ONE_ROW = CROSS_ROW + LAYERS * 27
+TWO_ROW = ONE_ROW + 8
+THREE_ROW = TWO_ROW + 8
+LAST_ROW = THREE_ROW + 4
+SMALL_ROWS = 128
 GELU_A = 0.7978845608028654
 GELU_B = 0.044715
 
@@ -646,8 +944,8 @@
 
 
 def dense_kernel(
-    batch, tiles_hbm, pooled_ref, dense_ref, label_ref, head_ref, last_ref, cross_bias_ref, one_bias_ref,
-    two_bias_ref, three_bias_ref, grads_hbm, grad_pooled_ref, grad_dense_ref, cross_grad_ref, small_ref,
+    batch, tiles_hbm, pooled_ref, feats_ref, dense_ref, label_ref, head_ref, last_ref, cross_bias_ref, one_bias_ref,
+    two_bias_ref, three_bias_ref, grads_hbm, grad_pooled_ref, small_ref,
     tiles, anchor, current, mixing, low, grad_anchor, wide_one, wide_two, stage, load_sem, store_sem,
 ):
     samples = dense_ref.shape[0]
@@ -680,6 +978,12 @@
             for h in range(4):
                 stage[slot, 4 * j + h, pl.ds(0, count)] = value[:, 16 * j : 16 * j + 16, 128 * h : 128 * h + 128]
         store(slot, first, count).start()
+
+    small_ref[...] = jnp.zeros_like(small_ref)
+
+    def note(row, value):
+        for m in range(value.shape[1] // 128):
+            small_ref[pl.ds(row + m, 1), :] = value[:, m * 128 : (m + 1) * 128]
 
     for i in range(F + 1):
         block = dense_ref[...] if i == 0 else pooled_ref[(i - 1) * EMB : i * EMB, :].astype(f32).T
@@ -757,19 +1061,20 @@
     labels = label_ref[...]
     losses = jnp.maximum(logits, 0.0) + jnp.log1p(jnp.exp(-jnp.abs(logits))) - labels * logits
     grad_logits = (1.0 / (1.0 + jnp.exp(-logits)) - labels) / batch
-    small_ref[6:7, :] = jnp.broadcast_to(jnp.sum(losses, axis=0, keepdims=True), (1, RANK))
-    small_ref[7:8, :] = jnp.broadcast_to(jnp.sum(grad_logits, axis=0, keepdims=True), (1, RANK))
-    small_ref[5:6, :] = jnp.sum(hidden_three * grad_logits, axis=0, keepdims=True)
+    first_lane = lax.broadcasted_iota(jnp.int32, (1, 128), 1) == 0
+    note(0, jnp.where(first_lane, jnp.sum(losses, axis=0, keepdims=True), 0.0))
+    note(LAST_ROW, jnp.where(first_lane, jnp.sum(grad_logits, axis=0, keepdims=True), 0.0))
+    note(HEAD_ROW, jnp.sum(hidden_three * grad_logits, axis=0, keepdims=True))
 
     grad_before = grad_logits * head * gelu_slope(pre_three)
-    small_ref[4:5, :] = jnp.sum(grad_before, axis=0, keepdims=True)
+    note(THREE_ROW, jnp.sum(grad_before, axis=0, keepdims=True))
     grad_low = grad_before.astype(bf16)
     emit(0, THREE_AT, 8, mul(hidden_two, grad_low, TN))
     grad_hidden = mul(grad_low, matrix(THREE_AT, 8), NT)
     parts = []
     for p in range(2):
         grad_before = grad_hidden[:, p * RANK : (p + 1) * RANK] * gelu_slope(pre_two[p])
-        small_ref[2 + p : 3 + p, :] = jnp.sum(grad_before, axis=0, keepdims=True)
+        note(TWO_ROW + 4 * p, jnp.sum(grad_before, axis=0, keepdims=True))
         parts.append(grad_before.astype(bf16))
     grad_low = jnp.concatenate(parts, axis=0)
     parts = []
@@ -782,7 +1087,7 @@
             [narrowed(wide[:, m * 2 * BR : (m + 1) * 2 * BR]) for m in range(4)], axis=1
         )
         grad_before = grad_hidden * gelu_slope(pre_one[c])
-        small_ref[c : c + 1, :] = jnp.sum(grad_before, axis=0, keepdims=True)
+        note(ONE_ROW + 4 * c, jnp.sum(grad_before, axis=0, keepdims=True))
         parts.append(grad_before.astype(bf16))
     grad_one = jnp.concatenate(parts, axis=0)
     store(1, TWO_AT, 8).wait()
@@ -815,7 +1120,7 @@
             slot = (base + c) % 2
             before = current[c]
             grad_mixing = anchor[c] * before
-            cross_grad_ref[pl.ds(depth * CHUNKS + c, 1), :] = jnp.sum(grad_mixing, axis=0, keepdims=True)
+            note(CROSS_ROW + depth * 27 + c * CBLK, jnp.sum(grad_mixing, axis=0, keepdims=True))
             grad_low = grad_mixing.astype(bf16)
 
             @pl.when(base + c >= 2)
@@ -841,15 +1146,19 @@
                 grad_anchor[c] = grad_anchor[c] + after
 
         sent += 2 * CHUNKS
-    grad_dense_ref[...] = grad_anchor[0, :, :EMB]
+    grad_dense = grad_anchor[0, :, :EMB]
+    note(DENSE_ROW, jnp.sum(grad_dense, axis=0, keepdims=True))
+    small_ref[PROJ_ROW : PROJ_ROW + NDENSE, :] = lax.dot_general(
+        feats_ref[...], grad_dense, TN, precision=highest, preferred_element_type=f32
+    )[:NDENSE]
     for i in range(1, F + 1):
         c, at = i // CBLK, (i % CBLK) * BR
-        grad_pooled_ref[:, (i - 1) * EMB : i * EMB] = grad_anchor[c, :, at : at + BR].astype(bf16)
+        grad_pooled_ref[i - 1] = grad_anchor[c, :, at : at + BR].astype(bf16)
     for slot in range(2):
         store(slot, 0, CBLK).wait()
 
 
-def dense_step(tiles, pooled, dense_part, labels, head, bias_last, bias_cross, bias_one, bias_two, bias_three, batch):
+def dense_step(tiles, pooled, feats, dense_part, labels, head, bias_last, bias_cross, bias_one, bias_two, bias_three, batch):
     samples = dense_part.shape[0]
     f32, bf16 = jnp.float32, jnp.bfloat16
     whole = pl.BlockSpec(memory_space=pltpu.VMEM)
@@ -859,13 +1168,11 @@
         functools.partial(dense_kernel, batch),
         out_shape=[
             shape(tiles.shape, bf16),
-            shape((samples, F * EMB), bf16),
-            shape((samples, EMB), f32),
-            shape((LAYERS * CHUNKS, CW), f32),
-            shape((8, RANK), f32),
+            shape((F, samples, EMB), bf16),
+            shape((SMALL_ROWS, 128), f32),
         ],
-        in_specs=[away] + [whole] * 9,
-        out_specs=[away] + [whole] * 4,
+        in_specs=[away] + [whole] * 10,
+        out_specs=[away] + [whole] * 2,
         scratch_shapes=[
             pltpu.VMEM(tiles.shape, bf16),
             pltpu.VMEM((CHUNKS, samples, CW), f32),
@@ -881,7 +1188,7 @@
         ],
         compiler_params=pltpu.CompilerParams(vmem_limit_bytes=61 << 20),
         name="dense_step",
-    )(tiles, pooled, dense_part, labels, head, bias_last, bias_cross, bias_one, bias_two, bias_three)
+    )(tiles, pooled, feats, dense_part, labels, head, bias_last, bias_cross, bias_one, bias_two, bias_three)
 
 
 def body(
@@ -1126,14 +1433,15 @@
     room = (capacity + samples - 1) // samples * samples + samples
     keys = jnp.pad(received, ((0, 0), (0, room - capacity)), constant_values=-1)
     counts, partial = count_tables(offsets, keys, embed_table, devices, samples)
-    pooled = scatter_sum(partial, 0, F * EMB, bf16, 16, (2, 4, 6, 7, 8), 0, "scatter_pooled")
+    pooled = scatter_sum(partial, 0, F * EMB, bf16, (0, 1) * 8, (2, 4, 6, 7, 8), 0, "scatter_pooled")
     dense_part = (
         jnp.dot(dense_feats, dense_proj, precision=highest, preferred_element_type=jnp.float32)
         + bias_dense
     )
-    grad_tiles, grad_pooled, grad_dense, grad_cross, grad_small = dense_step(
+    grad_tiles, grad_pooled, grad_small = dense_step(
         tiles,
         pooled,
+        jnp.pad(dense_feats, ((0, 0), (0, 3))),
         dense_part,
         click_labels.astype(jnp.float32)[:, None],
         head_weight[None, :],
@@ -1144,73 +1452,35 @@
         bias_three[None, :],
         samples * devices,
     )
-    gathered_grads = lax.all_gather(grad_pooled, "row", axis=0, tiled=True)
-    grad_mine = scatter_sum(
+    grad_mine, grad_table, small_total, grad_norm, clip_scale = back_exchange(
         grad_tiles.reshape(devices, block_count * 16, 128),
-        0,
-        block_count * 16,
-        jnp.float32,
-        16,
-        (2, 4, 6, 7, 8),
+        grad_pooled,
+        counts,
+        grad_small,
+        (0, 1, 0, 1, 2, 3, 0, 1) * 2,
+        (3, 6, 8, 9, 10),
+        13,
+        (1, 2, 3, 4, 5),
+        6,
+        (0, 1, 2),
         1,
-        "scatter_dense",
-    )
-    grad_table, table_squares = row_grads(counts, gathered_grads)
+    )
     matches = block_owners[None, :] == jnp.arange(devices * slot_count, dtype=jnp.int32)[:, None]
     inverse = jnp.sum(
         jnp.where(matches, jnp.arange(block_count, dtype=jnp.int32)[None, :], 0), axis=1
     )
     named = jnp.any(matches, axis=1)
     returned = jnp.take(
-        grad_mine.astype(bf16).reshape(block_count, 16, 128), inverse, axis=0, mode="clip"
+        grad_mine.reshape(block_count, 16, 128), inverse, axis=0, mode="clip"
     )
     returned = jnp.where(named[:, None, None], returned, 0)
     returned = lax.all_to_all(
         returned.reshape(devices, slot_count * 16, 128), "row", split_axis=0, concat_axis=0, tiled=True
     )
-    grad_proj_local = jnp.einsum(
-        "sa,sb->ab",
-        dense_feats,
-        grad_dense,
-        precision=highest,
-        preferred_element_type=jnp.float32,
-    )
-    bias_local = jnp.concatenate(
-        [
-            jnp.sum(grad_dense, axis=0),
-            grad_cross.reshape(-1),
-            grad_small[0:5].reshape(-1),
-            grad_small[7, :1],
-        ]
-    )
-    squares_local = jnp.sum(table_squares) + jnp.sum(grad_mine * grad_mine)
-    packed = jnp.concatenate(
-        [
-            grad_small[6, :1],
-            squares_local[None],
-            grad_proj_local.reshape(-1),
-            grad_small[5],
-            bias_local,
-        ]
-    )
-    room = -packed.shape[0] % 1024
-    packed = total_of(jnp.pad(packed, (0, room)).reshape(-1, 128), 2).reshape(-1)
-    cuts = [0, 1, 2]
-    for size in (dense_proj.size, head_weight.size, biases.size):
-        cuts.append(cuts[-1] + size)
-    loss_total, squares, grad_proj, grad_head, grad_bias = [
-        packed[first:last] for first, last in zip(cuts[:-1], cuts[1:])
-    ]
-    loss_total, squares = loss_total[0], squares[0]
-    grad_proj = grad_proj.reshape(dense_proj.shape)
-    squares = (
-        squares
-        + jnp.sum(grad_proj * grad_proj)
-        + jnp.sum(grad_head * grad_head)
-        + jnp.sum(grad_bias * grad_bias)
-    )
-    grad_norm = jnp.sqrt(squares)
-    clip_scale = clip_norm / jnp.maximum(grad_norm, clip_norm)
+    loss_total = small_total[0, 0]
+    grad_proj = small_total[PROJ_ROW : PROJ_ROW + NDENSE]
+    grad_head = small_total[HEAD_ROW : HEAD_ROW + 4].reshape(-1)
+    grad_bias = small_total[DENSE_ROW : LAST_ROW + 1].reshape(-1)[:NBIAS]
     table_new = adamw(embed_table, table_moment, table_square, clip_scale * grad_table, rate_table)
     dense_new = slot_update(
         clip_scale,

time: 776 us -> 716 us (0.923)
  Pallas kernels: 629 us -> 573 us
  waiting for transfers between devices: 5.07 us -> 17.6 us
    pallas_call x5 -> x3, Pallas kernels: 521 us -> 465 us  [the longest x1 257 us: back_exchange(): pl.pallas_call(functools.partial(back_kernel, kinds, lags, spread_slices,...]
    all_to_all x1, waiting for transfers between devices: 0.01 us -> 14 us  [body_counted(): lax.all_to_all(returned.reshape(devices, slot_count * 16, 128), 'row', sp...]
  transfers between devices with their start and end apart: 5 -> 4, of which waited for: 1 -> 2; matrix products, arithmetic and copies ran while one was open for 12% -> 10% of each run, Pallas kernels for 74% -> 37%
where the time goes in v3:
time: 716 us; the launch traced here: 712 us
  Pallas kernels  573 us (80%)
  other arithmetic  68.1 us (10%)
  local copies, waits for them, and re-layouts  18.7 us (3%)
  waiting for transfers between devices  17.6 us (2%)
  between operations  17.1 us (2%)
  starting transfers between devices  16.6 us (2%)
    pallas_call x1, Pallas kernels, back_exchange(): pl.pallas_call(functools.partial(back_kernel, kinds, lags, spread_slices,...  257 us
    pallas_call x1, Pallas kernels, scatter_sum(): pl.pallas_call(functools.partial(scatter_kernel, base, kinds, lags), out_...  199 us
    pallas_call x1, Pallas kernels, count_tables(): pl.pallas_call(functools.partial(count_kernel, devices, samples, table_ro...  60.9 us
    pallas_call x1, Pallas kernels, dense_step(): pl.pallas_call(functools.partial(dense_kernel, batch), out_shape=[shape(t...  46.4 us
    sort x1, other arithmetic, body_counted(): ordered = lax.sort(key.reshape(-1), is_stable=False)[:live_total]  37.7 us
    sub x4, other arithmetic, adamw(): weight - step_rate * (corrected / (jnp.sqrt(scaled) + adam_eps) + decay_r...  23.2 us
  transfers between devices with their start and end apart: 4, of which 2 were waited for; matrix products, arithmetic and copies ran while one was open for 10% of the time, Pallas kernels for 37%

profile of v3, /device:TPU:0, one launch (start us, length us, event | category | flops | bytes accessed | tf_op | source)
XLA Modules:
  0.0 711.6 jit_solution(5801235859805513939)
XLA Ops:
  7.2 2.1 convert_element_type.13
  9.3 0.4 reshape.110
  9.7 0.0 copy-start.11
  9.8 1.5 copy.63
  11.3 0.0 copy-start.6
  11.3 7.4 %all-to-all-start = ((bf16[32,192,128]{2,1,0:T(8,128)(2,1)}), bf16[32,192,128]{2,1,0:T(8,128)(2,1)}, u32[]{:S(2)}, u32[]{:S(2)}) async-start(bf16[32,192,128]{2,1,0:T(8,128)(2,1)} %bitcast.1), calls=%async_computation | async-start | bytes 3145728 | tf_op jit(solution)/shard_map/all_to_all | solution.py:1408
  18.7 0.0 all-gather.2.cloned.1.call-start
  18.8 0.0 copy-done.7
  18.8 1.5 fusion.5
  20.3 1.9 copy.64
  22.2 1.0 reshape.113
  23.2 37.7 %sort.7 = s32[99840]{0:T(1024)S(1)} sort(s32[99840]{0:T(1024)S(1)} %reshape.113), dimensions={0}, to_apply=%region_0.1 | sort | flops 1697280 | bytes 798720 | tf_op jit(solution)/shard_map/sort | solution.py:1419
  60.9 0.5 slice.65
  62.1 0.0 all-to-all-done
  62.2 3.1 gather_fusion
  65.3 0.0 all-gather.2.cloned.1.call-update
  65.3 1.0 and.31
  66.4 5.8 all-to-all-start.1
  72.2 0.5 slice.51
  72.7 0.6 slice.55
  73.3 0.6 reshape.118.one_bias_ref
  73.9 0.6 reshape.119.two_bias_ref
  74.5 0.1 copy.67
  74.6 0.6 reshape_reshape.6.cross_bias_ref
  75.2 0.7 copy.68.label_ref
  76.0 0.1 fusion.11
  76.1 0.1 broadcast_in_dim.68
  76.2 0.1 copy.69
  76.3 0.1 copy.70
  76.4 0.6 pad.9.feats_ref
  77.1 0.1 select_reduce_fusion
  77.2 0.9 convolution_add_fusion.dense_ref
  78.2 3.6 all-to-all-done.1
  81.8 0.8 convert_reduce_fusion
  82.6 0.1 copy.65
  82.7 0.1 reshape.116.off_ref
  82.8 0.1 fusion.13.most_ref
  82.9 60.9 %count_tables.1 = (bf16[26,512,4096]{2,1,0:T(8,128)(2,1)}, bf16[32,26,128,128]{3,2,1,0:T(8,128)(2,1)}) custom-call(s32[864]{0:T(1024)S(1)} %reshape.116.off_ref, s32[26]{0:T(128)S(1)} %fusion.13.most_ref, s32[32,1792]{1,0:T(8,128)S(1)} %pad.8.keys_ref, f32[26,512,128]{2,1,0:T(8,128)} %table_ref.1), custom_call_target="tpu_custom_call" | custom-call | tf_op jit(solution)/shard_map/count_tables/pallas_call | solution.py:242
  143.9 199.1 %scatter_pooled.1.pooled_ref = bf16[3328,128]{1,0:T(8,128)(2,1)} custom-call(bf16[4,2,2,2,3328,128]{5,4,3,2,1,0:T(8,128)(2,1)} %bitcast.39), custom_call_target="tpu_custom_call" | custom-call | tf_op jit(solution)/shard_map/scatter_pooled/pallas_call | solution.py:579
  343.0 0.0 all-gather.2.cloned.1.call-done
  343.0 1.3 broadcast_in_dim.66.last_ref
  344.3 46.4 %dense_step.1 = (bf16[32,240,16,128]{3,2,1,0:T(8,128)(2,1)}, bf16[26,128,128]{2,1,0:T(8,128)(2,1)}, f32[128,128]{1,0:T(8,128)}) custom-call(bf16[32,240,16,128]{3,2,1,0:T(8,128)(2,1)} %bitcast.38, bf16[3328,128]{1,0:T(8,128)(2,1)} %scatter_pooled.1.pooled_ref, f32[128,16]{1,0:T(8,128)} %pad.9.feats_ref, f32[128,128]{1,0:T(8,128)} %convolution_add_fusion.dense_ref, ...), custom_call_target="tpu_custom_call" | custom-call | tf_op jit(solution)/shard_map/dense_step/pallas_call | solution.py:1167
  390.7 257.2 %back_exchange.1 = (bf16[3840,128]{1,0:T(8,128)(2,1)}, bf16[4,2,2,2,26,128,128]{6,5,4,3,2,1,0:T(8,128)(2,1)}, f32[26,512,128]{2,1,0:T(8,128)}, f32[128,128]{1,0:...) custom-call(bf16[4,2,2,2,3840,128]{5,4,3,2,1,0:T(8,128)(2,1)} %bitcast.37, bf16[26,128,128]{2,1,0:T(8,128)(2,1)} %get-tuple-element.32.grads_ref, ...), custom_call_target="tpu_custom_call" | custom-call | tf_op jit(solution)/shard_map/back_exchange/pallas_call | solution.py:834
  647.9 0.0 copy-start.2
  648.0 0.0 copy-start.9
  648.0 0.0 copy-start.10
  648.0 0.0 copy-start.8
  648.0 0.0 copy-start.12
  648.0 0.0 copy-start.13
  648.0 0.0 copy-start.3
  648.0 0.0 copy-start.4
  648.0 2.3 gather_fusion.1
  650.3 2.3 bitcast_select_fusion
  652.7 3.4 all-to-all-start.2
  656.1 1.3 multiply_subtract_fusion.2
  657.4 0.0 copy-done.12
  657.4 1.3 multiply_subtract_fusion.3
  658.7 0.5 slice.56
  659.2 0.0 copy-done.3
  659.2 0.0 copy-done.4
  659.3 1.4 multiply_subtract_fusion.1
  660.6 19.3 %multiply_subtract_fusion = (f32[26,512,128]{2,1,0:T(8,128)}, f32[26,512,128]{2,1,0:T(8,128)}, f32[26,512,128]{2,1,0:T(8,128)}) fusion(f32[26,512,128]{2,1,0:T(8,128)} %table_ref.1, f32[26,512,128]{2,1,0:T(8,128)} %get-tuple-element.38, f32[]{:T(128)} %bitcast.14, f32[26,512,128]{2,1,0:T(8,128)} %param.26, f32[26,512,128]{2,1,0:T(8,128)} %param.27), kind=kLoop, calls=%fused_computation.4 | loop fusion | flops 27262976 | bytes 47710212 | tf_op jit(solution)/shard_map/sub | solution.py:153
  679.9 14.0 %all-to-all-done.2 = bf16[32,192,128]{2,1,0:T(8,128)(2,1)} async-done(((bf16[32,192,128]{2,1,0:T(8,128)(2,1)}), bf16[32,192,128]{2,1,0:T(8,128)(2,1)}, u32[]{:S(2)}, u32[]{:S(2)}) %all-to-all-start.2) | async-done | bytes 1572896 | tf_op jit(solution)/shard_map/all_to_all | solution.py:1477
  693.9 8.9 %slot_update.1 = (f32[12,128,512]{2,1,0:T(8,128)}, f32[12,128,512]{2,1,0:T(8,128)}, f32[12,128,512]{2,1,0:T(8,128)}) custom-call(f32[1]{0:T(128)} %bitcast.15.scale_ref, bf16[32,12,16,128]{3,2,1,0:T(8,128)(2,1)} %bitcast.19.tiles_ref, f32[12,128,512]{2,1,0:T(8,128)S(1)} %copy-done, f32[12,128,512]{2,1,0:T(8,128)} %moment_ref.1, f32[12,128,512]{2,1,0:T(8,128)} %square_ref.1), custom_call_target="tpu_custom_call" | custom-call | tf_op jit(solution)/shard_map/slot_update/pallas_call | solution.py:888
  (31 shorter events, 0.2 us)
Async XLA Ops:
  7.2 11.6 %copy-start.7 = (s32[128,26]{0,1:T(8,128)S(1)}, s32[128,26]{0,1:T(8,128)}, u32[]{:S(2)}) copy-start(s32[128,26]{0,1:T(8,128)} %param.21) | copy-start | bytes 39940
  9.7 52.4 %copy-start.11 = (s32[240]{0:T(256)S(1)}, s32[240]{0:T(256)}, u32[]{:S(2)}) copy-start(s32[240]{0:T(256)} %param.24) | copy-start | bytes 2884
  11.3 60.9 %copy-start.1 = (f32[13057]{0:T(1024)S(1)}, f32[13057]{0:T(1024)}, u32[]{:S(2)}) copy-start(f32[13057]{0:T(1024)} %param.37) | copy-start | bytes 156688
  11.3 63.2 %copy-start.5 = (f32[128,13]{0,1:T(8,128)S(1)}, f32[128,13]{0,1:T(8,128)}, u32[]{:S(2)}) copy-start(f32[128,13]{0,1:T(8,128)} %param.22) | copy-start | bytes 19972
  11.3 63.9 %copy-start.14 = (s32[128]{0:T(128)S(1)}, s32[128]{0:T(128)}, u32[]{:S(2)}) copy-start(s32[128]{0:T(128)} %param.23) | copy-start | bytes 1540
  11.3 65.9 %slice-start = ((f32[13057]{0:T(1024)}), f32[128]{0:T(128)S(1)}, s32[]{:S(2)}) async-start(f32[13057]{0:T(1024)} %param.37), calls=%async_computation.4 | async-start | bytes 1024 | tf_op jit(solution)/shard_map/slice | solution.py:52
  11.3 65.9 %copy-start.6 = (f32[13,128]{1,0:T(8,128)S(1)}, f32[13,128]{1,0:T(8,128)}, u32[]{:S(2)}) copy-start(f32[13,128]{1,0:T(8,128)} %param.31) | copy-start | bytes 19972
  11.3 50.8 %all-to-all-start = ((bf16[32,192,128]{2,1,0:T(8,128)(2,1)}), bf16[32,192,128]{2,1,0:T(8,128)(2,1)}, u32[]{:S(2)}, u32[]{:S(2)}) async-start(bf16[32,192,128]{2,1,0:T(8,128)(2,1)} %bitcast.1), calls=%async_computation | async-start | bytes 3145728 | tf_op jit(solution)/shard_map/all_to_all | solution.py:1408
  18.7 324.3 %all-gather.2.cloned.1.call-start = ((), (), s32[]{:S(2)}) async-start(), calls=%async_computation.3 | async-start | bytes 32440320 | tf_op jit(solution)/shard_map/all_gather | solution.py:1426
  66.4 15.4 %all-to-all-start.1 = ((s32[32,1,1612]{2,1,0:T(1,128)}), s32[32,1,1612]{2,1,0:T(1,128)S(1)}, u32[]{:S(2)}, u32[]{:S(2)}) async-start(s32[32,1,1612]{2,1,0:T(1,128)} %and.31), calls=%async_computation.1 | async-start | bytes 425984 | tf_op jit(solution)/shard_map/all_to_all | solution.py:1430
  647.9 8.1 %copy-start.2 = (f32[128,128]{1,0:T(8,128)S(1)}, f32[128,128]{1,0:T(8,128)}, u32[]{:S(2)}) copy-start(f32[128,128]{1,0:T(8,128)} %get-tuple-element.35) | copy-start | bytes 196612
  648.0 8.1 %copy-start.9 = (f32[13,128]{1,0:T(8,128)S(1)}, f32[13,128]{1,0:T(8,128)}, u32[]{:S(2)}) copy-start(f32[13,128]{1,0:T(8,128)} %param.32) | copy-start | bytes 19972
  648.0 8.1 %copy-start.10 = (f32[13,128]{1,0:T(8,128)S(1)}, f32[13,128]{1,0:T(8,128)}, u32[]{:S(2)}) copy-start(f32[13,128]{1,0:T(8,128)} %param.33) | copy-start | bytes 19972
  648.0 9.4 %copy-start.8 = (f32[512]{0:T(512)S(1)}, f32[512]{0:T(512)}, u32[]{:S(2)}) copy-start(f32[512]{0:T(512)} %param.34) | copy-start | bytes 6148
  648.0 9.4 %copy-start.12 = (f32[512]{0:T(512)S(1)}, f32[512]{0:T(512)}, u32[]{:S(2)}) copy-start(f32[512]{0:T(512)} %param.35) | copy-start | bytes 6148
  648.0 9.4 %copy-start.13 = (f32[512]{0:T(512)S(1)}, f32[512]{0:T(512)}, u32[]{:S(2)}) copy-start(f32[512]{0:T(512)} %param.36) | copy-start | bytes 6148
  648.0 11.2 %copy-start.3 = (f32[13057]{0:T(1024)S(1)}, f32[13057]{0:T(1024)}, u32[]{:S(2)}) copy-start(f32[13057]{0:T(1024)} %param.38) | copy-start | bytes 156688
  648.0 11.2 %copy-start.4 = (f32[13057]{0:T(1024)S(1)}, f32[13057]{0:T(1024)}, u32[]{:S(2)}) copy-start(f32[13057]{0:T(1024)} %param.39) | copy-start | bytes 156688
  652.7 41.2 %all-to-all-start.2 = ((bf16[32,192,128]{2,1,0:T(8,128)(2,1)}), bf16[32,192,128]{2,1,0:T(8,128)(2,1)}, u32[]{:S(2)}, u32[]{:S(2)}) async-start(bf16[32,192,128]{2,1,0:T(8,128)(2,1)} %bitcast_select_fusion), calls=%async_computation.2 | async-start | bytes 3145728 | tf_op jit(solution)/shard_map/all_to_all | solution.py:1477
  660.6 33.3 %copy-start = (f32[12,128,512]{2,1,0:T(8,128)S(1)}, f32[12,128,512]{2,1,0:T(8,128)}, u32[]{:S(2)}) copy-start(f32[12,128,512]{2,1,0:T(8,128)} %weight_ref.1) | copy-start | bytes 9437188
Sparse Core Ops, SparseCore 0:
  65.4 260.2 all-gather.1

commit v4 on v3

--- a/solution.py
+++ b/solution.py
@@ -554,16 +554,6 @@
             stage(tick - lag)
 
 
-def scatter_kernel(base, kinds, lags, *refs):
-    prepare, begin, stages, finish = scatter_parts(base, kinds, *refs)
-    prepare()
-    greet(*place())
-    begin()
-    for tick in range(len(kinds) + lags[-1]):
-        run_tick(tick, len(kinds), lags, stages)
-    finish()
-
-
 def scatter_room(slices, rows, lanes, low):
     return [
         pltpu.VMEM((slices, 4, 2, 2, rows, lanes), low),
@@ -573,22 +563,6 @@
     ] + [pltpu.SemaphoreType.DMA((slices,))] * 11
 
 
-def scatter_sum(array, base, chunk, out_dtype, kinds, lags, collective_id, name):
-    lanes = array.shape[-1]
-    slices = len(kinds)
-    return pl.pallas_call(
-        functools.partial(scatter_kernel, base, kinds, lags),
-        out_shape=jax.ShapeDtypeStruct((chunk, lanes), out_dtype),
-        in_specs=[pl.BlockSpec(memory_space=pl.ANY)],
-        out_specs=pl.BlockSpec(memory_space=pltpu.VMEM),
-        scratch_shapes=scatter_room(slices, chunk // slices, lanes, array.dtype),
-        compiler_params=pltpu.CompilerParams(
-            collective_id=collective_id, has_side_effects=True, vmem_limit_bytes=60 << 20
-        ),
-        name=name,
-    )(array.reshape(4, 2, 2, 2, -1, lanes))
-
-
 def spread_parts(
     slices, width, x_ref, out_ref, local_sem, send_one, recv_one, send_up, recv_up, send_down, recv_down,
     send_two, recv_two, send_core, recv_core,
@@ -706,8 +680,47 @@
     return [dma((slices,))] * 3 + [dma((slices, 3))] * 4 + [dma((slices,))] * 4
 
 
+def front_kernel(kinds, lags, spread_slices, spread_lags, delay, x_ref, tiles_ref, out_ref, gathered_ref, *rest):
+    slices = len(kinds)
+    prepare, begin, stages, finish = scatter_parts(0, kinds, x_ref, out_ref, *rest[:15])
+    also_prepare, also_begin, also_stages, also_finish = spread_parts(
+        spread_slices, tiles_ref.shape[0] // spread_slices, tiles_ref, gathered_ref, *rest[15:]
+    )
+    also_prepare()
+    prepare()
+    greet(*place())
+    also_begin()
+    begin()
+    for tick in range(max(slices + lags[-1], spread_slices + spread_lags[-1] + delay)):
+        run_tick(tick - delay, spread_slices, spread_lags, also_stages)
+        run_tick(tick, slices, lags, stages)
+    also_finish()
+    finish()
+
+
+def front_exchange(array, tiles, chunk, kinds, lags, spread_slices, spread_lags, delay, collective_id):
+    lanes = array.shape[-1]
+    slices = len(kinds)
+    away = pl.BlockSpec(memory_space=pl.ANY)
+    summed, gathered = pl.pallas_call(
+        functools.partial(front_kernel, kinds, lags, spread_slices, spread_lags, delay),
+        out_shape=[
+            jax.ShapeDtypeStruct((chunk, lanes), array.dtype),
+            jax.ShapeDtypeStruct((4, 2, 2, 2) + tiles.shape, tiles.dtype),
+        ],
+        in_specs=[away] * 2,
+        out_specs=[pl.BlockSpec(memory_space=pltpu.VMEM), away],
+        scratch_shapes=scatter_room(slices, chunk // slices, lanes, array.dtype) + spread_room(spread_slices),
+        compiler_params=pltpu.CompilerParams(
+            collective_id=collective_id, has_side_effects=True, vmem_limit_bytes=60 << 20
+        ),
+        name="front_exchange",
+    )(array.reshape(4, 2, 2, 2, -1, lanes), tiles)
+    return summed, gathered.reshape((32,) + tiles.shape)
+
+
 def back_kernel(
-    kinds, lags, spread_slices, spread_lags, compute_lag, order,
+    kinds, lags, spread_slices, spread_lags, compute_lag, delay,
     x_ref, grads_ref, counts_ref, small_ref, out_ref, gathered_ref, table_ref, small_out, norm_ref, scale_ref,
     square_ref, held, got_small, send_small, recv_small, counts_buf, grads_buf, partial, ready, counts_sem, grads_sem, table_sem, *rest,
 ):
@@ -779,15 +792,11 @@
     greet(*place(), far=1)
     also_begin()
     begin()
-    for tick in range(max(slices + lags[-1], spread_slices + compute_lag)):
-        for which in order:
-            if which == 0:
-                run_tick(tick, spread_slices, spread_lags, also_stages)
-            elif which == 1:
-                run_tick(tick, slices, lags, stages)
-            elif which == 2:
-                if 0 <= tick - compute_lag < spread_slices:
-                    compute(tick - compute_lag)
+    for tick in range(max(slices + lags[-1], spread_slices + compute_lag + delay)):
+        run_tick(tick - delay, spread_slices, spread_lags, also_stages)
+        run_tick(tick, slices, lags, stages)
+        if 0 <= tick - delay - compute_lag < spread_slices:
+            compute(tick - delay - compute_lag)
     z, y, x, core = place()
     row = lax.broadcasted_iota(jnp.int32, small_ref.shape, 0)
     lane = lax.broadcasted_iota(jnp.int32, small_ref.shape, 1)
@@ -822,7 +831,7 @@
     finish()
 
 
-def back_exchange(tiles, grads, counts, small, kinds, lags, spread_slices, spread_lags, compute_lag, order, collective_id):
+def back_exchange(tiles, grads, counts, small, kinds, lags, spread_slices, spread_lags, compute_lag, delay, collective_id):
     chunk, lanes = tiles.shape[-2:]
     slices = len(kinds)
     table_rows, batch = counts.shape[1:]
@@ -832,7 +841,7 @@
     near = pl.BlockSpec(memory_space=pltpu.VMEM)
     dma = pltpu.SemaphoreType.DMA
     mine, _, table, total, norm, scale = pl.pallas_call(
-        functools.partial(back_kernel, kinds, lags, spread_slices, spread_lags, compute_lag, order),
+        functools.partial(back_kernel, kinds, lags, spread_slices, spread_lags, compute_lag, delay),
         out_shape=[
             jax.ShapeDtypeStruct((chunk, lanes), bf16),
             jax.ShapeDtypeStruct((4, 2, 2, 2) + grads.shape, bf16),
@@ -944,7 +953,7 @@
 
 
 def dense_kernel(
-    batch, tiles_hbm, pooled_ref, feats_ref, dense_ref, label_ref, head_ref, last_ref, cross_bias_ref, one_bias_ref,
+    batch, early_hbm, tiles_hbm, pooled_ref, feats_ref, dense_ref, label_ref, head_ref, last_ref, cross_bias_ref, one_bias_ref,
     two_bias_ref, three_bias_ref, grads_hbm, grad_pooled_ref, small_ref,
     tiles, anchor, current, mixing, low, grad_anchor, wide_one, wide_two, stage, load_sem, store_sem,
 ):
@@ -953,8 +962,11 @@
 
     def load(group):
         first, count = GROUPS[group]
+        early = early_hbm.shape[1]
+        late = tiles.shape[1] - tiles_hbm.shape[1]
+        source, at = (early_hbm, first) if first < early else (tiles_hbm, first - late)
         return pltpu.make_async_copy(
-            tiles_hbm.at[:, pl.ds(first, count)], tiles.at[:, pl.ds(first, count)], load_sem.at[group]
+            source.at[:, pl.ds(at, count)], tiles.at[:, pl.ds(first, count)], load_sem.at[group]
         )
 
     for group in range(len(GROUPS)):
@@ -1158,8 +1170,9 @@
         store(slot, 0, CBLK).wait()
 
 
-def dense_step(tiles, pooled, feats, dense_part, labels, head, bias_last, bias_cross, bias_one, bias_two, bias_three, batch):
+def dense_step(early, tiles, pooled, feats, dense_part, labels, head, bias_last, bias_cross, bias_one, bias_two, bias_three, batch):
     samples = dense_part.shape[0]
+    block_count = THREE_AT + 8
     f32, bf16 = jnp.float32, jnp.bfloat16
     whole = pl.BlockSpec(memory_space=pltpu.VMEM)
     away = pl.BlockSpec(memory_space=pl.ANY)
@@ -1167,14 +1180,14 @@
     return pl.pallas_call(
         functools.partial(dense_kernel, batch),
         out_shape=[
-            shape(tiles.shape, bf16),
+            shape((32, block_count, 16, 128), bf16),
             shape((F, samples, EMB), bf16),
             shape((SMALL_ROWS, 128), f32),
         ],
-        in_specs=[away] + [whole] * 10,
+        in_specs=[away] * 2 + [whole] * 10,
         out_specs=[away] + [whole] * 2,
         scratch_shapes=[
-            pltpu.VMEM(tiles.shape, bf16),
+            pltpu.VMEM((32, block_count, 16, 128), bf16),
             pltpu.VMEM((CHUNKS, samples, CW), f32),
             pltpu.VMEM((CHUNKS, samples, CW), f32),
             pltpu.VMEM((LAYERS * CHUNKS, samples, CW), f32),
@@ -1188,7 +1201,7 @@
         ],
         compiler_params=pltpu.CompilerParams(vmem_limit_bytes=61 << 20),
         name="dense_step",
-    )(tiles, pooled, feats, dense_part, labels, head, bias_last, bias_cross, bias_one, bias_two, bias_three)
+    )(early, tiles, pooled, feats, dense_part, labels, head, bias_last, bias_cross, bias_one, bias_two, bias_three)
 
 
 def body(
@@ -1423,8 +1436,10 @@
         axis=0,
         mode="clip",
     )
-    tiles = lax.all_gather(block_tiles.reshape(block_count * 16, 128), "row", axis=0, tiled=True)
-    tiles = tiles.reshape(devices, block_count, 16, 128)
+    early_count = 81
+    early = lax.all_gather(
+        block_tiles[:early_count].reshape(early_count * 16, 128), "row", axis=0, tiled=True
+    ).reshape(devices, early_count, 16, 128)
     bias_dense, bias_cross, bias_one, bias_two, bias_three, bias_last = split_bias(biases)
     requests = (ordered & ((1 << 21) - 1)).reshape(devices, capacity)
     received = lax.all_to_all(requests, "row", split_axis=0, concat_axis=0, tiled=True)
@@ -1433,12 +1448,13 @@
     room = (capacity + samples - 1) // samples * samples + samples
     keys = jnp.pad(received, ((0, 0), (0, room - capacity)), constant_values=-1)
     counts, partial = count_tables(offsets, keys, embed_table, devices, samples)
-    pooled = scatter_sum(partial, 0, F * EMB, bf16, (0, 1) * 8, (2, 4, 6, 7, 8), 0, "scatter_pooled")
+    pooled, tiles = front_exchange(partial, block_tiles[early_count - 1 :], F * EMB, (2, 3) * 8, (2, 3, 4, 5, 8), 10, (1, 2, 3, 4, 5), 3, 0)
     dense_part = (
         jnp.dot(dense_feats, dense_proj, precision=highest, preferred_element_type=jnp.float32)
         + bias_dense
     )
     grad_tiles, grad_pooled, grad_small = dense_step(
+        early,
         tiles,
         pooled,
         jnp.pad(dense_feats, ((0, 0), (0, 3))),
@@ -1457,12 +1473,12 @@
         grad_pooled,
         counts,
         grad_small,
-        (0, 1, 0, 1, 2, 3, 0, 1) * 2,
-        (3, 6, 8, 9, 10),
+        (2, 3) * 8,
+        (2, 3, 4, 5, 8),
         13,
         (1, 2, 3, 4, 5),
         6,
-        (0, 1, 2),
+        3,
         1,
     )
     matches = block_owners[None, :] == jnp.arange(devices * slot_count, dtype=jnp.int32)[:, None]

time: 716 us -> 688 us (0.961)
  Pallas kernels: 573 us -> 543 us
    pallas_call x1, Pallas kernels: 257 us -> 238 us  [back_exchange(): pl.pallas_call(functools.partial(back_kernel, kinds, lags, spread_slices,...]
    pallas_call x2, Pallas kernels: 246 us -> 235 us  [the longest x1 189 us: front_exchange(): pl.pallas_call(functools.partial(front_kernel, kinds, lags, spread_slices...]
  transfers between devices with their start and end apart: 4 -> 4, of which waited for: 2 -> 2; matrix products, arithmetic and copies ran while one was open for 10% -> 11% of each run, Pallas kernels for 37% -> 37%
where the time goes in v4:
time: 688 us; the launch traced here: 684 us
  Pallas kernels  543 us (79%)
  other arithmetic  67.6 us (10%)
  local copies, waits for them, and re-layouts  19.5 us (3%)
  waiting for transfers between devices  18.7 us (3%)
  between operations  17.2 us (2%)
  starting transfers between devices  17.1 us (2%)
    pallas_call x1, Pallas kernels, back_exchange(): pl.pallas_call(functools.partial(back_kernel, kinds, lags, spread_slices,...  238 us
    pallas_call x1, Pallas kernels, front_exchange(): pl.pallas_call(functools.partial(front_kernel, kinds, lags, spread_slices...  189 us
    pallas_call x1, Pallas kernels, count_tables(): pl.pallas_call(functools.partial(count_kernel, devices, samples, table_ro...  60.9 us
    pallas_call x1, Pallas kernels, dense_step(): pl.pallas_call(functools.partial(dense_kernel, batch), out_shape=[shape((...  46.5 us
    sort x1, other arithmetic, body_counted(): ordered = lax.sort(key.reshape(-1), is_stable=False)[:live_total]  37.7 us
    sub x4, other arithmetic, adamw(): weight - step_rate * (corrected / (jnp.sqrt(scaled) + adam_eps) + decay_r...  22.8 us
    all_to_all x1, waiting for transfers between devices, body_counted(): lax.all_to_all(returned.reshape(devices, slot_count * 16, 128), 'row', sp...  14.4 us
  transfers between devices with their start and end apart: 4, of which 2 were waited for; matrix products, arithmetic and copies ran while one was open for 11% of the time, Pallas kernels for 37%

profile of v4, /device:TPU:0, one launch (start us, length us, event | category | flops | bytes accessed | tf_op | source)
XLA Modules:
  0.0 683.8 jit_solution(18021368765041145244)
XLA Ops:
  7.2 0.0 copy-start.7
  7.2 2.1 convert_element_type.13
  9.3 0.4 reshape.113
  9.7 0.0 copy-start.11
  9.8 1.5 copy.63
  11.3 0.0 copy-start.6
  11.3 7.4 %all-to-all-start = ((bf16[32,192,128]{2,1,0:T(8,128)(2,1)}), bf16[32,192,128]{2,1,0:T(8,128)(2,1)}, u32[]{:S(2)}, u32[]{:S(2)}) async-start(bf16[32,192,128]{2,1,0:T(8,128)(2,1)} %bitcast.1), calls=%async_computation | async-start | bytes 3145728 | tf_op jit(solution)/shard_map/all_to_all | solution.py:1421
  18.7 0.0 all-gather.2.cloned.1.call-start
  18.8 0.0 copy-done.7
  18.8 1.5 fusion.5
  20.3 1.9 copy.64
  22.2 1.0 reshape.116
  23.2 37.7 %sort.7 = s32[99840]{0:T(1024)S(1)} sort(s32[99840]{0:T(1024)S(1)} %reshape.116), dimensions={0}, to_apply=%region_0.1 | sort | flops 1697280 | bytes 798720 | tf_op jit(solution)/shard_map/sort | solution.py:1432
  60.9 0.5 slice.73
  62.1 0.0 all-to-all-done
  62.2 2.2 gather_fusion
  64.4 0.7 slice.74
  65.2 0.0 all-gather.2.cloned.1.call-update
  65.2 1.0 and.31
  66.2 5.8 all-to-all-start.1
  72.0 0.5 slice.59
  72.5 0.6 slice.63
  73.1 0.6 reshape.122.one_bias_ref
  73.7 0.6 reshape.123.two_bias_ref
  74.3 0.0 copy-done.5
  74.3 0.1 copy.67
  74.4 0.6 reshape_reshape.6.cross_bias_ref
  75.1 0.7 copy.68.label_ref
  75.8 0.1 fusion.11
  76.0 0.1 broadcast_in_dim.68
  76.1 0.1 copy.69
  76.2 0.1 copy.70
  76.3 0.6 pad.9.feats_ref
  76.9 0.1 select_reduce_fusion
  77.1 0.9 convolution_add_fusion.dense_ref
  78.0 4.3 all-to-all-done.1
  82.4 0.8 convert_reduce_fusion
  83.2 0.1 copy.65
  83.3 0.1 reshape.119.off_ref
  83.4 0.1 fusion.13.most_ref
  83.5 60.9 %count_tables.1 = (bf16[26,512,4096]{2,1,0:T(8,128)(2,1)}, bf16[32,26,128,128]{3,2,1,0:T(8,128)(2,1)}) custom-call(s32[864]{0:T(1024)S(1)} %reshape.119.off_ref, s32[26]{0:T(128)S(1)} %fusion.13.most_ref, s32[32,1792]{1,0:T(8,128)S(1)} %pad.8.keys_ref, f32[26,512,128]{2,1,0:T(8,128)} %table_ref.1), custom_call_target="tpu_custom_call" | custom-call | tf_op jit(solution)/shard_map/count_tables/pallas_call | solution.py:242
  144.4 0.9 slice.78.tiles_ref
  145.3 188.9 %front_exchange.1 = (bf16[3328,128]{1,0:T(8,128)(2,1)}, bf16[4,2,2,2,160,16,128]{6,5,4,3,2,1,0:T(8,128)(2,1)}) custom-call(bf16[4,2,2,2,3328,128]{5,4,3,2,1,0:T(8,128)(2,1)} %bitcast.39, bf16[160,16,128]{2,1,0:T(8,128)(2,1)} %slice.78.tiles_ref), custom_call_target="tpu_custom_call" | custom-call | tf_op jit(solution)/shard_map/front_exchange/pallas_call | solution.py:705
  334.2 0.0 all-gather.2.cloned.1.call-done
  334.2 1.3 broadcast_in_dim.66.last_ref
  335.5 46.5 %dense_step.1 = (bf16[32,240,16,128]{3,2,1,0:T(8,128)(2,1)}, bf16[26,128,128]{2,1,0:T(8,128)(2,1)}, f32[128,128]{1,0:T(8,128)}) custom-call(bf16[32,81,16,128]{3,2,1,0:T(8,128)(2,1)} %bitcast.41, bf16[32,160,16,128]{3,2,1,0:T(8,128)(2,1)} %bitcast.40, bf16[3328,128]{1,0:T(8,128)(2,1)} %get-tuple-element.34.pooled_ref, f32[128,16]{1,0:T(8,128)} %pad.9.feats_ref, ...), custom_call_target="tpu_custom_call" | custom-call | tf_op jit(solution)/shard_map/dense_step/pallas_call | solution.py:1180
  382.0 237.7 %back_exchange.1 = (bf16[3840,128]{1,0:T(8,128)(2,1)}, bf16[4,2,2,2,26,128,128]{6,5,4,3,2,1,0:T(8,128)(2,1)}, f32[26,512,128]{2,1,0:T(8,128)}, f32[128,128]{1,0:...) custom-call(bf16[4,2,2,2,3840,128]{5,4,3,2,1,0:T(8,128)(2,1)} %bitcast.38, bf16[26,128,128]{2,1,0:T(8,128)(2,1)} %get-tuple-element.36.grads_ref, ...), custom_call_target="tpu_custom_call" | custom-call | tf_op jit(solution)/shard_map/back_exchange/pallas_call | solution.py:843
  619.8 0.0 copy-start.9
  619.8 0.0 copy-start.10
  619.8 0.0 copy-start.8
  619.8 0.0 copy-start.12
  619.8 0.0 copy-start.13
  619.8 0.0 copy-start.3
  619.9 0.0 copy-start.4
  619.9 2.3 gather_fusion.1
  622.1 2.3 bitcast_select_fusion
  624.5 3.9 all-to-all-start.2
  628.4 1.2 multiply_subtract_fusion.2
  629.6 1.2 multiply_subtract_fusion.3
  630.8 0.5 slice.64
  631.3 1.2 multiply_subtract_fusion.1
  632.6 19.2 %multiply_subtract_fusion = (f32[26,512,128]{2,1,0:T(8,128)}, f32[26,512,128]{2,1,0:T(8,128)}, f32[26,512,128]{2,1,0:T(8,128)}) fusion(f32[26,512,128]{2,1,0:T(8,128)} %table_ref.1, f32[26,512,128]{2,1,0:T(8,128)} %get-tuple-element.42, f32[]{:T(128)} %bitcast.15, f32[26,512,128]{2,1,0:T(8,128)} %param.26, f32[26,512,128]{2,1,0:T(8,128)} %param.27), kind=kLoop, calls=%fused_computation.4 | loop fusion | flops 27262976 | bytes 47710212 | tf_op jit(solution)/shard_map/sub | solution.py:153
  651.8 14.4 %all-to-all-done.2 = bf16[32,192,128]{2,1,0:T(8,128)(2,1)} async-done(((bf16[32,192,128]{2,1,0:T(8,128)(2,1)}), bf16[32,192,128]{2,1,0:T(8,128)(2,1)}, u32[]{:S(2)}, u32[]{:S(2)}) %all-to-all-start.2) | async-done | bytes 1572896 | tf_op jit(solution)/shard_map/all_to_all | solution.py:1493
  666.1 8.7 %slot_update.1 = (f32[12,128,512]{2,1,0:T(8,128)}, f32[12,128,512]{2,1,0:T(8,128)}, f32[12,128,512]{2,1,0:T(8,128)}) custom-call(f32[1]{0:T(128)} %bitcast.16.scale_ref, bf16[32,12,16,128]{3,2,1,0:T(8,128)(2,1)} %bitcast.20.tiles_ref, f32[12,128,512]{2,1,0:T(8,128)S(1)} %copy-done, f32[12,128,512]{2,1,0:T(8,128)} %moment_ref.1, f32[12,128,512]{2,1,0:T(8,128)} %square_ref.1), custom_call_target="tpu_custom_call" | custom-call | tf_op jit(solution)/shard_map/slot_update/pallas_call | solution.py:897
  (33 shorter events, 0.2 us)
Async XLA Ops:
  7.2 11.6 %copy-start.7 = (s32[128,26]{0,1:T(8,128)S(1)}, s32[128,26]{0,1:T(8,128)}, u32[]{:S(2)}) copy-start(s32[128,26]{0,1:T(8,128)} %param.21) | copy-start | bytes 39940
  9.7 52.4 %copy-start.11 = (s32[240]{0:T(256)S(1)}, s32[240]{0:T(256)}, u32[]{:S(2)}) copy-start(s32[240]{0:T(256)} %param.24) | copy-start | bytes 2884
  11.3 60.7 %copy-start.1 = (f32[13057]{0:T(1024)S(1)}, f32[13057]{0:T(1024)}, u32[]{:S(2)}) copy-start(f32[13057]{0:T(1024)} %param.37) | copy-start | bytes 156688
  11.3 63.0 %copy-start.5 = (f32[128,13]{0,1:T(8,128)S(1)}, f32[128,13]{0,1:T(8,128)}, u32[]{:S(2)}) copy-start(f32[128,13]{0,1:T(8,128)} %param.22) | copy-start | bytes 19972
  11.3 63.8 %copy-start.14 = (s32[128]{0:T(128)S(1)}, s32[128]{0:T(128)}, u32[]{:S(2)}) copy-start(s32[128]{0:T(128)} %param.23) | copy-start | bytes 1540
  11.3 65.8 %slice-start = ((f32[13057]{0:T(1024)}), f32[128]{0:T(128)S(1)}, s32[]{:S(2)}) async-start(f32[13057]{0:T(1024)} %param.37), calls=%async_computation.4 | async-start | bytes 1024 | tf_op jit(solution)/shard_map/slice | solution.py:52
  11.3 65.8 %copy-start.6 = (f32[13,128]{1,0:T(8,128)S(1)}, f32[13,128]{1,0:T(8,128)}, u32[]{:S(2)}) copy-start(f32[13,128]{1,0:T(8,128)} %param.31) | copy-start | bytes 19972
  11.3 50.8 %all-to-all-start = ((bf16[32,192,128]{2,1,0:T(8,128)(2,1)}), bf16[32,192,128]{2,1,0:T(8,128)(2,1)}, u32[]{:S(2)}, u32[]{:S(2)}) async-start(bf16[32,192,128]{2,1,0:T(8,128)(2,1)} %bitcast.1), calls=%async_computation | async-start | bytes 3145728 | tf_op jit(solution)/shard_map/all_to_all | solution.py:1421
  18.7 315.5 %all-gather.2.cloned.1.call-start = ((), (), s32[]{:S(2)}) async-start(), calls=%async_computation.3 | async-start | bytes 10948608 | tf_op jit(solution)/shard_map/all_gather | solution.py:1440
  66.2 16.1 %all-to-all-start.1 = ((s32[32,1,1612]{2,1,0:T(1,128)}), s32[32,1,1612]{2,1,0:T(1,128)S(1)}, u32[]{:S(2)}, u32[]{:S(2)}) async-start(s32[32,1,1612]{2,1,0:T(1,128)} %and.31), calls=%async_computation.1 | async-start | bytes 425984 | tf_op jit(solution)/shard_map/all_to_all | solution.py:1445
  619.8 8.6 %copy-start.2 = (f32[128,128]{1,0:T(8,128)S(1)}, f32[128,128]{1,0:T(8,128)}, u32[]{:S(2)}) copy-start(f32[128,128]{1,0:T(8,128)} %get-tuple-element.39) | copy-start | bytes 196612
  619.8 8.6 %copy-start.9 = (f32[13,128]{1,0:T(8,128)S(1)}, f32[13,128]{1,0:T(8,128)}, u32[]{:S(2)}) copy-start(f32[13,128]{1,0:T(8,128)} %param.32) | copy-start | bytes 19972
  619.8 8.6 %copy-start.10 = (f32[13,128]{1,0:T(8,128)S(1)}, f32[13,128]{1,0:T(8,128)}, u32[]{:S(2)}) copy-start(f32[13,128]{1,0:T(8,128)} %param.33) | copy-start | bytes 19972
  619.8 9.8 %copy-start.8 = (f32[512]{0:T(512)S(1)}, f32[512]{0:T(512)}, u32[]{:S(2)}) copy-start(f32[512]{0:T(512)} %param.34) | copy-start | bytes 6148
  619.8 9.8 %copy-start.12 = (f32[512]{0:T(512)S(1)}, f32[512]{0:T(512)}, u32[]{:S(2)}) copy-start(f32[512]{0:T(512)} %param.35) | copy-start | bytes 6148
  619.8 9.8 %copy-start.13 = (f32[512]{0:T(512)S(1)}, f32[512]{0:T(512)}, u32[]{:S(2)}) copy-start(f32[512]{0:T(512)} %param.36) | copy-start | bytes 6148
  619.8 11.5 %copy-start.3 = (f32[13057]{0:T(1024)S(1)}, f32[13057]{0:T(1024)}, u32[]{:S(2)}) copy-start(f32[13057]{0:T(1024)} %param.38) | copy-start | bytes 156688
  619.9 11.5 %copy-start.4 = (f32[13057]{0:T(1024)S(1)}, f32[13057]{0:T(1024)}, u32[]{:S(2)}) copy-start(f32[13057]{0:T(1024)} %param.39) | copy-start | bytes 156688
  624.5 41.6 %all-to-all-start.2 = ((bf16[32,192,128]{2,1,0:T(8,128)(2,1)}), bf16[32,192,128]{2,1,0:T(8,128)(2,1)}, u32[]{:S(2)}, u32[]{:S(2)}) async-start(bf16[32,192,128]{2,1,0:T(8,128)(2,1)} %bitcast_select_fusion), calls=%async_computation.2 | async-start | bytes 3145728 | tf_op jit(solution)/shard_map/all_to_all | solution.py:1493
  632.6 33.5 %copy-start = (f32[12,128,512]{2,1,0:T(8,128)S(1)}, f32[12,128,512]{2,1,0:T(8,128)}, u32[]{:S(2)}) copy-start(f32[12,128,512]{2,1,0:T(8,128)} %weight_ref.1) | copy-start | bytes 9437188
Sparse Core Ops, SparseCore 0:
  65.3 90.9 all-gather.1
